TPU v7x, 32 devices: a whole 2x2x4 slice. The times are simulated.
32 devices in a mesh: groups: 2 (over x), rows: 16 (over z, y, core).
Axes of the slice: x: 2, y: 2, z: 4, core: 2. Of those that a mesh axis runs over, the one named last changes fastest.
Arguments:
- features: bfloat16 [128, 4, 3072], P(('groups', 'rows')), parts along dimension 0, may hold values from -6 to 6
- cotangent: bfloat16 [128, 4, 3072], P(('groups', 'rows')), parts along dimension 0, may hold values from -6 to 6
- depth_kernel: float32 [7, 7, 3072], replicated, may hold values from -0.875 to 0.875
- depth_bias: float32 [3072], replicated, may hold values from -3 to 3
- norm_gain: float32 [3072], replicated, may hold values from 0.1 to 1.9
- norm_shift: float32 [3072], replicated, may hold values from -3 to 3
- up_weight: bfloat16 [3072, 12288], P(None, 'rows'), may hold values from -0.109375 to 0.109375
- up_bias: float32 [12288], P('rows'), may hold values from -3 to 3
- down_weight: bfloat16 [12288, 3072], P('rows'), may hold values from -0.109375 to 0.109375
- layer_scale: float32 [3072], replicated, may hold values from 0.3 to 3
Outputs:
- input_grad: bfloat16 [128, 4, 3072], P(('groups', 'rows')), parts along dimension 0
- up_grad: float32 [6144, 12288], P('groups', 'rows'), parts along dimension 0
- up_bias_grad: float32 [24576], P(('groups', 'rows')), parts along dimension 0
- down_grad: float32 [24576, 3072], P(('groups', 'rows')), parts along dimension 0
- kernel_grad: float32 [14, 7, 3072], P('groups'), parts along dimension 0
- depth_bias_grad: float32 [6144], P('groups'), parts along dimension 0
- gain_grad: float32 [6144], P('groups'), parts along dimension 0
- shift_grad: float32 [6144], P('groups'), parts along dimension 0
There are 2 independent parts, one for each index of `groups`. A program takes and returns all parts, laid end to end along the dimension named above; an argument that names none is the same for every part. Nothing has to cross between parts.
All inputs are finite; a program needn't handle non-finite values.
Results may differ from a plain program's by a relative error of at most 0.0075.
Values may be sent and summed in bfloat16 or wider, within the bound.
No kernel may reach another device: no remote copies, remote signals or barrier semaphores. Data moves between devices by JAX's collectives and lax.ppermute only.
A program may use at most 128 MiB of HBM per device.

v0:
```python
import jax
import jax.numpy as jnp
from jax import lax
from jax.sharding import PartitionSpec as P

IMG_ROWS = 32


def extended(cells, sides, width):
    for axis, dim in sides:
        count = lax.axis_size(axis)
        head = lax.slice_in_dim(cells, 0, width, axis=dim)
        tail = lax.slice_in_dim(cells, cells.shape[dim] - width, cells.shape[dim], axis=dim)
        cells = jnp.concatenate(
            [
                lax.ppermute(tail, axis, [(i, (i + 1) % count) for i in range(count)]),
                cells,
                lax.ppermute(head, axis, [((i + 1) % count, i) for i in range(count)]),
            ],
            axis=dim,
        )
    return cells


def gelu_value(pre_act):
    return 0.5 * pre_act * (1.0 + jax.scipy.special.erf(pre_act * 0.7071067811865476))


def gelu_slope(pre_act):
    cdf_part = 0.5 * (1.0 + jax.scipy.special.erf(pre_act * 0.7071067811865476))
    return cdf_part + pre_act * jnp.exp(-0.5 * pre_act * pre_act) * 0.3989422804014327


def contract(left, right, left_dim, right_dim):
    return lax.dot_general(
        left, right, (((left_dim,), (right_dim,)), ((), ())), preferred_element_type=jnp.float32
    )


def depthwise(padded, kernel, offset_term, row_count, col_count):
    summed = jnp.zeros(padded[..., 3 : 3 + row_count, 3 : 3 + col_count, :].shape, padded.dtype)
    for tap_row in range(7):
        for tap_col in range(7):
            summed = (
                summed
                + kernel[tap_row, tap_col]
                * padded[..., tap_row : tap_row + row_count, tap_col : tap_col + col_count, :]
            )
    return summed + offset_term


def depthwise_back(padded_grad, kernel, row_count, col_count):
    summed = jnp.zeros(
        padded_grad[..., 3 : 3 + row_count, 3 : 3 + col_count, :].shape, padded_grad.dtype
    )
    for tap_row in range(7):
        for tap_col in range(7):
            summed = (
                summed
                + kernel[tap_row, tap_col]
                * padded_grad[
                    ...,
                    6 - tap_row : 6 - tap_row + row_count,
                    6 - tap_col : 6 - tap_col + col_count,
                    :,
                ]
            )
    return summed


def normalize(conv_out):
    row_mean = jnp.mean(conv_out, axis=-1, keepdims=True)
    centred = conv_out - row_mean
    inv_std = lax.rsqrt(jnp.mean(centred * centred, axis=-1, keepdims=True) + 1e-06)
    return (centred * inv_std, inv_std)


def norm_back(norm_grad, unit_norm, inv_std, norm_gain):
    scaled = norm_grad * norm_gain
    return inv_std * (
        scaled
        - jnp.mean(scaled, axis=-1, keepdims=True)
        - unit_norm * jnp.mean(scaled * unit_norm, axis=-1, keepdims=True)
    )


def pad_columns(block):
    return jnp.pad(block, ((0, 0), (3, 3), (0, 0)))


def on_device(
    features,
    cotangent,
    depth_kernel,
    depth_bias,
    norm_gain,
    norm_shift,
    up_weight,
    up_bias,
    down_weight,
    layer_scale,
):
    rows_dev, col_count, channels = features.shape
    total_rows = rows_dev * lax.axis_size("rows")
    half_image = IMG_ROWS // 2
    my_index = lax.axis_index("rows")
    first_row = my_index * rows_dev
    row_offsets = first_row - 3 + jnp.arange(rows_dev + 6, dtype=jnp.int32)
    row_image = jnp.mod(row_offsets - half_image, total_rows) // IMG_ROWS
    own_image = jnp.mod(first_row - half_image, total_rows) // IMG_ROWS
    row_mask = (row_image == own_image).astype(jnp.float32)[:, None, None]
    cot_scaled = (
        (cotangent.astype(jnp.float32) * layer_scale)
        .astype(jnp.bfloat16)
        .reshape(rows_dev * col_count, channels)
    )
    cot_all = lax.all_gather(cot_scaled, "rows", axis=0, tiled=True)
    near_rows = extended(features, (("rows", 0),), 3)
    padded = pad_columns(near_rows.astype(jnp.float32) * row_mask)
    conv_out = depthwise(padded, depth_kernel, depth_bias, rows_dev, col_count)
    unit_norm, inv_std = normalize(conv_out)
    normed = (
        (unit_norm * norm_gain + norm_shift)
        .astype(jnp.bfloat16)
        .reshape(rows_dev * col_count, channels)
    )
    normed_all = lax.all_gather(normed, "rows", axis=0, tiled=True)
    pre_act = jnp.dot(normed_all, up_weight, preferred_element_type=jnp.float32) + up_bias
    hidden = gelu_value(pre_act).astype(jnp.bfloat16)
    down_grad = contract(hidden, cot_all, 0, 0)
    hid_grad = contract(cot_all, down_weight, 1, 1)
    act_grad = (hid_grad * gelu_slope(pre_act)).astype(jnp.bfloat16)
    up_bias_grad = jnp.sum(act_grad.astype(jnp.float32), axis=0)
    up_grad = contract(normed_all, act_grad, 0, 0)
    norm_grad = lax.psum_scatter(
        contract(act_grad, up_weight, 1, 1), "rows", scatter_dimension=0, tiled=True
    ).reshape(rows_dev, col_count, channels)
    gain_part = jnp.sum(norm_grad * unit_norm, axis=(0, 1))
    shift_part = jnp.sum(norm_grad, axis=(0, 1))
    conv_grad = norm_back(norm_grad, unit_norm, inv_std, norm_gain)
    bias_part = jnp.sum(conv_grad, axis=(0, 1))
    kernel_rows = []
    for tap_row in range(7):
        kernel_cols = []
        for tap_col in range(7):
            kernel_cols.append(
                jnp.sum(
                    conv_grad
                    * padded[tap_row : tap_row + rows_dev, tap_col : tap_col + col_count, :],
                    axis=(0, 1),
                )
            )
        kernel_rows.append(jnp.stack(kernel_cols))
    kernel_part = jnp.stack(kernel_rows)
    near_grad = extended(conv_grad.astype(jnp.bfloat16), (("rows", 0),), 3).astype(conv_grad.dtype)
    grad_padded = pad_columns(near_grad * row_mask)
    back_term = depthwise_back(grad_padded, depth_kernel, rows_dev, col_count)
    input_grad = (cotangent.astype(jnp.float32) + back_term).astype(jnp.bfloat16)
    gain_grad, shift_grad, kernel_grad, depth_bias_grad = lax.psum(
        (gain_part, shift_part, kernel_part, bias_part), "rows"
    )
    return (
        input_grad,
        up_grad,
        up_bias_grad,
        down_grad,
        kernel_grad,
        depth_bias_grad,
        gain_grad,
        shift_grad,
    )


def solution(mesh):
    in_specs = (
        P(("groups", "rows"), None, None),
        P(("groups", "rows"), None, None),
        P(),
        P(),
        P(),
        P(),
        P(None, "rows"),
        P("rows"),
        P("rows", None),
        P(),
    )
    out_specs = (
        P(("groups", "rows"), None, None),
        P("groups", "rows"),
        P(("groups", "rows")),
        P(("groups", "rows"), None),
        P("groups", None, None),
        P("groups"),
        P("groups"),
        P("groups"),
    )
    return jax.shard_map(
        on_device, mesh=mesh, in_specs=in_specs, out_specs=out_specs, check_vma=False
    )
```

profile of v0, /device:TPU:0, one launch (start us, length us, event | category | flops | bytes accessed | tf_op | source)
XLA Modules:
  0.0 296.4 jit_solution(8445374431140622717)
XLA Ops:
  8.7 5.1 %collective-permute-start.1 = (bf16[3,4,3072]{2,1,0:T(4,128)(2,1)S(1)}, bf16[3,4,3072]{2,1,0:T(4,128)(2,1)S(1)}, u32[]{:S(2)}, u32[]{:S(2)}) collective-permute-start(bf16[3,4,3072]{2,1,0:T(4,128)(2,1)S(1)} %get-tuple-element.121), channel_id=1, source_target_pairs={{1,0},{2,1},{3,2},{4,3},{5,4},{6,5},{7,6},{8,7},{9,8},{10,9},{11,1... | collective-permute-start | bytes 221192 | tf_op jit(solution)/shard_map/ppermute | solution.py:18
  13.8 1.7 fusion.105
  15.6 2.3 fusion.103
  18.1 2.8 fusion.104
  21.6 1.1 convert_multiply_fusion.1
  22.7 5.2 %fusion.102 = (f32[4,4]{1,0:T(4,128)S(1)}, f32[4,4,3072]{2,1,0:T(4,128)S(1)}) fusion(f32[3072]{0:T(1024)S(1)} %copy-done.85, f32[3072]{0:T(1024)S(1)} %bitcast.139, f32[3072]{0:T(1024)S(1)} %bitcast.141, f32[3072]{0:T(1024)S(1)} %bitcast.145, f32[10,4,3072]{2,1,0:T(4,128)S(1)} %convert_multiply_fusion.1, f32[3072]{0:T(1024)S(1)} %bitcast.147, ...), kind=kLoop, calls=%fused_computation.279 | loop fusion | flops 4866032 | bytes 2678848 | tf_op jit(solution)/shard_map/reduce_sum | solution.py:72
  30.3 37.9 %all-gather.5.cloned.1.call-done = bf16[256,3072]{1,0:T(8,128)(2,1)} async-done(((bf16[16,3072]{1,0:T(8,128)(2,1)}), bf16[256,3072]{1,0:T(8,128)(2,1)}) %all-gather.5.cloned.1.call-update) | async-done | bytes 1572880 | tf_op jit(solution)/shard_map/all_gather | solution.py:127
  68.2 4.2 %convolution_add_fusion = f32[256,768]{1,0:T(8,128)S(1)} fusion(bf16[256,3072]{1,0:T(8,128)(2,1)} %all-gather.5.cloned.1.call-done, bf16[3072,768]{1,0:T(8,128)(2,1)} %param.16, f32[768]{0:T(1024)S(1)} %copy-done.88), kind=kOutput, calls=%fused_computation.85 | convolution fusion | flops 1208156160 | bytes 7080960 | tf_op jit(solution)/shard_map/dot_general | solution.py:128
  72.4 37.2 %all-gather.3.cloned.1.call-done = bf16[256,3072]{1,0:T(8,128)(2,1)} async-done(((bf16[16,3072]{1,0:T(8,128)(2,1)}), bf16[256,3072]{1,0:T(8,128)(2,1)}) %all-gather.3.cloned.1.call-update) | async-done | bytes 1572880 | tf_op jit(solution)/shard_map/all_gather | solution.py:117
  109.7 5.0 %convert_reduce_fusion = (f32[768]{0:T(1024)}, bf16[256,768]{1,0:T(8,128)(2,1)S(1)}) fusion(f32[256,768]{1,0:T(8,128)S(1)} %convolution_add_fusion, bf16[256,3072]{1,0:T(8,128)(2,1)} %all-gather.3.cloned.1.call-done, bf16[768,3072]{1,0:T(8,128)(2,1)} %param.18), kind=kOutput, calls=%fused_computation.93 | convolution fusion | flops 1210318080 | bytes 7474176 | tf_op jit(solution)/shard_map/dot_general | solution.py:35
  114.6 5.4 %fusion.108 = f32[256,3072]{1,0:T(8,128)} fusion(bf16[256,768]{1,0:T(8,128)(2,1)S(1)} %get-tuple-element.123, bf16[3072,768]{1,0:T(8,128)(2,1)} %param.16), kind=kOutput, calls=%fused_computation.285 | convolution fusion | flops 1207959552 | bytes 8257536 | tf_op jit(solution)/shard_map/dot_general | solution.py:35
  120.3 1.2 copy-done
  121.5 5.2 %fusion.109 = f32[3072,768]{1,0:T(8,128)} fusion(bf16[256,3072]{1,0:T(8,128)(2,1)S(1)} %copy-done, bf16[256,768]{1,0:T(8,128)(2,1)S(1)} %get-tuple-element.123), kind=kOutput, calls=%fused_computation.286 | convolution fusion | flops 1207959552 | bytes 11403264 | tf_op jit(solution)/shard_map/dot_general | solution.py:35
  126.7 5.2 %fusion.5 = f32[768,3072]{1,0:T(8,128)} fusion(bf16[256,3072]{1,0:T(8,128)(2,1)S(1)} %copy-done.1, f32[256,768]{1,0:T(8,128)S(1)} %convolution_add_fusion), kind=kOutput, calls=%fused_computation.97 | convolution fusion | flops 1208942592 | bytes 11796480 | tf_op jit(solution)/shard_map/dot_general | solution.py:35
  131.9 53.5 %reduce-scatter.2.cloned.1.call-done = f32[16,3072]{1,0:T(8,128)} async-done(((f32[256,3072]{1,0:T(8,128)}), f32[16,3072]{1,0:T(8,128)}) %reduce-scatter.2.cloned.1.call-update) | async-done | bytes 196624 | tf_op jit(solution)/shard_map/reduce_scatter | solution.py:135
  185.4 1.1 fusion.101
  187.8 1.5 multiply_reduce_fusion.1
  189.3 1.0 multiply_reduce_fusion.37
  190.3 1.3 multiply_reduce_fusion.19
  191.8 4.4 %collective-permute-start.3 = (bf16[3,4,3072]{2,1,0:T(4,128)(2,1)S(1)}, bf16[3,4,3072]{2,1,0:T(4,128)(2,1)S(1)}, u32[]{:S(2)}, u32[]{:S(2)}) collective-permute-start(bf16[3,4,3072]{2,1,0:T(4,128)(2,1)S(1)} %get-tuple-element.119), channel_id=1, source_target_pairs={{1,0},{2,1},{3,2},{4,3},{5,4},{6,5},{7,6},{8,7},{9,8},{10,9},{11,1... | collective-permute-start | bytes 221192 | tf_op jit(solution)/shard_map/ppermute | solution.py:18
  198.6 58.5 %all-reduce.2 = (f32[3072]{0:T(1024)}, f32[3072]{0:T(1024)}, f32[3072]{0:T(1024)}) all-reduce(f32[3072]{0:T(1024)S(1)} %get-tuple-element.61, f32[3072]{0:T(1024)S(1)} %get-tuple-element.57, f32[3072]{0:T(1024)S(1)} %get-tuple-element.59), channel_id=1, replica_groups=mesh['groups'=2,'rows'=16] {'rows'}, use_global_device_ids=true, to_apply=%region_57.58 | all-reduce | flops 9216 | bytes 73728 | tf_op jit(solution)/shard_map/psum | solution.py:159
  258.3 4.2 %fusion.8 = bf16[4,4,3072]{2,1,0:T(4,128)(2,1)} fusion(bf16[4,4,3072]{2,1,0:T(4,128)(2,1)S(1)} %copy-done.3, f32[10,4,3072]{2,1,0:T(4,128)S(1)} %convert_multiply_fusion, f32[3072]{0:T(1024)S(1)} %bitcast.140, f32[3072]{0:T(1024)S(1)} %bitcast.142, f32[3072]{0:T(1024)S(1)} %bitcast.146, f32[3072]{0:T(1024)S(1)} %bitcast.148, f32[3072]{0:T(1024)S(1)} %bitcast.150, ...), kind=kLoop, calls=%fused_computation.102 | loop fusion | flops 4915200 | bytes 2666496 | tf_op jit(solution)/shard_map/convert_element_type | solution.py:158
  262.6 25.3 %all-reduce.5.cloned.1.call-done = f32[7,7,3072]{2,1,0:T(8,128)} async-done(((f32[7,7,3072]{2,1,0:T(8,128)}), f32[7,7,3072]{2,1,0:T(8,128)}) %all-reduce.5.cloned.1.call-update) | async-done | bytes 602128 | tf_op jit(solution)/shard_map/psum | solution.py:159
  287.9 2.0 copy.25
  (221 shorter events, 8.8 us)
Async XLA Ops:
  7.2 61.0 %all-gather.5.cloned.1.call-start = ((), (), s32[]{:S(2)}) async-start(), calls=%async_computation.2 | async-start | bytes 1671168 | tf_op jit(solution)/shard_map/all_gather | solution.py:127
  8.2 13.4 %collective-permute-start = (bf16[3,4,3072]{2,1,0:T(4,128)(2,1)S(1)}, bf16[3,4,3072]{2,1,0:T(4,128)(2,1)S(1)}, u32[]{:S(2)}, u32[]{:S(2)}) collective-permute-start(bf16[3,4,3072]{2,1,0:T(4,128)(2,1)S(1)} %get-tuple-element.120), channel_id=1, source_target_pairs={{0,1},{1,2},{2,3},{3,4},{4,5},{5,6},{6,7},{7,8},{8,9},{9,10},{10,1... | collective-permute-start | bytes 221192 | tf_op jit(solution)/shard_map/ppermute | solution.py:16
  8.7 12.9 %collective-permute-start.1 = (bf16[3,4,3072]{2,1,0:T(4,128)(2,1)S(1)}, bf16[3,4,3072]{2,1,0:T(4,128)(2,1)S(1)}, u32[]{:S(2)}, u32[]{:S(2)}) collective-permute-start(bf16[3,4,3072]{2,1,0:T(4,128)(2,1)S(1)} %get-tuple-element.121), channel_id=1, source_target_pairs={{1,0},{2,1},{3,2},{4,3},{5,4},{6,5},{7,6},{8,7},{9,8},{10,9},{11,1... | collective-permute-start | bytes 221192 | tf_op jit(solution)/shard_map/ppermute | solution.py:18
  29.5 80.2 %all-gather.3.cloned.1.call-start = ((), (), s32[]{:S(2)}) async-start(), calls=%async_computation.1 | async-start | bytes 1671168 | tf_op jit(solution)/shard_map/all_gather | solution.py:117
  30.3 155.1 %reduce-scatter.2.cloned.1.call-start = ((), (), s32[]{:S(2)}) async-start(), calls=%async_computation.3 | async-start | bytes 3342336 | tf_op jit(solution)/shard_map/reduce_scatter | solution.py:135
  120.1 167.8 %all-reduce.5.cloned.1.call-start = ((), (), s32[]{:S(2)}) async-start(), calls=%async_computation.4 | async-start | bytes 1376256 | tf_op jit(solution)/shard_map/psum | solution.py:159
  191.7 65.4 %collective-permute-start.2 = (bf16[3,4,3072]{2,1,0:T(4,128)(2,1)S(1)}, bf16[3,4,3072]{2,1,0:T(4,128)(2,1)S(1)}, u32[]{:S(2)}, u32[]{:S(2)}) collective-permute-start(bf16[3,4,3072]{2,1,0:T(4,128)(2,1)S(1)} %get-tuple-element.118), channel_id=1, source_target_pairs={{0,1},{1,2},{2,3},{3,4},{4,5},{5,6},{6,7},{7,8},{8,9},{9,10},{10,1... | collective-permute-start | bytes 221192 | tf_op jit(solution)/shard_map/ppermute | solution.py:16
  191.8 65.3 %collective-permute-start.3 = (bf16[3,4,3072]{2,1,0:T(4,128)(2,1)S(1)}, bf16[3,4,3072]{2,1,0:T(4,128)(2,1)S(1)}, u32[]{:S(2)}, u32[]{:S(2)}) collective-permute-start(bf16[3,4,3072]{2,1,0:T(4,128)(2,1)S(1)} %get-tuple-element.119), channel_id=1, source_target_pairs={{1,0},{2,1},{3,2},{4,3},{5,4},{6,5},{7,6},{8,7},{9,8},{10,9},{11,1... | collective-permute-start | bytes 221192 | tf_op jit(solution)/shard_map/ppermute | solution.py:18
  196.4 61.6 %copy-start.6 = (f32[1,1,3072]{2,1,0:T(1,128)S(1)}, f32[1,1,3072]{2,1,0:T(1,128)}, u32[]{:S(2)}) copy-start(f32[1,1,3072]{2,1,0:T(1,128)} %copy-done.5) | copy-start | bytes 36868
  196.4 61.6 %copy-start.8 = (f32[1,1,3072]{2,1,0:T(1,128)S(1)}, f32[1,1,3072]{2,1,0:T(1,128)}, u32[]{:S(2)}) copy-start(f32[1,1,3072]{2,1,0:T(1,128)} %copy-done.7) | copy-start | bytes 36868
  196.4 61.6 %copy-start.10 = (f32[1,1,3072]{2,1,0:T(1,128)S(1)}, f32[1,1,3072]{2,1,0:T(1,128)}, u32[]{:S(2)}) copy-start(f32[1,1,3072]{2,1,0:T(1,128)} %copy-done.9) | copy-start | bytes 36868
  196.4 61.6 %copy-start.12 = (f32[1,1,3072]{2,1,0:T(1,128)S(1)}, f32[1,1,3072]{2,1,0:T(1,128)}, u32[]{:S(2)}) copy-start(f32[1,1,3072]{2,1,0:T(1,128)} %copy-done.11) | copy-start | bytes 36868
  196.4 61.6 %copy-start.14 = (f32[1,1,3072]{2,1,0:T(1,128)S(1)}, f32[1,1,3072]{2,1,0:T(1,128)}, u32[]{:S(2)}) copy-start(f32[1,1,3072]{2,1,0:T(1,128)} %copy-done.13) | copy-start | bytes 36868
  196.4 61.6 %copy-start.16 = (f32[1,1,3072]{2,1,0:T(1,128)S(1)}, f32[1,1,3072]{2,1,0:T(1,128)}, u32[]{:S(2)}) copy-start(f32[1,1,3072]{2,1,0:T(1,128)} %copy-done.15) | copy-start | bytes 36868
  196.4 61.6 %copy-start.18 = (f32[1,1,3072]{2,1,0:T(1,128)S(1)}, f32[1,1,3072]{2,1,0:T(1,128)}, u32[]{:S(2)}) copy-start(f32[1,1,3072]{2,1,0:T(1,128)} %copy-done.17) | copy-start | bytes 36868
  196.4 61.6 %copy-start.20 = (f32[1,1,3072]{2,1,0:T(1,128)S(1)}, f32[1,1,3072]{2,1,0:T(1,128)}, u32[]{:S(2)}) copy-start(f32[1,1,3072]{2,1,0:T(1,128)} %copy-done.19) | copy-start | bytes 36868
  196.4 61.6 %copy-start.22 = (f32[1,1,3072]{2,1,0:T(1,128)S(1)}, f32[1,1,3072]{2,1,0:T(1,128)}, u32[]{:S(2)}) copy-start(f32[1,1,3072]{2,1,0:T(1,128)} %copy-done.21) | copy-start | bytes 36868
  196.4 61.6 %copy-start.24 = (f32[1,1,3072]{2,1,0:T(1,128)S(1)}, f32[1,1,3072]{2,1,0:T(1,128)}, u32[]{:S(2)}) copy-start(f32[1,1,3072]{2,1,0:T(1,128)} %copy-done.23) | copy-start | bytes 36868
  196.5 61.6 %copy-start.26 = (f32[1,1,3072]{2,1,0:T(1,128)S(1)}, f32[1,1,3072]{2,1,0:T(1,128)}, u32[]{:S(2)}) copy-start(f32[1,1,3072]{2,1,0:T(1,128)} %copy-done.25) | copy-start | bytes 36868
  196.5 61.6 %copy-start.28 = (f32[1,1,3072]{2,1,0:T(1,128)S(1)}, f32[1,1,3072]{2,1,0:T(1,128)}, u32[]{:S(2)}) copy-start(f32[1,1,3072]{2,1,0:T(1,128)} %copy-done.27) | copy-start | bytes 36868
  196.5 61.6 %copy-start.30 = (f32[1,1,3072]{2,1,0:T(1,128)S(1)}, f32[1,1,3072]{2,1,0:T(1,128)}, u32[]{:S(2)}) copy-start(f32[1,1,3072]{2,1,0:T(1,128)} %copy-done.29) | copy-start | bytes 36868
  196.5 61.6 %copy-start.32 = (f32[1,1,3072]{2,1,0:T(1,128)S(1)}, f32[1,1,3072]{2,1,0:T(1,128)}, u32[]{:S(2)}) copy-start(f32[1,1,3072]{2,1,0:T(1,128)} %copy-done.31) | copy-start | bytes 36868
  196.5 61.6 %copy-start.34 = (f32[1,1,3072]{2,1,0:T(1,128)S(1)}, f32[1,1,3072]{2,1,0:T(1,128)}, u32[]{:S(2)}) copy-start(f32[1,1,3072]{2,1,0:T(1,128)} %copy-done.33) | copy-start | bytes 36868
  196.5 61.6 %copy-start.36 = (f32[1,1,3072]{2,1,0:T(1,128)S(1)}, f32[1,1,3072]{2,1,0:T(1,128)}, u32[]{:S(2)}) copy-start(f32[1,1,3072]{2,1,0:T(1,128)} %copy-done.35) | copy-start | bytes 36868
  (73 other events, 1978.4 us)
Sparse Core Ops, SparseCore 0:
  29.6 38.5 all-gather.4
  71.1 38.5 all-gather.2
  120.2 65.0 reduce-scatter.1
  198.7 89.1 all-reduce.4
where the time goes:
time: 297 us; the launch traced here: 296 us
  waiting for transfers between devices  154 us (52%)
  blocking collectives  58.5 us (20%)
  matrix products  25 us (8%)
  other arithmetic  17.7 us (6%)
  local copies, waits for them, and re-layouts  15.6 us (5%)
  between operations  15.3 us (5%)
  starting transfers between devices  10.4 us (4%)
    psum x1, blocking collectives, on_device(): lax.psum((gain_part, shift_part, kernel_part, bias_part), 'rows')  58.5 us
    reduce_scatter x1, waiting for transfers between devices, on_device(): lax.psum_scatter(contract(act_grad, up_weight, 1, 1), 'rows', scatter_dim...  53.5 us
    all_gather x1, waiting for transfers between devices, on_device(): normed_all = lax.all_gather(normed, 'rows', axis=0, tiled=True)  37.9 us
    all_gather x1, waiting for transfers between devices, on_device(): cot_all = lax.all_gather(cot_scaled, 'rows', axis=0, tiled=True)  37.2 us
    psum x1, waiting for transfers between devices, on_device(): lax.psum((gain_part, shift_part, kernel_part, bias_part), 'rows')  25.3 us
    dot_general x4, matrix products, contract(): lax.dot_general(left, right, (((left_dim,), (right_dim,)), ((), ())), pre...  20.8 us
    ppermute x2, starting transfers between devices, extended(): lax.ppermute(head, axis, [((i + 1) % count, i) for i in range(count)])  9.49 us
  transfers between devices with their start and end apart: 8, of which 4 were waited for; matrix products, arithmetic and copies ran while one was open for 10% of the time, Pallas kernels for 0%

commit v1 on v0

v1 whole, which is shorter than its diff:
```python
import jax
import jax.numpy as jnp
from jax import lax
from jax.sharding import PartitionSpec as P

IMG_ROWS = 32
BF16 = jnp.bfloat16
F32 = jnp.float32


def stages_of(count):
    sizes = []
    chips = count // 2
    while chips % 4 == 0 and chips > 4:
        sizes.append(4)
        chips //= 4
    if chips > 1:
        sizes.append(chips)
    out = [(1, 2)]
    stride = 2
    for size in reversed(sizes):
        out.insert(0, (stride, size))
        stride *= size
    return out


def from_ahead(count, stride, size, step):
    pairs = []
    for i in range(count):
        digit = (i // stride) % size
        src = i + ((digit + step) % size - digit) * stride
        pairs.append((src, i))
    return pairs


def send(value, pairs):
    return lax.ppermute(value, "rows", pairs)


def gather_stage(value, count, stride, size):
    parts = [value]
    for step in range(1, size):
        parts.append(send(value, from_ahead(count, stride, size, step)))
    return jnp.stack(parts)


def scatter_stage(value, count, stride, size):
    total = value[0].astype(F32)
    for step in range(1, size):
        back = [(dst, src) for src, dst in from_ahead(count, stride, size, step)]
        total = total + send(value[step], back).astype(F32)
    return total


def gelu_parts(pre_act):
    cdf = 0.5 * (1.0 + jax.scipy.special.erf(pre_act * 0.7071067811865476))
    slope = cdf + pre_act * jnp.exp(-0.5 * pre_act * pre_act) * 0.3989422804014327
    return pre_act * cdf, slope


def contract(left, right, left_dim, right_dim):
    return lax.dot_general(
        left, right, (((left_dim,), (right_dim,)), ((), ())), preferred_element_type=F32
    )


def extended(cells, width, fwd, bwd):
    head = lax.slice_in_dim(cells, 0, width, axis=0)
    tail = lax.slice_in_dim(cells, cells.shape[0] - width, cells.shape[0], axis=0)
    return jnp.concatenate([send(tail, fwd), cells, send(head, bwd)], axis=0)


def on_device(
    features,
    cotangent,
    depth_kernel,
    depth_bias,
    norm_gain,
    norm_shift,
    up_weight,
    up_bias,
    down_weight,
    layer_scale,
):
    rows_dev, cols, channels = features.shape
    count = lax.axis_size("rows")
    stages = stages_of(count)
    shard = rows_dev * cols
    half_image = IMG_ROWS // 2
    crossing = [
        (i, (i + 1) % count)
        for i in range(count)
        if ((i + 1) * rows_dev - half_image) % IMG_ROWS != 0
    ]
    fwd = crossing
    bwd = [(b, a) for a, b in crossing]
    pieces = 2
    width = channels // pieces

    def gather(value):
        outs = []
        for p in range(pieces):
            part = value[:, p * width : (p + 1) * width]
            for stride, size in stages:
                part = gather_stage(part, count, stride, size)
            outs.append(part.reshape(shard * count, width))
        return outs

    near = extended(features, 3, fwd, bwd).astype(F32)
    cot_scaled = (
        (cotangent.astype(F32) * layer_scale).astype(BF16).reshape(shard, channels)
    )
    cot_all = gather(cot_scaled)
    padded = jnp.pad(near, ((0, 0), (3, 3), (0, 0)))
    conv_out = jnp.zeros((rows_dev, cols, channels), F32)
    for i in range(7):
        for j in range(7):
            conv_out = conv_out + depth_kernel[i, j] * padded[i : i + rows_dev, j : j + cols]
    conv_out = conv_out + depth_bias
    row_mean = jnp.mean(conv_out, axis=-1, keepdims=True)
    centred = conv_out - row_mean
    inv_std = lax.rsqrt(jnp.mean(centred * centred, axis=-1, keepdims=True) + 1e-06)
    unit_norm = centred * inv_std
    normed = (unit_norm * norm_gain + norm_shift).astype(BF16).reshape(shard, channels)
    normed_all = gather(normed)

    hid_grad = sum(
        contract(cot_all[p], down_weight[:, p * width : (p + 1) * width], 1, 1)
        for p in range(pieces)
    )
    pre_act = up_bias + sum(
        contract(normed_all[p], up_weight[p * width : (p + 1) * width], 1, 0)
        for p in range(pieces)
    )
    value, slope = gelu_parts(pre_act)
    hidden = value.astype(BF16)
    act_grad = (hid_grad * slope).astype(BF16)

    norm_parts = []
    for p in range(pieces):
        part = contract(act_grad, up_weight[p * width : (p + 1) * width], 1, 1).astype(BF16)
        lead = [size for _, size in reversed(stages)]
        part = part.reshape(*lead, shard, width)
        for stride, size in reversed(stages):
            part = scatter_stage(part, count, stride, size)
            if stride != stages[0][0]:
                part = part.astype(BF16)
        norm_parts.append(part)
    norm_grad = jnp.concatenate(norm_parts, axis=-1).reshape(rows_dev, cols, channels)

    up_bias_grad = jnp.sum(act_grad.astype(F32), axis=0)
    down_grad = jnp.concatenate([contract(hidden, c, 0, 0) for c in cot_all], axis=1)
    up_grad = jnp.concatenate([contract(n, act_grad, 0, 0) for n in normed_all], axis=0)

    gain_part = jnp.sum(norm_grad * unit_norm, axis=(0, 1))
    shift_part = jnp.sum(norm_grad, axis=(0, 1))
    scaled = norm_grad * norm_gain
    conv_grad = inv_std * (
        scaled
        - jnp.mean(scaled, axis=-1, keepdims=True)
        - unit_norm * jnp.mean(scaled * unit_norm, axis=-1, keepdims=True)
    )
    bias_part = jnp.sum(conv_grad, axis=(0, 1))
    rows_out = [
        jnp.sum(conv_grad * padded[i : i + rows_dev, j : j + cols], axis=(0, 1))
        for i in range(7)
        for j in range(7)
    ]
    near_grad = extended(conv_grad.astype(BF16), 3, fwd, bwd).astype(F32)
    grad_padded = jnp.pad(near_grad, ((0, 0), (3, 3), (0, 0)))

    chips = count // 2
    per = -(-52 // chips)
    small = jnp.stack(rows_out + [gain_part, shift_part, bias_part])
    small = jnp.pad(small, ((0, per * chips - 52), (0, 0)))
    half = channels // 2
    small = small.reshape(chips, per, 2, half).transpose(2, 0, 1, 3)
    core = lax.axis_index("rows") % 2
    swapped = jnp.where(core == 0, small, small[::-1])
    swapped = swapped.astype(BF16)
    mine = swapped[0].astype(F32) + send(
        swapped[1], from_ahead(count, 1, 2, 1)
    ).astype(F32)
    mine = mine.astype(BF16)
    chip = lax.axis_index("rows") // 2
    ahead = jnp.roll(mine, -chip, axis=0)
    total = ahead[0].astype(F32)
    for step in range(1, chips):
        back = [(dst, src) for src, dst in from_ahead(count, 2, chips, step)]
        total = total + send(ahead[step], back).astype(F32)
    total = total.astype(BF16)
    every = [total] + [
        send(total, from_ahead(count, 2, chips, step)) for step in range(1, chips)
    ]
    every = jnp.roll(jnp.stack(every), chip, axis=0)
    other = send(every, from_ahead(count, 1, 2, 1))
    both = jnp.where(
        core == 0,
        jnp.concatenate([every, other], axis=-1),
        jnp.concatenate([other, every], axis=-1),
    )
    both = both.reshape(per * chips, channels).astype(F32)
    kernel_grad = both[:49].reshape(7, 7, channels)
    gain_grad, shift_grad, depth_bias_grad = both[49], both[50], both[51]

    back_term = jnp.zeros((rows_dev, cols, channels), F32)
    for i in range(7):
        for j in range(7):
            back_term = back_term + depth_kernel[i, j] * grad_padded[
                6 - i : 6 - i + rows_dev, 6 - j : 6 - j + cols
            ]
    input_grad = (cotangent.astype(F32) + back_term).astype(BF16)
    return (
        input_grad,
        up_grad,
        up_bias_grad,
        down_grad,
        kernel_grad,
        depth_bias_grad,
        gain_grad,
        shift_grad,
    )


def solution(mesh):
    in_specs = (
        P(("groups", "rows"), None, None),
        P(("groups", "rows"), None, None),
        P(),
        P(),
        P(),
        P(),
        P(None, "rows"),
        P("rows"),
        P("rows", None),
        P(),
    )
    out_specs = (
        P(("groups", "rows"), None, None),
        P("groups", "rows"),
        P(("groups", "rows")),
        P(("groups", "rows"), None),
        P("groups", None, None),
        P("groups"),
        P("groups"),
        P("groups"),
    )
    return jax.shard_map(
        on_device, mesh=mesh, in_specs=in_specs, out_specs=out_specs, check_vma=False
    )
```

time: 297 us -> 162 us (0.55)
  waiting for transfers between devices: 154 us -> 33.4 us
  blocking collectives: 58.5 us -> 0 us
  starting transfers between devices: 10.4 us -> 66.4 us
  between operations: 15.3 us -> 2.77 us
  other arithmetic: 17.7 us -> 29 us
  matrix products: 25 us -> 16.8 us
    all_gather x2 -> x0, waiting for transfers between devices: 75.1 us -> none  [the longest x1 37.9 us: on_device(): normed_all = lax.all_gather(normed, 'rows', axis=0, tiled=True)]
    psum x1 -> x0, blocking collectives: 58.5 us -> none  [on_device(): lax.psum((gain_part, shift_part, kernel_part, bias_part), 'rows')]
    ppermute x4 -> x50, starting transfers between devices: 10.1 us -> 66.4 us  [send(): return lax.ppermute(value, 'rows', pairs)]
    reduce_scatter x1 -> x0, waiting for transfers between devices: 53.5 us -> none  [on_device(): lax.psum_scatter(contract(act_grad, up_weight, 1, 1), 'rows', scatter_dim...]
    ppermute x4 -> x50, waiting for transfers between devices: 0.01 us -> 33.4 us  [send(): return lax.ppermute(value, 'rows', pairs)]
    psum x1 -> x0, waiting for transfers between devices: 25.3 us -> none  [on_device(): lax.psum((gain_part, shift_part, kernel_part, bias_part), 'rows')]
    concatenate x0 -> x4, other arithmetic: none -> 11.5 us  [the longest x1 6.68 us: on_device(): jnp.concatenate([contract(n, act_grad, 0, 0) for n in normed_all], axis=0)]
    dot_general x1 -> x0, matrix products: 4.2 us -> none  [on_device(): jnp.dot(normed_all, up_weight, preferred_element_type=jnp.float32) + up_bias]
  transfers between devices with their start and end apart: 8 -> 50, of which waited for: 4 -> 13; matrix products, arithmetic and copies ran while one was open for 10% -> 24% of each run, Pallas kernels for 0% -> 0%
where the time goes in v1:
time: 162 us
  starting transfers between devices  66.4 us (41%)
  waiting for transfers between devices  33.4 us (21%)
  other arithmetic  29 us (18%)
  matrix products  16.8 us (10%)
  local copies, waits for them, and re-layouts  13.2 us (8%)
  between operations  2.77 us (2%)
    ppermute x50, starting transfers between devices, send(): return lax.ppermute(value, 'rows', pairs)  66.4 us
    ppermute x50, waiting for transfers between devices, send(): return lax.ppermute(value, 'rows', pairs)  33.4 us
    dot_general x10, matrix products, contract(): lax.dot_general(left, right, (((left_dim,), (right_dim,)), ((), ())), pre...  16.8 us
    concatenate x1, other arithmetic, on_device(): jnp.concatenate([contract(n, act_grad, 0, 0) for n in normed_all], axis=0)  6.68 us
    reduce_sum x1, other arithmetic, on_device(): row_mean = jnp.mean(conv_out, axis=-1, keepdims=True)  5.13 us
    concatenate x1, other arithmetic, on_device(): jnp.concatenate([contract(hidden, c, 0, 0) for c in cot_all], axis=1)  4.6 us
    convert_element_type x1, other arithmetic, on_device(): input_grad = (cotangent.astype(F32) + back_term).astype(BF16)  4.12 us
    slice x2, local copies, waits for them, and re-layouts, on_device(): depth_kernel[i, j] * padded[i:i + rows_dev, j:j + cols]  4.1 us
  transfers between devices with their start and end apart: 50, of which 13 were waited for; matrix products, arithmetic and copies ran while one was open for 24% of the time, Pallas kernels for 0%

profile of v1, /device:TPU:0, one launch (start us, length us, event | category | flops | bytes accessed | tf_op | source)
XLA Modules:
  0.0 161.6 jit_solution(11287483705252071508)
XLA Ops:
  1.7 4.1 %collective-permute-start.8 = (bf16[16,1536]{1,0:T(8,128)(2,1)S(1)}, bf16[16,1536]{1,0:T(8,128)(2,1)S(1)}, u32[]{:S(2)}, u32[]{:S(2)}) collective-permute-start(bf16[16,1536]{1,0:T(8,128)(2,1)S(1)} %get-tuple-element.164), channel_id=1, source_target_pairs={{8,0},{9,1},{10,2},{11,3},{12,4},{13,5},{14,6},{15,7},{0,8},{1,9},... | collective-permute-start | bytes 147464 | tf_op jit(solution)/shard_map/ppermute | solution.py:37
  8.8 2.9 %collective-permute-start.2 = (bf16[16,1536]{1,0:T(8,128)(2,1)S(1)}, bf16[16,1536]{1,0:T(8,128)(2,1)S(1)}, u32[]{:S(2)}, u32[]{:S(2)}) collective-permute-start(bf16[16,1536]{1,0:T(8,128)(2,1)S(1)} %get-tuple-element.165), channel_id=1, source_target_pairs={{4,0},{5,1},{6,2},{7,3},{8,4},{9,5},{10,6},{11,7},{12,8},{13,9},{1... | collective-permute-start | bytes 147464 | tf_op jit(solution)/shard_map/ppermute | solution.py:37
  15.7 2.6 %fusion.158 = (f32[1,1,3072]{2,1,0:T(1,128)S(1)}, f32[1,1,3072]{2,1,0:T(1,128)S(1)}, f32[1,1,3072]{2,1,0:T(1,128)S(1)}, f32[1,1,3072]{2,1,0:T(1,128)S(1)}, f32[1...) fusion(f32[7,7,3072]{2,1,0:T(8,128)} %param.14), kind=kLoop, calls=%fused_computation.373 | loop fusion | bytes 466944 | tf_op jit(solution)/shard_map/slice | solution.py:118
  21.6 6.3 %collective-permute-start.1 = (bf16[3,4,3072]{2,1,0:T(4,128)(2,1)S(1)}, bf16[3,4,3072]{2,1,0:T(4,128)(2,1)S(1)}, u32[]{:S(2)}, u32[]{:S(2)}) collective-permute-start(bf16[3,4,3072]{2,1,0:T(4,128)(2,1)S(1)} %get-tuple-element.167), channel_id=1, source_target_pairs={{1,0},{2,1},{3,2},{5,4},{6,5},{7,6},{8,7},{9,8},{10,9},{11,10},{13... | collective-permute-start | bytes 221192 | tf_op jit(solution)/shard_map/ppermute | solution.py:37
  30.1 5.1 %fusion.153 = (f32[4,4]{1,0:T(4,128)S(1)}, f32[4,4,3072]{2,1,0:T(4,128)S(1)}) fusion(f32[3072]{0:T(1024)S(1)} %copy-done.83, f32[3072]{0:T(1024)S(1)} %bitcast.313, f32[3072]{0:T(1024)S(1)} %bitcast.315, f32[3072]{0:T(1024)S(1)} %bitcast.319, f32[10,4,3072]{2,1,0:T(4,128)S(1)} %maximum_convert_fusion, f32[3072]{0:T(1024)S(1)} %bitcast.321, ...), kind=kLoop, calls=%fused_computation.368 | loop fusion | flops 4866032 | bytes 2678848 | tf_op jit(solution)/shard_map/reduce_sum | solution.py:120
  41.7 2.7 %collective-permute-start.12 = (bf16[16,1536]{1,0:T(8,128)(2,1)S(1)}, bf16[16,1536]{1,0:T(8,128)(2,1)S(1)}, u32[]{:S(2)}, u32[]{:S(2)}) collective-permute-start(bf16[16,1536]{1,0:T(8,128)(2,1)S(1)} %get-tuple-element.161), channel_id=1, source_target_pairs={{4,0},{5,1},{6,2},{7,3},{8,4},{9,5},{10,6},{11,7},{12,8},{13,9},{1... | collective-permute-start | bytes 147464 | tf_op jit(solution)/shard_map/ppermute | solution.py:37
  44.7 3.2 %collective-permute-done.13 = bf16[16,1536]{1,0:T(8,128)(2,1)S(1)} collective-permute-done((bf16[16,1536]{1,0:T(8,128)(2,1)S(1)}, bf16[16,1536]{1,0:T(8,128)(2,1)S(1)}, u32[]{:S(2)}, u32[]{:S(2)}) %collective-permute-start.13) | collective-permute-done | bytes 49184 | tf_op jit(solution)/shard_map/ppermute | solution.py:37
  47.9 2.7 %collective-permute-done.14 = bf16[16,1536]{1,0:T(8,128)(2,1)S(1)} collective-permute-done((bf16[16,1536]{1,0:T(8,128)(2,1)S(1)}, bf16[16,1536]{1,0:T(8,128)(2,1)S(1)}, u32[]{:S(2)}, u32[]{:S(2)}) %collective-permute-start.14) | collective-permute-done | bytes 49184 | tf_op jit(solution)/shard_map/ppermute | solution.py:37
  54.1 3.6 %collective-permute-done.15 = bf16[4,16,1536]{2,1,0:T(8,128)(2,1)S(1)} collective-permute-done((bf16[4,16,1536]{2,1,0:T(8,128)(2,1)S(1)}, bf16[4,16,1536]{2,1,0:T(8,128)(2,1)S(1)}, u32[]{:S(2)}, u32[]{:S(2)}) %collective-permute-start.15) | collective-permute-done | bytes 196640 | tf_op jit(solution)/shard_map/ppermute | solution.py:37
  58.0 2.8 %fusion = f32[256,768]{1,0:T(8,128)S(1)} fusion(bf16[256,1536]{1,0:T(8,128)(2,1)S(1)} %bitcast.277, bf16[768,3072]{1,0:T(8,128)(2,1)} %param.20), kind=kOutput, calls=%fused_computation.88 | convolution fusion | flops 603979776 | bytes 3932160 | tf_op jit(solution)/shard_map/dot_general | solution.py:62
  67.5 3.0 %fusion.162 = f32[1536,768]{1,0:T(8,128)} fusion(bf16[256,1536]{1,0:T(8,128)(2,1)S(1)} %bitcast.276, bf16[256,768]{1,0:T(8,128)(2,1)S(1)} %get-tuple-element.169), kind=kOutput, calls=%fused_computation.377 | convolution fusion | flops 603979776 | bytes 5898240 | tf_op jit(solution)/shard_map/dot_general | solution.py:62
  71.3 6.7 %pad_maximum_fusion = f32[3072,768]{1,0:T(8,128)} fusion(f32[1536,768]{1,0:T(8,128)S(1)} %fusion.163, f32[1536,768]{1,0:T(8,128)} %fusion.162), kind=kLoop, calls=%fused_computation.84 | loop fusion | flops 2359296 | bytes 18874368 | tf_op jit(solution)/shard_map/concatenate | solution.py:153
  78.0 3.0 %fusion.151 = f32[768,1536]{1,0:T(8,128)} fusion(bf16[256,1536]{1,0:T(8,128)(2,1)S(1)} %bitcast.280, f32[256,768]{1,0:T(8,128)S(1)} %fusion.13), kind=kOutput, calls=%fused_computation.367 | convolution fusion | flops 604962816 | bytes 6291456 | tf_op jit(solution)/shard_map/dot_general | solution.py:62
  83.4 5.5 %collective-permute-done.28 = bf16[4,16,1536]{2,1,0:T(8,128)(2,1)S(1)} collective-permute-done((bf16[4,16,1536]{2,1,0:T(8,128)(2,1)S(1)}, bf16[4,16,1536]{2,1,0:T(8,128)(2,1)S(1)}, u32[]{:S(2)}, u32[]{:S(2)}) %collective-permute-start.28) | collective-permute-done | bytes 196640 | tf_op jit(solution)/shard_map/ppermute | solution.py:37
  89.8 3.1 %collective-permute-start.31 = (bf16[16,1536]{1,0:T(8,128)(2,1)S(1)}, bf16[16,1536]{1,0:T(8,128)(2,1)S(1)}, u32[]{:S(2)}, u32[]{:S(2)}) collective-permute-start(bf16[16,1536]{1,0:T(8,128)(2,1)S(1)} %get-tuple-element.138), channel_id=1, source_target_pairs={{0,12},{1,13},{2,14},{3,15},{4,0},{5,1},{6,2},{7,3},{8,4},{9,5},{1... | collective-permute-start | bytes 147464 | tf_op jit(solution)/shard_map/ppermute | solution.py:37
  111.8 2.6 %collective-permute-start.41 = (bf16[7,1536]{1,0:T(8,128)(2,1)}, bf16[7,1536]{1,0:T(8,128)(2,1)}, u32[]{:S(2)}, u32[]{:S(2)}) collective-permute-start(bf16[7,1536]{1,0:T(8,128)(2,1)} %bitcast.263), channel_id=1, source_target_pairs={{0,14},{1,15},{2,0},{3,1},{4,2},{5,3},{6,4},{7,5},{8,6},{9,7},{10,... | collective-permute-start | bytes 64520 | tf_op jit(solution)/shard_map/ppermute | solution.py:37
  114.4 4.6 %pad_maximum_fusion.1 = f32[768,3072]{1,0:T(8,128)} fusion(f32[768,1536]{1,0:T(8,128)S(1)} %fusion.150, f32[768,1536]{1,0:T(8,128)S(1)} %bitcast.272), kind=kLoop, calls=%fused_computation.85 | loop fusion | flops 2359296 | bytes 18874368 | tf_op jit(solution)/shard_map/concatenate | solution.py:152
  122.1 2.8 %collective-permute-start.38 = (bf16[7,1536]{1,0:T(8,128)(2,1)S(1)}, bf16[7,1536]{1,0:T(8,128)(2,1)S(1)}, u32[]{:S(2)}, u32[]{:S(2)}) collective-permute-start(bf16[7,1536]{1,0:T(8,128)(2,1)S(1)} %bitcast.453), channel_id=1, source_target_pairs={{0,8},{1,9},{2,10},{3,11},{4,12},{5,13},{6,14},{7,15},{8,0},{9,1},... | collective-permute-start | bytes 64520 | tf_op jit(solution)/shard_map/ppermute | solution.py:37
  124.9 2.9 %collective-permute-start.40 = (bf16[7,1536]{1,0:T(8,128)(2,1)S(1)}, bf16[7,1536]{1,0:T(8,128)(2,1)S(1)}, u32[]{:S(2)}, u32[]{:S(2)}) collective-permute-start(bf16[7,1536]{1,0:T(8,128)(2,1)S(1)} %bitcast.451), channel_id=1, source_target_pairs={{0,12},{1,13},{2,14},{3,15},{4,0},{5,1},{6,2},{7,3},{8,4},{9,5},{1... | collective-permute-start | bytes 64520 | tf_op jit(solution)/shard_map/ppermute | solution.py:37
  129.8 6.3 %collective-permute-start.33 = (bf16[3,4,3072]{2,1,0:T(4,128)(2,1)S(1)}, bf16[3,4,3072]{2,1,0:T(4,128)(2,1)S(1)}, u32[]{:S(2)}, u32[]{:S(2)}) collective-permute-start(bf16[3,4,3072]{2,1,0:T(4,128)(2,1)S(1)} %get-tuple-element.157), channel_id=1, source_target_pairs={{1,0},{2,1},{3,2},{5,4},{6,5},{7,6},{8,7},{9,8},{10,9},{11,10},{13... | collective-permute-start | bytes 221192 | tf_op jit(solution)/shard_map/ppermute | solution.py:37
  138.9 4.2 %collective-permute-start.45 = (bf16[7,1536]{1,0:T(8,128)(2,1)S(1)}, bf16[7,1536]{1,0:T(8,128)(2,1)S(1)}, u32[]{:S(2)}, u32[]{:S(2)}) collective-permute-start(bf16[7,1536]{1,0:T(8,128)(2,1)S(1)} %get-tuple-element.64), channel_id=1, source_target_pairs={{8,0},{9,1},{10,2},{11,3},{12,4},{13,5},{14,6},{15,7},{0,8},{1,9},... | collective-permute-start | bytes 64520 | tf_op jit(solution)/shard_map/ppermute | solution.py:37
  143.1 3.0 %collective-permute-start.43 = (bf16[7,1536]{1,0:T(8,128)(2,1)S(1)}, bf16[7,1536]{1,0:T(8,128)(2,1)S(1)}, u32[]{:S(2)}, u32[]{:S(2)}) collective-permute-start(bf16[7,1536]{1,0:T(8,128)(2,1)S(1)} %get-tuple-element.64), channel_id=1, source_target_pairs={{4,0},{5,1},{6,2},{7,3},{8,4},{9,5},{10,6},{11,7},{12,8},{13,9},{1... | collective-permute-start | bytes 64520 | tf_op jit(solution)/shard_map/ppermute | solution.py:37
  148.7 6.3 %collective-permute-done.48 = bf16[7,1536]{1,0:T(8,128)(2,1)S(1)} collective-permute-done((bf16[7,1536]{1,0:T(8,128)(2,1)S(1)}, bf16[7,1536]{1,0:T(8,128)(2,1)S(1)}, u32[]{:S(2)}, u32[]{:S(2)}) %collective-permute-start.48) | collective-permute-done | bytes 21536 | tf_op jit(solution)/shard_map/ppermute | solution.py:37
  155.6 4.1 %fusion.37 = bf16[4,4,3072]{2,1,0:T(4,128)(2,1)} fusion(bf16[4,4,3072]{2,1,0:T(4,128)(2,1)S(1)} %copy-done.3, f32[10,4,3072]{2,1,0:T(4,128)S(1)} %maximum_convert_fusion.1, f32[3072]{0:T(1024)S(1)} %bitcast.314, f32[3072]{0:T(1024)S(1)} %bitcast.316, f32[3072]{0:T(1024)S(1)} %bitcast.320, f32[3072]{0:T(1024)S(1)} %bitcast.322, f32[3072]{0:T(1024)S(1)} %bitcast.324, ...), kind=kLoop, calls=%fused_computation.143 | loop fusion | flops 4915200 | bytes 2666496 | tf_op jit(solution)/shard_map/convert_element_type | solution.py:212
  (356 shorter events, 64.5 us)
Async XLA Ops:
  1.7 17.9 %collective-permute-start.8 = (bf16[16,1536]{1,0:T(8,128)(2,1)S(1)}, bf16[16,1536]{1,0:T(8,128)(2,1)S(1)}, u32[]{:S(2)}, u32[]{:S(2)}) collective-permute-start(bf16[16,1536]{1,0:T(8,128)(2,1)S(1)} %get-tuple-element.164), channel_id=1, source_target_pairs={{8,0},{9,1},{10,2},{11,3},{12,4},{13,5},{14,6},{15,7},{0,8},{1,9},... | collective-permute-start | bytes 147464 | tf_op jit(solution)/shard_map/ppermute | solution.py:37
  5.8 13.9 %collective-permute-start.7 = (bf16[16,1536]{1,0:T(8,128)(2,1)S(1)}, bf16[16,1536]{1,0:T(8,128)(2,1)S(1)}, u32[]{:S(2)}, u32[]{:S(2)}) collective-permute-start(bf16[16,1536]{1,0:T(8,128)(2,1)S(1)} %get-tuple-element.164), channel_id=1, source_target_pairs={{4,0},{5,1},{6,2},{7,3},{8,4},{9,5},{10,6},{11,7},{12,8},{13,9},{1... | collective-permute-start | bytes 147464 | tf_op jit(solution)/shard_map/ppermute | solution.py:37
  7.1 14.5 %collective-permute-start.9 = (bf16[16,1536]{1,0:T(8,128)(2,1)S(1)}, bf16[16,1536]{1,0:T(8,128)(2,1)S(1)}, u32[]{:S(2)}, u32[]{:S(2)}) collective-permute-start(bf16[16,1536]{1,0:T(8,128)(2,1)S(1)} %get-tuple-element.164), channel_id=1, source_target_pairs={{12,0},{13,1},{14,2},{15,3},{0,4},{1,5},{2,6},{3,7},{4,8},{5,9},{6... | collective-permute-start | bytes 147464 | tf_op jit(solution)/shard_map/ppermute | solution.py:37
  7.8 28.3 %collective-permute-start.3 = (bf16[16,1536]{1,0:T(8,128)(2,1)S(1)}, bf16[16,1536]{1,0:T(8,128)(2,1)S(1)}, u32[]{:S(2)}, u32[]{:S(2)}) collective-permute-start(bf16[16,1536]{1,0:T(8,128)(2,1)S(1)} %get-tuple-element.165), channel_id=1, source_target_pairs={{8,0},{9,1},{10,2},{11,3},{12,4},{13,5},{14,6},{15,7},{0,8},{1,9},... | collective-permute-start | bytes 147464 | tf_op jit(solution)/shard_map/ppermute | solution.py:37
  8.8 28.4 %collective-permute-start.2 = (bf16[16,1536]{1,0:T(8,128)(2,1)S(1)}, bf16[16,1536]{1,0:T(8,128)(2,1)S(1)}, u32[]{:S(2)}, u32[]{:S(2)}) collective-permute-start(bf16[16,1536]{1,0:T(8,128)(2,1)S(1)} %get-tuple-element.165), channel_id=1, source_target_pairs={{4,0},{5,1},{6,2},{7,3},{8,4},{9,5},{10,6},{11,7},{12,8},{13,9},{1... | collective-permute-start | bytes 147464 | tf_op jit(solution)/shard_map/ppermute | solution.py:37
  19.6 18.6 %collective-permute-start.4 = (bf16[16,1536]{1,0:T(8,128)(2,1)S(1)}, bf16[16,1536]{1,0:T(8,128)(2,1)S(1)}, u32[]{:S(2)}, u32[]{:S(2)}) collective-permute-start(bf16[16,1536]{1,0:T(8,128)(2,1)S(1)} %get-tuple-element.165), channel_id=1, source_target_pairs={{12,0},{13,1},{14,2},{15,3},{0,4},{1,5},{2,6},{3,7},{4,8},{5,9},{6... | collective-permute-start | bytes 147464 | tf_op jit(solution)/shard_map/ppermute | solution.py:37
  19.7 8.4 %collective-permute-start = (bf16[3,4,3072]{2,1,0:T(4,128)(2,1)S(1)}, bf16[3,4,3072]{2,1,0:T(4,128)(2,1)S(1)}, u32[]{:S(2)}, u32[]{:S(2)}) collective-permute-start(bf16[3,4,3072]{2,1,0:T(4,128)(2,1)S(1)} %get-tuple-element.166), channel_id=1, source_target_pairs={{0,1},{1,2},{2,3},{4,5},{5,6},{6,7},{7,8},{8,9},{9,10},{10,11},{12... | collective-permute-start | bytes 221192 | tf_op jit(solution)/shard_map/ppermute | solution.py:37
  28.1 23.9 %collective-permute-start.10 = (bf16[4,16,1536]{2,1,0:T(8,128)(2,1)S(1)}, bf16[4,16,1536]{2,1,0:T(8,128)(2,1)S(1)}, u32[]{:S(2)}, u32[]{:S(2)}) collective-permute-start(bf16[4,16,1536]{2,1,0:T(8,128)(2,1)S(1)} %get-tuple-element.147), channel_id=1, source_target_pairs={{2,0},{3,1},{0,2},{1,3},{6,4},{7,5},{4,6},{5,7},{10,8},{11,9},{8,1... | collective-permute-start | bytes 589832 | tf_op jit(solution)/shard_map/ppermute | solution.py:37
  38.3 13.9 %collective-permute-start.5 = (bf16[4,16,1536]{2,1,0:T(8,128)(2,1)S(1)}, bf16[4,16,1536]{2,1,0:T(8,128)(2,1)S(1)}, u32[]{:S(2)}, u32[]{:S(2)}) collective-permute-start(bf16[4,16,1536]{2,1,0:T(8,128)(2,1)S(1)} %get-tuple-element.145), channel_id=1, source_target_pairs={{2,0},{3,1},{0,2},{1,3},{6,4},{7,5},{4,6},{5,7},{10,8},{11,9},{8,1... | collective-permute-start | bytes 589832 | tf_op jit(solution)/shard_map/ppermute | solution.py:37
  52.2 8.6 %collective-permute-start.6 = (bf16[2,4,16,1536]{3,2,1,0:T(8,128)(2,1)S(1)}, bf16[2,4,16,1536]{3,2,1,0:T(8,128)(2,1)S(1)}, u32[]{:S(2)}, u32[]{:S(2)}) collective-permute-start(bf16[2,4,16,1536]{3,2,1,0:T(8,128)(2,1)S(1)} %get-tuple-element.129), channel_id=1, source_target_pairs={{1,0},{0,1},{3,2},{2,3},{5,4},{4,5},{7,6},{6,7},{9,8},{8,9},{11,10... | collective-permute-start | bytes 1179656 | tf_op jit(solution)/shard_map/ppermute | solution.py:37
  70.6 10.4 %collective-permute-start.27 = (bf16[2,4,16,1536]{3,2,1,0:T(8,128)(2,1)S(1)}, bf16[2,4,16,1536]{3,2,1,0:T(8,128)(2,1)S(1)}, u32[]{:S(2)}, u32[]{:S(2)}) collective-permute-start(bf16[2,4,16,1536]{3,2,1,0:T(8,128)(2,1)S(1)} %bitcast.290), channel_id=1, source_target_pairs={{0,1},{1,0},{2,3},{3,2},{4,5},{5,4},{6,7},{7,6},{8,9},{9,8},{10,11... | collective-permute-start | bytes 1179656 | tf_op jit(solution)/shard_map/ppermute | solution.py:37
  71.2 11.0 %collective-permute-start.22 = (bf16[2,4,16,1536]{3,2,1,0:T(8,128)(2,1)S(1)}, bf16[2,4,16,1536]{3,2,1,0:T(8,128)(2,1)S(1)}, u32[]{:S(2)}, u32[]{:S(2)}) collective-permute-start(bf16[2,4,16,1536]{3,2,1,0:T(8,128)(2,1)S(1)} %bitcast.289), channel_id=1, source_target_pairs={{0,1},{1,0},{2,3},{3,2},{4,5},{5,4},{6,7},{7,6},{8,9},{9,8},{10,11... | collective-permute-start | bytes 1179656 | tf_op jit(solution)/shard_map/ppermute | solution.py:37
  82.3 10.5 %collective-permute-start.23 = (bf16[4,16,1536]{2,1,0:T(8,128)(2,1)S(1)}, bf16[4,16,1536]{2,1,0:T(8,128)(2,1)S(1)}, u32[]{:S(2)}, u32[]{:S(2)}) collective-permute-start(bf16[4,16,1536]{2,1,0:T(8,128)(2,1)S(1)} %slice_bitcast_fusion.2), channel_id=1, source_target_pairs={{0,2},{1,3},{2,0},{3,1},{4,6},{5,7},{6,4},{7,5},{8,10},{9,11},{10,... | collective-permute-start | bytes 589832 | tf_op jit(solution)/shard_map/ppermute | solution.py:37
  111.8 13.1 %collective-permute-start.41 = (bf16[7,1536]{1,0:T(8,128)(2,1)}, bf16[7,1536]{1,0:T(8,128)(2,1)}, u32[]{:S(2)}, u32[]{:S(2)}) collective-permute-start(bf16[7,1536]{1,0:T(8,128)(2,1)} %bitcast.263), channel_id=1, source_target_pairs={{0,14},{1,15},{2,0},{3,1},{4,2},{5,3},{6,4},{7,5},{8,6},{9,7},{10,... | collective-permute-start | bytes 64520 | tf_op jit(solution)/shard_map/ppermute | solution.py:37
  114.4 10.5 %collective-permute-start.35 = (bf16[7,1536]{1,0:T(8,128)(2,1)}, bf16[7,1536]{1,0:T(8,128)(2,1)}, u32[]{:S(2)}, u32[]{:S(2)}) collective-permute-start(bf16[7,1536]{1,0:T(8,128)(2,1)} %bitcast.269), channel_id=1, source_target_pairs={{0,2},{1,3},{2,4},{3,5},{4,6},{5,7},{6,8},{7,9},{8,10},{9,11},{10,... | collective-permute-start | bytes 64520 | tf_op jit(solution)/shard_map/ppermute | solution.py:37
  119.6 10.2 %collective-permute-start.37 = (bf16[7,1536]{1,0:T(8,128)(2,1)S(1)}, bf16[7,1536]{1,0:T(8,128)(2,1)S(1)}, u32[]{:S(2)}, u32[]{:S(2)}) collective-permute-start(bf16[7,1536]{1,0:T(8,128)(2,1)S(1)} %bitcast.454), channel_id=1, source_target_pairs={{0,6},{1,7},{2,8},{3,9},{4,10},{5,11},{6,12},{7,13},{8,14},{9,15},... | collective-permute-start | bytes 64520 | tf_op jit(solution)/shard_map/ppermute | solution.py:37
  122.1 14.1 %collective-permute-start.38 = (bf16[7,1536]{1,0:T(8,128)(2,1)S(1)}, bf16[7,1536]{1,0:T(8,128)(2,1)S(1)}, u32[]{:S(2)}, u32[]{:S(2)}) collective-permute-start(bf16[7,1536]{1,0:T(8,128)(2,1)S(1)} %bitcast.453), channel_id=1, source_target_pairs={{0,8},{1,9},{2,10},{3,11},{4,12},{5,13},{6,14},{7,15},{8,0},{9,1},... | collective-permute-start | bytes 64520 | tf_op jit(solution)/shard_map/ppermute | solution.py:37
  124.9 11.3 %collective-permute-start.39 = (bf16[7,1536]{1,0:T(8,128)(2,1)S(1)}, bf16[7,1536]{1,0:T(8,128)(2,1)S(1)}, u32[]{:S(2)}, u32[]{:S(2)}) collective-permute-start(bf16[7,1536]{1,0:T(8,128)(2,1)S(1)} %bitcast.452), channel_id=1, source_target_pairs={{0,10},{1,11},{2,12},{3,13},{4,14},{5,15},{6,0},{7,1},{8,2},{9,3},... | collective-permute-start | bytes 64520 | tf_op jit(solution)/shard_map/ppermute | solution.py:37
  124.9 11.3 %collective-permute-start.40 = (bf16[7,1536]{1,0:T(8,128)(2,1)S(1)}, bf16[7,1536]{1,0:T(8,128)(2,1)S(1)}, u32[]{:S(2)}, u32[]{:S(2)}) collective-permute-start(bf16[7,1536]{1,0:T(8,128)(2,1)S(1)} %bitcast.451), channel_id=1, source_target_pairs={{0,12},{1,13},{2,14},{3,15},{4,0},{5,1},{6,2},{7,3},{8,4},{9,5},{1... | collective-permute-start | bytes 64520 | tf_op jit(solution)/shard_map/ppermute | solution.py:37
  127.9 9.2 %collective-permute-start.32 = (bf16[3,4,3072]{2,1,0:T(4,128)(2,1)S(1)}, bf16[3,4,3072]{2,1,0:T(4,128)(2,1)S(1)}, u32[]{:S(2)}, u32[]{:S(2)}) collective-permute-start(bf16[3,4,3072]{2,1,0:T(4,128)(2,1)S(1)} %get-tuple-element.156), channel_id=1, source_target_pairs={{0,1},{1,2},{2,3},{4,5},{5,6},{6,7},{7,8},{8,9},{9,10},{10,11},{12... | collective-permute-start | bytes 221192 | tf_op jit(solution)/shard_map/ppermute | solution.py:37
  129.8 8.5 %collective-permute-start.33 = (bf16[3,4,3072]{2,1,0:T(4,128)(2,1)S(1)}, bf16[3,4,3072]{2,1,0:T(4,128)(2,1)S(1)}, u32[]{:S(2)}, u32[]{:S(2)}) collective-permute-start(bf16[3,4,3072]{2,1,0:T(4,128)(2,1)S(1)} %get-tuple-element.157), channel_id=1, source_target_pairs={{1,0},{2,1},{3,2},{5,4},{6,5},{7,6},{8,7},{9,8},{10,9},{11,10},{13... | collective-permute-start | bytes 221192 | tf_op jit(solution)/shard_map/ppermute | solution.py:37
  138.4 10.3 %collective-permute-start.47 = (bf16[7,1536]{1,0:T(8,128)(2,1)S(1)}, bf16[7,1536]{1,0:T(8,128)(2,1)S(1)}, u32[]{:S(2)}, u32[]{:S(2)}) collective-permute-start(bf16[7,1536]{1,0:T(8,128)(2,1)S(1)} %get-tuple-element.64), channel_id=1, source_target_pairs={{12,0},{13,1},{14,2},{15,3},{0,4},{1,5},{2,6},{3,7},{4,8},{5,9},{6... | collective-permute-start | bytes 64520 | tf_op jit(solution)/shard_map/ppermute | solution.py:37
  138.5 10.2 %collective-permute-start.46 = (bf16[7,1536]{1,0:T(8,128)(2,1)S(1)}, bf16[7,1536]{1,0:T(8,128)(2,1)S(1)}, u32[]{:S(2)}, u32[]{:S(2)}) collective-permute-start(bf16[7,1536]{1,0:T(8,128)(2,1)S(1)} %get-tuple-element.64), channel_id=1, source_target_pairs={{10,0},{11,1},{12,2},{13,3},{14,4},{15,5},{0,6},{1,7},{2,8},{3,9},... | collective-permute-start | bytes 64520 | tf_op jit(solution)/shard_map/ppermute | solution.py:37
  138.9 9.8 %collective-permute-start.45 = (bf16[7,1536]{1,0:T(8,128)(2,1)S(1)}, bf16[7,1536]{1,0:T(8,128)(2,1)S(1)}, u32[]{:S(2)}, u32[]{:S(2)}) collective-permute-start(bf16[7,1536]{1,0:T(8,128)(2,1)S(1)} %get-tuple-element.64), channel_id=1, source_target_pairs={{8,0},{9,1},{10,2},{11,3},{12,4},{13,5},{14,6},{15,7},{0,8},{1,9},... | collective-permute-start | bytes 64520 | tf_op jit(solution)/shard_map/ppermute | solution.py:37
  (118 other events, 2485.4 us)

commit v2 on v1

--- a/solution.py
+++ b/solution.py
@@ -1,6 +1,8 @@
 import jax
 import jax.numpy as jnp
 from jax import lax
+from jax.experimental import pallas as pl
+from jax.experimental.pallas import tpu as pltpu
 from jax.sharding import PartitionSpec as P
 
 IMG_ROWS = 32
@@ -70,7 +72,7 @@
     return jnp.concatenate([send(tail, fwd), cells, send(head, bwd)], axis=0)
 
 
-def on_device(
+def generic_device(
     features,
     cotangent,
     depth_kernel,
@@ -222,6 +224,511 @@
     )
 
 
+LANES = 128
+VMEM = pltpu.VMEM
+VSPEC = pl.BlockSpec(memory_space=pltpu.VMEM)
+SSPEC = pl.BlockSpec(memory_space=pltpu.SMEM)
+PARAMS = pltpu.CompilerParams(vmem_limit_bytes=40 * 1024 * 1024)
+GRID_PARAMS = pltpu.CompilerParams(
+    vmem_limit_bytes=40 * 1024 * 1024, dimension_semantics=("arbitrary",)
+)
+EXACT = lax.Precision.HIGHEST
+
+
+def z_pairs(step):
+    return from_ahead(16, 4, 4, step)
+
+
+Y_PAIRS = from_ahead(16, 2, 2, 1)
+C_PAIRS = from_ahead(16, 1, 2, 1)
+
+
+def gather_tokens(shard):
+    planes = [shard] + [send(shard, z_pairs(step)) for step in (1, 2, 3)]
+    across = [send(plane, Y_PAIRS) for plane in planes]
+    core_planes = send(jnp.stack(planes), C_PAIRS)
+    core_across = send(jnp.stack(across), C_PAIRS)
+    return (*planes, *across, core_planes, core_across)
+
+
+def each_piece(idx, pieces):
+    z, y, c = idx[0], idx[1], idx[2]
+    for yr in range(2):
+        for cr in range(2):
+            for step in range(4):
+                if cr == 0:
+                    piece = pieces[4 * yr + step]
+                else:
+                    piece = pieces[8 + yr].at[step]
+                place = (z + step + 3) % 4
+                image = place // 2
+                row = 16 * (place % 2) + 8 * ((y + yr) % 2) + 4 * ((c + cr) % 2)
+                yield piece, image, row
+
+
+def lane_tile(tile):
+    return pl.ds(pl.multiple_of(tile * LANES, LANES), LANES)
+
+
+def conv_norm_kernel(idx, *refs):
+    pieces = refs[:10]
+    kern, bias, gain, shift = refs[10:14]
+    normed, f_slice, u_slice, inv_slice = refs[14:18]
+    feats, conv, total, mean_ref, inv_ref = refs[18:]
+    tiles = feats.shape[0]
+    edge = jnp.zeros((tiles, 8, 8, LANES), F32)
+    feats[:, :, 0:8, :] = edge
+    feats[:, :, 40:48, :] = edge
+    for piece, image, row in each_piece(idx, pieces):
+        for tile in range(tiles):
+            block = piece[:, tile * LANES : (tile + 1) * LANES].astype(F32)
+            for col in range(4):
+                feats[tile, image * 4 + col, pl.ds(8 + row, 4), :] = block[
+                    4 * col : 4 * col + 4
+                ]
+    total[...] = jnp.zeros_like(total)
+
+    def conv_tile(tile, carry):
+        lanes = lane_tile(tile)
+        for image in range(2):
+            for part in range(2):
+                acc = [jnp.broadcast_to(bias[0:1, lanes], (16, LANES))] * 4
+                for i in range(7):
+                    for src in range(4):
+                        rows = feats[tile, image * 4 + src, pl.ds(5 + 16 * part + i, 16), :]
+                        for col in range(4):
+                            j = src - col + 3
+                            acc[col] = acc[col] + kern[i, j : j + 1, lanes] * rows
+                for col in range(4):
+                    at = pl.ds(image * 128 + col * 32 + 16 * part, 16)
+                    conv[tile, at, :] = acc[col]
+                    total[at, :] = total[at, :] + acc[col]
+        return carry
+
+    lax.fori_loop(0, tiles, conv_tile, 0)
+    channels = tiles * LANES
+    mean = jnp.sum(total[...], axis=-1, keepdims=True) / channels
+    mean_ref[...] = jnp.broadcast_to(mean, mean_ref.shape)
+    total[...] = jnp.zeros_like(total)
+
+    def square_tile(tile, carry):
+        centred = conv[tile] - mean_ref[...]
+        total[...] = total[...] + centred * centred
+        return carry
+
+    lax.fori_loop(0, tiles, square_tile, 0)
+    spread = jnp.sum(total[...], axis=-1, keepdims=True) / channels
+    inv_ref[...] = jnp.broadcast_to(lax.rsqrt(spread + 1e-06), inv_ref.shape)
+    place = lax.broadcasted_iota(jnp.int32, (16, LANES), 0)
+
+    def norm_tile(tile, carry):
+        lanes = lane_tile(tile)
+        scale, offset = gain[0:1, lanes], shift[0:1, lanes]
+        unit = (conv[tile] - mean_ref[...]) * inv_ref[...]
+        normed[pl.ds(0, 256), lanes] = (unit * scale + offset).astype(BF16)
+        scale_hi = scale.astype(BF16).astype(F32)
+        offset_hi = offset.astype(BF16).astype(F32)
+        extra = jnp.where(place == 0, scale_hi, 0.0)
+        extra = jnp.where(place == 1, scale - scale_hi, extra)
+        extra = jnp.where(place == 2, offset_hi, extra)
+        extra = jnp.where(place == 3, offset - offset_hi, extra)
+        normed[pl.ds(256, 16), lanes] = extra.astype(BF16)
+        return carry
+
+    lax.fori_loop(0, tiles, norm_tile, 0)
+    chip, core = idx[0] * 2 + idx[1], idx[2]
+    own = pl.ds(pl.multiple_of(core * 128, 128), 128)
+    inv_slice[...] = inv_ref[own, :]
+    for k in range(3):
+        tile = chip * 3 + k
+        u_slice[k] = (conv[tile, own, :] - mean_ref[own, :]) * inv_ref[own, :]
+        for col in range(4):
+            f_slice[k, col] = feats[tile, core * 4 + col]
+
+
+def cot_kernel(idx, *refs):
+    pieces = refs[:10]
+    layer_scale, cot_all, cot_slice, raw = refs[10:]
+    tiles = cot_all.shape[1] // LANES
+    for piece, image, row in each_piece(idx, pieces):
+        for tile in range(tiles):
+            block = piece[:, tile * LANES : (tile + 1) * LANES].astype(F32)
+            for col in range(4):
+                raw[tile, pl.ds(image * 128 + col * 32 + row, 4), :] = block[
+                    4 * col : 4 * col + 4
+                ]
+    for tile in range(tiles):
+        lanes = slice(tile * LANES, (tile + 1) * LANES)
+        cot_all[:, lanes] = (raw[tile] * layer_scale[0:1, lanes]).astype(BF16)
+    chip, core = idx[0] * 2 + idx[1], idx[2]
+    for k in range(3):
+        cot_slice[k] = raw[chip * 3 + k, pl.ds(pl.multiple_of(core * 128, 128), 128), :]
+
+
+def up_kernel(normed, weight, up_bias, hidden, slope, centred, gain_dot):
+    product = jnp.dot(normed[...], weight[...], preferred_element_type=F32)
+    plain = product[0:256]
+    pre_act = plain + up_bias[0:1, :]
+    cdf = 0.5 * (1.0 + lax.erf(pre_act * 0.7071067811865476))
+    hidden[...] = (pre_act * cdf).astype(BF16)
+    slope[...] = cdf + pre_act * jnp.exp(-0.5 * pre_act * pre_act) * 0.3989422804014327
+    centred[...] = plain - (product[258:259] + product[259:260])
+    gain_dot[...] = jnp.broadcast_to(product[256:257] + product[257:258], gain_dot.shape)
+
+
+def act_kernel(cot_all, weight, slope, centred, gain_dot, act_grad, bias_grad, sums, first, second):
+    hid_grad = contract(cot_all[...], weight[...], 1, 1)
+    act = (hid_grad * slope[...]).astype(BF16)
+    act_grad[...] = act
+    act = act.astype(F32)
+    bias_grad[...] = jnp.broadcast_to(jnp.sum(act, axis=0, keepdims=True), bias_grad.shape)
+
+    @pl.when(pl.program_id(0) == 0)
+    def _():
+        first[...] = jnp.zeros_like(first)
+        second[...] = jnp.zeros_like(second)
+
+    for tile in range(act.shape[1] // LANES):
+        lanes = slice(tile * LANES, (tile + 1) * LANES)
+        first[...] = first[...] + act[:, lanes] * gain_dot[0:1, lanes]
+        second[...] = second[...] + act[:, lanes] * centred[:, lanes]
+
+    @pl.when(pl.program_id(0) == pl.num_programs(0) - 1)
+    def _():
+        ones = jnp.ones((8, LANES), F32)
+        for image in range(2):
+            at = slice(image * 128, (image + 1) * 128)
+            for row, ref in ((0, first), (8, second)):
+                sums[image, row : row + 8, :] = lax.dot_general(
+                    ones, ref[at, :], (((1,), (1,)), ((), ())),
+                    precision=EXACT, preferred_element_type=F32,
+                )
+
+
+def norm_grad_kernel(idx, act_grad, weight, sums, keep, away):
+    core = idx[2]
+    for ref, image in ((keep, core), (away, 1 - core)):
+        at = pl.ds(pl.multiple_of(image * 128, 128), 128)
+        ref[0, 0:128, :] = contract(act_grad[at, :], weight[...], 1, 1).astype(ref.dtype)
+        ref[0, 128:144, 0:128] = sums[image].astype(ref.dtype)
+        ref[0, 128:144, 128:384] = jnp.zeros((16, 256), ref.dtype)
+
+
+def conv_back_kernel(
+    idx, own, near_1, near_2, near_3, f_slice, u_slice, inv_slice, gain, kern, cot_slice,
+    ig_keep, core_msg, small_keep, cg, back, small,
+):
+    chip, y, core = idx[0] * 2 + idx[1], idx[1], idx[2]
+    channels = gain.shape[1]
+
+    def summed(rows, lanes):
+        return (
+            own[rows, lanes]
+            + near_1[rows, lanes].astype(F32)
+            + near_2[rows, lanes].astype(F32)
+            + near_3[rows, lanes].astype(F32)
+        )
+
+    sums = summed(slice(128, 144), slice(0, 128))
+    place = lax.broadcasted_iota(jnp.int32, (16, LANES), 0)
+
+    def per_token(row):
+        pick = jnp.where(place == row, 1.0 / channels, 0.0).astype(F32)
+        return lax.dot_general(
+            sums, pick, (((0,), (0,)), ((), ())), precision=EXACT, preferred_element_type=F32
+        )
+
+    mean_1, mean_2 = per_token(0), per_token(8)
+    cg[:, :, 0:8, :] = jnp.zeros((3, 4, 8, LANES), F32)
+    cg[:, :, 40:48, :] = jnp.zeros((3, 4, 8, LANES), F32)
+    small[...] = jnp.zeros_like(small)
+    for k in range(3):
+        lanes = slice(k * LANES, (k + 1) * LANES)
+        wide = lane_tile(chip * 3 + k)
+        norm_grad = summed(slice(0, 128), lanes)
+        unit = u_slice[k]
+        scaled = norm_grad * gain[0:1, wide]
+        grad = inv_slice[...] * (scaled - mean_1 - unit * mean_2)
+        for col in range(4):
+            cg[k, col, 8:40, :] = grad[32 * col : 32 * col + 32]
+        small[56:57, lanes] = jnp.sum(norm_grad * unit, axis=0, keepdims=True)
+        small[57:58, lanes] = jnp.sum(norm_grad, axis=0, keepdims=True)
+        small[58:59, lanes] = jnp.sum(grad, axis=0, keepdims=True)
+        for i in range(7):
+            acc = [None] * 7
+            for src in range(4):
+                rows = f_slice[k, src, 5 + i : 37 + i, :]
+                for col in range(4):
+                    j = src - col + 3
+                    term = cg[k, col, 8:40, :] * rows
+                    acc[j] = term if acc[j] is None else acc[j] + term
+            for j in range(7):
+                small[8 * i + j : 8 * i + j + 1, lanes] = jnp.sum(acc[j], axis=0, keepdims=True)
+        for part in range(2):
+            acc = [
+                cot_slice[k, 32 * col + 16 * part : 32 * col + 16 * part + 16, :]
+                for col in range(4)
+            ]
+            for i in range(7):
+                for src in range(4):
+                    start = 11 + 16 * part - i
+                    rows = cg[k, src, start : start + 16, :]
+                    for col in range(4):
+                        j = col - src + 3
+                        acc[col] = acc[col] + kern[i, j : j + 1, wide] * rows
+            for col in range(4):
+                back[k, col, 16 * part : 16 * part + 16, :] = acc[col]
+        for half in range(2):
+            for yr in range(2):
+                for cr in range(2):
+                    start = 16 * half + 8 * ((y + yr) % 2) + 4 * ((core + cr) % 2)
+                    block = jnp.concatenate(
+                        [back[k, col, pl.ds(start, 4), :] for col in range(4)], axis=0
+                    )
+                    ref = core_msg if cr else ig_keep
+                    ref[2 * half + yr, :, lanes] = block.astype(BF16)
+    for part in range(2):
+        away = pl.ds(pl.multiple_of(32 * (1 - core) + 16 * part, 16), 16)
+        core_msg[4 + part] = small[away, :].astype(BF16)
+        mine = pl.ds(pl.multiple_of(32 * core + 16 * part, 16), 16)
+        small_keep[part] = small[mine, :]
+
+
+def route_kernel(idx, ig_keep, core_msg, small_keep, *msgs):
+    z, core = idx[0], idx[2]
+    total = [
+        (small_keep[part] + core_msg[4 + part].astype(F32)).astype(BF16) for part in range(2)
+    ]
+    for step in range(4):
+        place = (z + step + 3) % 4
+        image, half = place // 2, place % 2
+        for yr in range(2):
+            kept, came = ig_keep[2 * half + yr], core_msg[2 * half + yr]
+            msgs[step][yr] = jnp.where(image == core, kept, came)
+        for part in range(2):
+            msgs[step][2 + part] = total[part]
+
+
+def place_kernel(idx, *refs):
+    msgs, came, core_a, core_b = refs[:4], refs[4], refs[5], refs[6]
+    tokens, small = refs[7], refs[8]
+    z, y, core = idx[0], idx[1], idx[2]
+    for step in range(4):
+        plane = (z + 4 - step) % 4
+        for yr in range(2):
+            chip = plane * 2 + (y + yr) % 2
+            lanes = pl.ds(pl.multiple_of(chip * 384, 128), 384)
+            tokens[:, lanes] = came[step, 0] if yr else msgs[step][0]
+            for part in range(2):
+                mine = came[step, 1 + part] if yr else msgs[step][2 + part]
+                other = core_b[step, part] if yr else core_a[step, part]
+                for block, at in ((mine, core), (other, 1 - core)):
+                    block = block.astype(F32)
+                    for sub in range(2):
+                        small[4 * at + 2 * part + sub, :, lanes] = block[8 * sub : 8 * sub + 8]
+
+
+def call(kernel, out_shape, inputs, specs, scratch=()):
+    return pl.pallas_call(
+        kernel,
+        out_shape=out_shape,
+        in_specs=specs,
+        out_specs=jax.tree.map(lambda _: VSPEC, out_shape),
+        scratch_shapes=list(scratch),
+        compiler_params=PARAMS,
+    )(*inputs)
+
+
+def shape(dims, dtype):
+    return jax.ShapeDtypeStruct(dims, dtype)
+
+
+def sliced_device(
+    features,
+    cotangent,
+    depth_kernel,
+    depth_bias,
+    norm_gain,
+    norm_shift,
+    up_weight,
+    up_bias,
+    down_weight,
+    layer_scale,
+):
+    channels, hidden_dev = up_weight.shape
+    tiles = channels // LANES
+    index = lax.axis_index("rows")
+    idx = jnp.stack([index // 4, (index // 2) % 2, index % 2]).astype(jnp.int32)
+    bias_row, gain_row = depth_bias.reshape(1, channels), norm_gain.reshape(1, channels)
+    shift_row, scale_row = norm_shift.reshape(1, channels), layer_scale.reshape(1, channels)
+
+    feat_shard = features.transpose(1, 0, 2).reshape(16, channels)
+    cot_shard = cotangent.transpose(1, 0, 2).reshape(16, channels)
+    feat_pieces = gather_tokens(feat_shard)
+    cot_pieces = gather_tokens(cot_shard)
+
+    normed, f_slice, u_slice, inv_slice = call(
+        conv_norm_kernel,
+        (
+            shape((272, channels), BF16),
+            shape((3, 4, 48, LANES), F32),
+            shape((3, 128, LANES), F32),
+            shape((128, LANES), F32),
+        ),
+        (idx, *feat_pieces, depth_kernel, bias_row, gain_row, shift_row),
+        [SSPEC] + [VSPEC] * 14,
+        (
+            VMEM((tiles, 8, 48, LANES), F32),
+            VMEM((tiles, 256, LANES), F32),
+            VMEM((256, LANES), F32),
+            VMEM((256, LANES), F32),
+            VMEM((256, LANES), F32),
+        ),
+    )
+    cot_all, cot_slice = call(
+        cot_kernel,
+        (shape((256, channels), BF16), shape((3, 128, LANES), F32)),
+        (idx, *cot_pieces, scale_row),
+        [SSPEC] + [VSPEC] * 11,
+        (VMEM((tiles, 256, LANES), F32),),
+    )
+
+    tile = 256
+    steps = hidden_dev // tile
+    hidden, slope, centred, gain_dot = pl.pallas_call(
+        up_kernel,
+        grid=(steps,),
+        out_shape=(
+            shape((256, hidden_dev), BF16),
+            shape((256, hidden_dev), F32),
+            shape((256, hidden_dev), F32),
+            shape((8, hidden_dev), F32),
+        ),
+        in_specs=[
+            pl.BlockSpec((272, channels), lambda n: (0, 0)),
+            pl.BlockSpec((channels, tile), lambda n: (0, n)),
+            pl.BlockSpec((1, tile), lambda n: (0, n)),
+        ],
+        out_specs=(
+            pl.BlockSpec((256, tile), lambda n: (0, n)),
+            pl.BlockSpec((256, tile), lambda n: (0, n)),
+            pl.BlockSpec((256, tile), lambda n: (0, n)),
+            pl.BlockSpec((8, tile), lambda n: (0, n)),
+        ),
+        compiler_params=GRID_PARAMS,
+    )(normed, up_weight, up_bias.reshape(1, hidden_dev))
+
+    act_grad, bias_grad, sums = pl.pallas_call(
+        act_kernel,
+        grid=(steps,),
+        out_shape=(
+            shape((256, hidden_dev), BF16),
+            shape((8, hidden_dev), F32),
+            shape((2, 16, LANES), F32),
+        ),
+        in_specs=[
+            pl.BlockSpec((256, channels), lambda n: (0, 0)),
+            pl.BlockSpec((tile, channels), lambda n: (n, 0)),
+            pl.BlockSpec((256, tile), lambda n: (0, n)),
+            pl.BlockSpec((256, tile), lambda n: (0, n)),
+            pl.BlockSpec((8, tile), lambda n: (0, n)),
+        ],
+        out_specs=(
+            pl.BlockSpec((256, tile), lambda n: (0, n)),
+            pl.BlockSpec((8, tile), lambda n: (0, n)),
+            pl.BlockSpec((2, 16, LANES), lambda n: (0, 0, 0)),
+        ),
+        scratch_shapes=[VMEM((256, LANES), F32), VMEM((256, LANES), F32)],
+        compiler_params=GRID_PARAMS,
+    )(cot_all, down_weight, slope, centred, gain_dot)
+
+    def norm_grad_for(step):
+        def weight_block(yr, idx):
+            return (2 * ((idx[0] + step) % 4) + (idx[1] + yr) % 2, 0)
+
+        return pl.pallas_call(
+            norm_grad_kernel,
+            grid_spec=pltpu.PrefetchScalarGridSpec(
+                num_scalar_prefetch=1,
+                grid=(2,),
+                in_specs=[
+                    pl.BlockSpec((256, hidden_dev), lambda yr, idx: (0, 0)),
+                    pl.BlockSpec((384, hidden_dev), weight_block),
+                    pl.BlockSpec((2, 16, LANES), lambda yr, idx: (0, 0, 0)),
+                ],
+                out_specs=(
+                    pl.BlockSpec((1, 144, 384), lambda yr, idx: (yr, 0, 0)),
+                    pl.BlockSpec((1, 144, 384), lambda yr, idx: (yr, 0, 0)),
+                ),
+            ),
+            out_shape=(shape((2, 144, 384), F32), shape((2, 144, 384), BF16)),
+            compiler_params=GRID_PARAMS,
+        )(idx, act_grad, up_weight, sums)
+
+    arrived = {}
+    for step in (1, 2, 3, 0):
+        keep, away = norm_grad_for(step)
+        came = send(away, C_PAIRS)
+        across = send((keep[1] + came[1].astype(F32)).astype(BF16), Y_PAIRS)
+        total = keep[0] + came[0].astype(F32) + across.astype(F32)
+        if step:
+            back = [(dst, src) for src, dst in z_pairs(step)]
+            total = send(total.astype(BF16), back)
+        arrived[step] = total
+
+    ig_keep, core_msg, small_keep = call(
+        conv_back_kernel,
+        (shape((4, 16, 384), BF16), shape((6, 16, 384), BF16), shape((2, 16, 384), F32)),
+        (
+            idx, arrived[0], arrived[1], arrived[2], arrived[3], f_slice, u_slice, inv_slice,
+            gain_row, depth_kernel, cot_slice,
+        ),
+        [SSPEC] + [VSPEC] * 10,
+        (
+            VMEM((3, 4, 48, LANES), F32),
+            VMEM((3, 4, 32, LANES), F32),
+            VMEM((64, 384), F32),
+        ),
+    )
+    core_msg = send(core_msg, C_PAIRS)
+    msgs = call(
+        route_kernel,
+        tuple(shape((4, 16, 384), BF16) for _ in range(4)),
+        (idx, ig_keep, core_msg, small_keep),
+        [SSPEC] + [VSPEC] * 3,
+    )
+    msgs = [msgs[0]] + [
+        send(msgs[step], [(dst, src) for src, dst in z_pairs(step)]) for step in (1, 2, 3)
+    ]
+    came = send(jnp.stack([msg[1:4] for msg in msgs]), Y_PAIRS)
+    core_a = send(jnp.stack([msg[2:4] for msg in msgs]), C_PAIRS)
+    core_b = send(came[:, 1:3], C_PAIRS)
+    tokens, small = call(
+        place_kernel,
+        (shape((16, channels), BF16), shape((8, 8, channels), F32)),
+        (idx, *msgs, came, core_a, core_b),
+        [SSPEC] + [VSPEC] * 7,
+    )
+    down_grad = contract(hidden, cot_all, 0, 0)
+    up_grad = contract(normed[0:256], act_grad, 0, 0)
+    return (
+        tokens.reshape(4, 4, channels).transpose(1, 0, 2),
+        up_grad,
+        bias_grad[0],
+        down_grad,
+        small[0:7, 0:7],
+        small[7, 2],
+        small[7, 0],
+        small[7, 1],
+    )
+
+
+def on_device(features, *rest):
+    rows_dev, cols, channels = features.shape
+    fits = lax.axis_size("rows") == 16 and rows_dev == 4 and cols == 4 and channels == 3072
+    return (sliced_device if fits else generic_device)(features, *rest)
+
+
 def solution(mesh):
     in_specs = (
         P(("groups", "rows"), None, None),

time: 162 us -> 115 us (0.71)
  starting transfers between devices: 66.4 us -> 38 us
  Pallas kernels: 0 us -> 27.5 us
  other arithmetic: 29 us -> 3.6 us
  waiting for transfers between devices: 33.4 us -> 26.9 us
  matrix products: 16.8 us -> 10.4 us
  local copies, waits for them, and re-layouts: 13.2 us -> 7.31 us
  between operations: 2.77 us -> 1.1 us
    ppermute x50 -> x36, starting transfers between devices: 66.4 us -> 38 us  [send(): return lax.ppermute(value, 'rows', pairs)]
    pallas_call x0 -> x11, Pallas kernels: none -> 27.5 us  [the longest x5 16 us: call(): pl.pallas_call(kernel, out_shape=out_shape, in_specs=specs, out_specs=jax...]
    concatenate x4 -> x0, other arithmetic: 11.5 us -> none  [the longest x1 6.68 us: on_device(): jnp.concatenate([contract(n, act_grad, 0, 0) for n in normed_all], axis=0)]
    reduce_sum x7 -> x0, other arithmetic: 9.62 us -> none  [the longest x1 5.13 us: on_device(): row_mean = jnp.mean(conv_out, axis=-1, keepdims=True)]
    ppermute x50 -> x36, waiting for transfers between devices: 33.4 us -> 26.9 us  [send(): return lax.ppermute(value, 'rows', pairs)]
    dot_general x10 -> x2, matrix products: 16.8 us -> 10.4 us  [contract(): lax.dot_general(left, right, (((left_dim,), (right_dim,)), ((), ())), pre...]
    convert_element_type x13 -> x7, other arithmetic: 6.32 us -> 0.25 us  [the longest x3 0.14 us: sliced_device(): total = send(total.astype(BF16), back)]
    slice x8 -> x4, local copies, waits for them, and re-layouts: 8.16 us -> 2.14 us  [the longest x1 0.89 us: sliced_device(): small[0:7, 0:7]]
  transfers between devices with their start and end apart: 50 -> 36, of which waited for: 13 -> 15; matrix products, arithmetic and copies ran while one was open for 24% -> 14% of each run, Pallas kernels for 0% -> 15%
where the time goes in v2:
time: 115 us
  starting transfers between devices  38 us (33%)
  Pallas kernels  27.5 us (24%)
  waiting for transfers between devices  26.9 us (23%)
  matrix products  10.4 us (9%)
  local copies, waits for them, and re-layouts  7.31 us (6%)
  other arithmetic  3.6 us (3%)
    ppermute x36, starting transfers between devices, send(): return lax.ppermute(value, 'rows', pairs)  38 us
    ppermute x36, waiting for transfers between devices, send(): return lax.ppermute(value, 'rows', pairs)  26.9 us
    pallas_call x5, Pallas kernels, call(): pl.pallas_call(kernel, out_shape=out_shape, in_specs=specs, out_specs=jax...  16 us
    dot_general x2, matrix products, contract(): lax.dot_general(left, right, (((left_dim,), (right_dim,)), ((), ())), pre...  10.4 us
    pallas_call x4, Pallas kernels, norm_grad_for(): pl.pallas_call(norm_grad_kernel, grid_spec=pltpu.PrefetchScalarGridSpec(n...  6.12 us
    pallas_call x1, Pallas kernels, sliced_device(): pl.pallas_call(act_kernel, grid=(steps,), out_shape=(shape((256, hidden_d...  2.79 us
    pallas_call x1, Pallas kernels, sliced_device(): pl.pallas_call(up_kernel, grid=(steps,), out_shape=(shape((256, hidden_de...  2.52 us
    unnamed x26, local copies, waits for them, and re-layouts  2.4 us
  transfers between devices with their start and end apart: 36, of which 15 were waited for; matrix products, arithmetic and copies ran while one was open for 14% of the time, Pallas kernels for 15%

profile of v2, /device:TPU:0, one launch (start us, length us, event | category | flops | bytes accessed | tf_op | source)
XLA Modules:
  0.0 114.7 jit_solution(14583318143696809658)
XLA Ops:
  1.6 3.1 %collective-permute-start.11 = (bf16[16,3072]{1,0:T(8,128)(2,1)S(1)}, bf16[16,3072]{1,0:T(8,128)(2,1)S(1)}, u32[]{:S(2)}, u32[]{:S(2)}) collective-permute-start(bf16[16,3072]{1,0:T(8,128)(2,1)S(1)} %reshape.62.refs_0_), channel_id=1, source_target_pairs={{12,0},{13,1},{14,2},{15,3},{0,4},{1,5},{2,6},{3,7},{4,8},{5,9},{6... | collective-permute-start | bytes 294920 | tf_op jit(solution)/shard_map/ppermute | solution.py:39
  4.7 2.6 %collective-permute-start.10 = (bf16[16,3072]{1,0:T(8,128)(2,1)S(1)}, bf16[16,3072]{1,0:T(8,128)(2,1)S(1)}, u32[]{:S(2)}, u32[]{:S(2)}) collective-permute-start(bf16[16,3072]{1,0:T(8,128)(2,1)S(1)} %reshape.62.refs_0_), channel_id=1, source_target_pairs={{8,0},{9,1},{10,2},{11,3},{12,4},{13,5},{14,6},{15,7},{0,8},{1,9},... | collective-permute-start | bytes 294920 | tf_op jit(solution)/shard_map/ppermute | solution.py:39
  9.6 1.6 %collective-permute-start.3 = (bf16[16,3072]{1,0:T(8,128)(2,1)S(1)}, bf16[16,3072]{1,0:T(8,128)(2,1)S(1)}, u32[]{:S(2)}, u32[]{:S(2)}) collective-permute-start(bf16[16,3072]{1,0:T(8,128)(2,1)S(1)} %reshape.60.refs_0_), channel_id=1, source_target_pairs={{2,0},{3,1},{0,2},{1,3},{6,4},{7,5},{4,6},{5,7},{10,8},{11,9},{8,1... | collective-permute-start | bytes 294920 | tf_op jit(solution)/shard_map/ppermute | solution.py:39
  12.0 3.6 %collective-permute-start.1 = (bf16[16,3072]{1,0:T(8,128)(2,1)S(1)}, bf16[16,3072]{1,0:T(8,128)(2,1)S(1)}, u32[]{:S(2)}, u32[]{:S(2)}) collective-permute-start(bf16[16,3072]{1,0:T(8,128)(2,1)S(1)} %reshape.60.refs_0_), channel_id=1, source_target_pairs={{8,0},{9,1},{10,2},{11,3},{12,4},{13,5},{14,6},{15,7},{0,8},{1,9},... | collective-permute-start | bytes 294920 | tf_op jit(solution)/shard_map/ppermute | solution.py:39
  15.6 4.1 %collective-permute-start = (bf16[16,3072]{1,0:T(8,128)(2,1)S(1)}, bf16[16,3072]{1,0:T(8,128)(2,1)S(1)}, u32[]{:S(2)}, u32[]{:S(2)}) collective-permute-start(bf16[16,3072]{1,0:T(8,128)(2,1)S(1)} %reshape.60.refs_0_), channel_id=1, source_target_pairs={{4,0},{5,1},{6,2},{7,3},{8,4},{9,5},{10,6},{11,7},{12,8},{13,9},{1... | collective-permute-start | bytes 294920 | tf_op jit(solution)/shard_map/ppermute | solution.py:39
  25.6 2.0 %collective-permute-done.15.refs_7_ = bf16[16,3072]{1,0:T(8,128)(2,1)S(1)} collective-permute-done((bf16[16,3072]{1,0:T(8,128)(2,1)S(1)}, bf16[16,3072]{1,0:T(8,128)(2,1)S(1)}, u32[]{:S(2)}, u32[]{:S(2)}) %collective-permute-start.15) | collective-permute-done | bytes 98336 | tf_op jit(solution)/shard_map/ppermute | solution.py:39
  33.6 1.8 %collective-permute-done.5.refs_6_ = bf16[16,3072]{1,0:T(8,128)(2,1)S(1)} collective-permute-done((bf16[16,3072]{1,0:T(8,128)(2,1)S(1)}, bf16[16,3072]{1,0:T(8,128)(2,1)S(1)}, u32[]{:S(2)}, u32[]{:S(2)}) %collective-permute-start.5) | collective-permute-done | bytes 98336 | tf_op jit(solution)/shard_map/ppermute | solution.py:39
  37.4 9.9 %shard_map.162 = (bf16[272,3072]{1,0:T(8,128)(2,1)S(1)}, f32[3,4,48,128]{3,2,1,0:T(8,128)S(1)}, f32[3,128,128]{2,1,0:T(8,128)S(1)}, f32[128,128]{1,0:T(8,128)S(1)}) custom-call(s32[3]{0:T(128)S(1)} %pad_add_fusion.idx, bf16[16,3072]{1,0:T(8,128)(2,1)S(1)} %reshape.62.refs_0_, bf16[16,3072]{1,0:T(8,128)(2,1)S(1)} %collective-permute-done.9.refs_1_, ...), custom_call_target="tpu_custom_call" | custom-call | tf_op jit(solution)/shard_map/pallas_call | solution.py:532
  47.4 2.3 %copy-done = bf16[3072,768]{1,0:T(8,128)(2,1)S(1)} copy-done((bf16[3072,768]{1,0:T(8,128)(2,1)S(1)}, bf16[3072,768]{1,0:T(8,128)(2,1)}, u32[]{:S(2)}) %copy-start) | copy-done | bytes 4718616
  49.7 2.5 %shard_map.163 = (bf16[256,768]{1,0:T(8,128)(2,1)S(1)}, f32[256,768]{1,0:T(8,128)S(1)}, f32[256,768]{1,0:T(8,128)S(1)}, f32[8,768]{1,0:T(8,128)S(1)}) custom-call(bf16[272,3072]{1,0:T(8,128)(2,1)S(1)} %get-tuple-element.39.normed, bf16[3072,768]{1,0:T(8,128)(2,1)S(1)} %copy-done, f32[1,768]{1,0:T(1,128)S(1)} %reshape.66.up_bias), custom_call_target="tpu_custom_call" | custom-call | tf_op jit(solution)/shard_map/pallas_call | solution.py:598
  52.3 2.5 %shard_map.161 = (bf16[256,3072]{1,0:T(8,128)(2,1)S(1)}, f32[3,128,128]{2,1,0:T(8,128)S(1)}) custom-call(s32[3]{0:T(128)S(1)} %pad_add_fusion.idx, bf16[16,3072]{1,0:T(8,128)(2,1)S(1)} %copy-done.3, bf16[16,3072]{1,0:T(8,128)(2,1)S(1)} %collective-permute-done.refs_1_, bf16[16,3072]{1,0:T(8,128)(2,1)S(1)} %collective-permute-done.1.refs_2_, ...), custom_call_target="tpu_custom_call" | custom-call | tf_op jit(solution)/shard_map/pallas_call | solution.py:532
  54.9 2.8 %shard_map.164 = (bf16[256,768]{1,0:T(8,128)(2,1)S(1)}, f32[8,768]{1,0:T(8,128)S(1)}, f32[2,16,128]{2,1,0:T(8,128)S(1)}) custom-call(bf16[256,3072]{1,0:T(8,128)(2,1)S(1)} %get-tuple-element.38.cot_all, bf16[768,3072]{1,0:T(8,128)(2,1)S(1)} %bitcast.73, f32[256,768]{1,0:T(8,128)S(1)} %get-tuple-element.40.slope, f32[256,768]{1,0:T(8,128)S(1)} %get-tuple-element.41.centred, ...), custom_call_target="tpu_custom_call" | custom-call | tf_op jit(solution)/shard_map/pallas_call | solution.py:621
  57.7 1.5 %shard_map.168 = (f32[2,144,384]{2,1,0:T(8,128)S(1)}, bf16[2,144,384]{2,1,0:T(8,128)(2,1)S(1)}) custom-call(s32[3]{0:T(128)S(1)} %pad_add_fusion.idx, bf16[256,768]{1,0:T(8,128)(2,1)S(1)} %get-tuple-element.43.act_grad, bf16[3072,768]{1,0:T(8,128)(2,1)S(1)} %bitcast.71, f32[2,16,128]{2,1,0:T(8,128)S(1)} %get-tuple-element.44.sums), custom_call_target="tpu_custom_call" | custom-call | tf_op jit(solution)/shard_map/pallas_call | solution.py:649
  59.8 5.2 %fusion = f32[3072,768]{1,0:T(8,128)} fusion(bf16[256,768]{1,0:T(8,128)(2,1)S(1)} %get-tuple-element.43.act_grad, bf16[272,3072]{1,0:T(8,128)(2,1)S(1)} %get-tuple-element.39.normed), kind=kOutput, calls=%fused_computation | convolution fusion | flops 1207959552 | bytes 11403264 | tf_op jit(solution)/shard_map/dot_general | solution.py:64
  66.5 1.5 %shard_map.166 = (f32[2,144,384]{2,1,0:T(8,128)S(1)}, bf16[2,144,384]{2,1,0:T(8,128)(2,1)S(1)}) custom-call(s32[3]{0:T(128)S(1)} %pad_add_fusion.idx, bf16[256,768]{1,0:T(8,128)(2,1)S(1)} %get-tuple-element.43.act_grad, bf16[3072,768]{1,0:T(8,128)(2,1)S(1)} %bitcast.71, f32[2,16,128]{2,1,0:T(8,128)S(1)} %get-tuple-element.44.sums), custom_call_target="tpu_custom_call" | custom-call | tf_op jit(solution)/shard_map/pallas_call | solution.py:649
  68.1 1.5 %shard_map.165 = (f32[2,144,384]{2,1,0:T(8,128)S(1)}, bf16[2,144,384]{2,1,0:T(8,128)(2,1)S(1)}) custom-call(s32[3]{0:T(128)S(1)} %pad_add_fusion.idx, bf16[256,768]{1,0:T(8,128)(2,1)S(1)} %get-tuple-element.43.act_grad, bf16[3072,768]{1,0:T(8,128)(2,1)S(1)} %bitcast.71, f32[2,16,128]{2,1,0:T(8,128)S(1)} %get-tuple-element.44.sums), custom_call_target="tpu_custom_call" | custom-call | tf_op jit(solution)/shard_map/pallas_call | solution.py:649
  81.0 1.8 %collective-permute-start.22 = (bf16[144,384]{1,0:T(8,128)(2,1)S(1)}, bf16[144,384]{1,0:T(8,128)(2,1)S(1)}, u32[]{:S(2)}, u32[]{:S(2)}) collective-permute-start(bf16[144,384]{1,0:T(8,128)(2,1)S(1)} %fusion.4), channel_id=1, source_target_pairs={{0,4},{1,5},{2,6},{3,7},{4,8},{5,9},{6,10},{7,11},{8,12},{9,13},{1... | collective-permute-start | bytes 331784 | tf_op jit(solution)/shard_map/ppermute | solution.py:39
  82.9 6.3 %collective-permute-done.25.near_2 = bf16[144,384]{1,0:T(8,128)(2,1)S(1)} collective-permute-done((bf16[144,384]{1,0:T(8,128)(2,1)S(1)}, bf16[144,384]{1,0:T(8,128)(2,1)S(1)}, u32[]{:S(2)}, u32[]{:S(2)}) %collective-permute-start.25) | collective-permute-done | bytes 110624 | tf_op jit(solution)/shard_map/ppermute | solution.py:39
  89.2 2.3 %shard_map.169 = (bf16[4,16,384]{2,1,0:T(8,128)(2,1)S(1)}, bf16[6,16,384]{2,1,0:T(8,128)(2,1)S(1)}, f32[2,16,384]{2,1,0:T(8,128)S(1)}) custom-call(s32[3]{0:T(128)S(1)} %pad_add_fusion.idx, f32[144,384]{1,0:T(8,128)S(1)} %bitcast_add_fusion.3.own, bf16[144,384]{1,0:T(8,128)(2,1)S(1)} %collective-permute-done.22.near_1, ...), custom_call_target="tpu_custom_call" | custom-call | tf_op jit(solution)/shard_map/pallas_call | solution.py:532
  91.6 5.2 %fusion.10 = f32[768,3072]{1,0:T(8,128)} fusion(bf16[256,768]{1,0:T(8,128)(2,1)S(1)} %get-tuple-element.66, bf16[256,3072]{1,0:T(8,128)(2,1)S(1)} %get-tuple-element.38.cot_all), kind=kOutput, calls=%fused_computation.35 | convolution fusion | flops 1207959552 | bytes 11403264 | tf_op jit(solution)/shard_map/dot_general | solution.py:64
  98.6 2.7 %collective-permute-start.32 = (bf16[4,16,384]{2,1,0:T(8,128)(2,1)S(1)}, bf16[4,16,384]{2,1,0:T(8,128)(2,1)S(1)}, u32[]{:S(2)}, u32[]{:S(2)}) collective-permute-start(bf16[4,16,384]{2,1,0:T(8,128)(2,1)S(1)} %get-tuple-element.63), channel_id=1, source_target_pairs={{0,12},{1,13},{2,14},{3,15},{4,0},{5,1},{6,2},{7,3},{8,4},{9,5},{1... | collective-permute-start | bytes 147464 | tf_op jit(solution)/shard_map/ppermute | solution.py:39
  101.4 2.5 %collective-permute-done.30.refs_1_ = bf16[4,16,384]{2,1,0:T(8,128)(2,1)S(1)} collective-permute-done((bf16[4,16,384]{2,1,0:T(8,128)(2,1)S(1)}, bf16[4,16,384]{2,1,0:T(8,128)(2,1)S(1)}, u32[]{:S(2)}, u32[]{:S(2)}) %collective-permute-start.30) | collective-permute-done | bytes 49184 | tf_op jit(solution)/shard_map/ppermute | solution.py:39
  104.7 1.6 %collective-permute-start.33 = (bf16[4,3,16,384]{3,2,1,0:T(8,128)(2,1)S(1)}, bf16[4,3,16,384]{3,2,1,0:T(8,128)(2,1)S(1)}, u32[]{:S(2)}, u32[]{:S(2)}) collective-permute-start(bf16[4,3,16,384]{3,2,1,0:T(8,128)(2,1)S(1)} %pad_maximum_fusion.4), channel_id=1, source_target_pairs={{2,0},{3,1},{0,2},{1,3},{6,4},{7,5},{4,6},{5,7},{10,8},{11,9},{8,1... | collective-permute-start | bytes 442376 | tf_op jit(solution)/shard_map/ppermute | solution.py:39
  106.4 4.1 %collective-permute-done.33.refs_4_ = bf16[4,3,16,384]{3,2,1,0:T(8,128)(2,1)S(1)} collective-permute-done((bf16[4,3,16,384]{3,2,1,0:T(8,128)(2,1)S(1)}, bf16[4,3,16,384]{3,2,1,0:T(8,128)(2,1)S(1)}, u32[]{:S(2)}, u32[]{:S(2)}) %collective-permute-start.33) | collective-permute-done | bytes 147488 | tf_op jit(solution)/shard_map/ppermute | solution.py:39
  (125 shorter events, 38.6 us)
Async XLA Ops:
  1.6 10.4 %collective-permute-start.11 = (bf16[16,3072]{1,0:T(8,128)(2,1)S(1)}, bf16[16,3072]{1,0:T(8,128)(2,1)S(1)}, u32[]{:S(2)}, u32[]{:S(2)}) collective-permute-start(bf16[16,3072]{1,0:T(8,128)(2,1)S(1)} %reshape.62.refs_0_), channel_id=1, source_target_pairs={{12,0},{13,1},{14,2},{15,3},{0,4},{1,5},{2,6},{3,7},{4,8},{5,9},{6... | collective-permute-start | bytes 294920 | tf_op jit(solution)/shard_map/ppermute | solution.py:39
  4.7 10.9 %collective-permute-start.10 = (bf16[16,3072]{1,0:T(8,128)(2,1)S(1)}, bf16[16,3072]{1,0:T(8,128)(2,1)S(1)}, u32[]{:S(2)}, u32[]{:S(2)}) collective-permute-start(bf16[16,3072]{1,0:T(8,128)(2,1)S(1)} %reshape.62.refs_0_), channel_id=1, source_target_pairs={{8,0},{9,1},{10,2},{11,3},{12,4},{13,5},{14,6},{15,7},{0,8},{1,9},... | collective-permute-start | bytes 294920 | tf_op jit(solution)/shard_map/ppermute | solution.py:39
  7.3 12.4 %collective-permute-start.9 = (bf16[16,3072]{1,0:T(8,128)(2,1)S(1)}, bf16[16,3072]{1,0:T(8,128)(2,1)S(1)}, u32[]{:S(2)}, u32[]{:S(2)}) collective-permute-start(bf16[16,3072]{1,0:T(8,128)(2,1)S(1)} %reshape.62.refs_0_), channel_id=1, source_target_pairs={{4,0},{5,1},{6,2},{7,3},{8,4},{9,5},{10,6},{11,7},{12,8},{13,9},{1... | collective-permute-start | bytes 294920 | tf_op jit(solution)/shard_map/ppermute | solution.py:39
  9.6 23.2 %collective-permute-start.3 = (bf16[16,3072]{1,0:T(8,128)(2,1)S(1)}, bf16[16,3072]{1,0:T(8,128)(2,1)S(1)}, u32[]{:S(2)}, u32[]{:S(2)}) collective-permute-start(bf16[16,3072]{1,0:T(8,128)(2,1)S(1)} %reshape.60.refs_0_), channel_id=1, source_target_pairs={{2,0},{3,1},{0,2},{1,3},{6,4},{7,5},{4,6},{5,7},{10,8},{11,9},{8,1... | collective-permute-start | bytes 294920 | tf_op jit(solution)/shard_map/ppermute | solution.py:39
  11.2 10.8 %collective-permute-start.2 = (bf16[16,3072]{1,0:T(8,128)(2,1)S(1)}, bf16[16,3072]{1,0:T(8,128)(2,1)S(1)}, u32[]{:S(2)}, u32[]{:S(2)}) collective-permute-start(bf16[16,3072]{1,0:T(8,128)(2,1)S(1)} %reshape.60.refs_0_), channel_id=1, source_target_pairs={{12,0},{13,1},{14,2},{15,3},{0,4},{1,5},{2,6},{3,7},{4,8},{5,9},{6... | collective-permute-start | bytes 294920 | tf_op jit(solution)/shard_map/ppermute | solution.py:39
  12.0 10.5 %collective-permute-start.1 = (bf16[16,3072]{1,0:T(8,128)(2,1)S(1)}, bf16[16,3072]{1,0:T(8,128)(2,1)S(1)}, u32[]{:S(2)}, u32[]{:S(2)}) collective-permute-start(bf16[16,3072]{1,0:T(8,128)(2,1)S(1)} %reshape.60.refs_0_), channel_id=1, source_target_pairs={{8,0},{9,1},{10,2},{11,3},{12,4},{13,5},{14,6},{15,7},{0,8},{1,9},... | collective-permute-start | bytes 294920 | tf_op jit(solution)/shard_map/ppermute | solution.py:39
  15.6 8.4 %collective-permute-start = (bf16[16,3072]{1,0:T(8,128)(2,1)S(1)}, bf16[16,3072]{1,0:T(8,128)(2,1)S(1)}, u32[]{:S(2)}, u32[]{:S(2)}) collective-permute-start(bf16[16,3072]{1,0:T(8,128)(2,1)S(1)} %reshape.60.refs_0_), channel_id=1, source_target_pairs={{4,0},{5,1},{6,2},{7,3},{8,4},{9,5},{10,6},{11,7},{12,8},{13,9},{1... | collective-permute-start | bytes 294920 | tf_op jit(solution)/shard_map/ppermute | solution.py:39
  22.5 6.9 %collective-permute-start.14 = (bf16[16,3072]{1,0:T(8,128)(2,1)S(1)}, bf16[16,3072]{1,0:T(8,128)(2,1)S(1)}, u32[]{:S(2)}, u32[]{:S(2)}) collective-permute-start(bf16[16,3072]{1,0:T(8,128)(2,1)S(1)} %collective-permute-done.10.refs_2_), channel_id=1, source_target_pairs={{2,0},{3,1},{0,2},{1,3},{6,4},{7,5},{4,6},{5,7},{10,8},{11,9},{8,1... | collective-permute-start | bytes 294920 | tf_op jit(solution)/shard_map/ppermute | solution.py:39
  24.0 7.5 %collective-permute-start.13 = (bf16[16,3072]{1,0:T(8,128)(2,1)S(1)}, bf16[16,3072]{1,0:T(8,128)(2,1)S(1)}, u32[]{:S(2)}, u32[]{:S(2)}) collective-permute-start(bf16[16,3072]{1,0:T(8,128)(2,1)S(1)} %collective-permute-done.9.refs_1_), channel_id=1, source_target_pairs={{2,0},{3,1},{0,2},{1,3},{6,4},{7,5},{4,6},{5,7},{10,8},{11,9},{8,1... | collective-permute-start | bytes 294920 | tf_op jit(solution)/shard_map/ppermute | solution.py:39
  25.6 26.7 %collective-permute-start.7 = (bf16[4,16,3072]{2,1,0:T(8,128)(2,1)}, bf16[4,16,3072]{2,1,0:T(8,128)(2,1)}, u32[]{:S(2)}, u32[]{:S(2)}) collective-permute-start(bf16[4,16,3072]{2,1,0:T(8,128)(2,1)} %pad_maximum_fusion), channel_id=1, source_target_pairs={{1,0},{0,1},{3,2},{2,3},{5,4},{4,5},{7,6},{6,7},{9,8},{8,9},{11,10... | collective-permute-start | bytes 1179656 | tf_op jit(solution)/shard_map/ppermute | solution.py:39
  27.6 6.0 %collective-permute-start.6 = (bf16[16,3072]{1,0:T(8,128)(2,1)S(1)}, bf16[16,3072]{1,0:T(8,128)(2,1)S(1)}, u32[]{:S(2)}, u32[]{:S(2)}) collective-permute-start(bf16[16,3072]{1,0:T(8,128)(2,1)S(1)} %collective-permute-done.2.refs_3_), channel_id=1, source_target_pairs={{2,0},{3,1},{0,2},{1,3},{6,4},{7,5},{4,6},{5,7},{10,8},{11,9},{8,1... | collective-permute-start | bytes 294920 | tf_op jit(solution)/shard_map/ppermute | solution.py:39
  29.4 6.0 %collective-permute-start.5 = (bf16[16,3072]{1,0:T(8,128)(2,1)S(1)}, bf16[16,3072]{1,0:T(8,128)(2,1)S(1)}, u32[]{:S(2)}, u32[]{:S(2)}) collective-permute-start(bf16[16,3072]{1,0:T(8,128)(2,1)S(1)} %collective-permute-done.1.refs_2_), channel_id=1, source_target_pairs={{2,0},{3,1},{0,2},{1,3},{6,4},{7,5},{4,6},{5,7},{10,8},{11,9},{8,1... | collective-permute-start | bytes 294920 | tf_op jit(solution)/shard_map/ppermute | solution.py:39
  37.2 15.0 %collective-permute-start.8 = (bf16[4,16,3072]{2,1,0:T(8,128)(2,1)}, bf16[4,16,3072]{2,1,0:T(8,128)(2,1)}, u32[]{:S(2)}, u32[]{:S(2)}) collective-permute-start(bf16[4,16,3072]{2,1,0:T(8,128)(2,1)} %pad_maximum_fusion.1), channel_id=1, source_target_pairs={{1,0},{0,1},{3,2},{2,3},{5,4},{4,5},{7,6},{6,7},{9,8},{8,9},{11,10... | collective-permute-start | bytes 1179656 | tf_op jit(solution)/shard_map/ppermute | solution.py:39
  59.2 11.0 %collective-permute-start.26 = (bf16[2,144,384]{2,1,0:T(8,128)(2,1)S(1)}, bf16[2,144,384]{2,1,0:T(8,128)(2,1)S(1)}, u32[]{:S(2)}, u32[]{:S(2)}) collective-permute-start(bf16[2,144,384]{2,1,0:T(8,128)(2,1)S(1)} %get-tuple-element.52), channel_id=1, source_target_pairs={{1,0},{0,1},{3,2},{2,3},{5,4},{4,5},{7,6},{6,7},{9,8},{8,9},{11,10... | collective-permute-start | bytes 663560 | tf_op jit(solution)/shard_map/ppermute | solution.py:39
  70.3 5.9 %collective-permute-start.27 = (bf16[144,384]{1,0:T(8,128)(2,1)S(1)}, bf16[144,384]{1,0:T(8,128)(2,1)S(1)}, u32[]{:S(2)}, u32[]{:S(2)}) collective-permute-start(bf16[144,384]{1,0:T(8,128)(2,1)S(1)} %fusion.8), channel_id=1, source_target_pairs={{2,0},{3,1},{0,2},{1,3},{6,4},{7,5},{4,6},{5,7},{10,8},{11,9},{8,1... | collective-permute-start | bytes 331784 | tf_op jit(solution)/shard_map/ppermute | solution.py:39
  71.6 7.0 %collective-permute-start.24 = (bf16[144,384]{1,0:T(8,128)(2,1)S(1)}, bf16[144,384]{1,0:T(8,128)(2,1)S(1)}, u32[]{:S(2)}, u32[]{:S(2)}) collective-permute-start(bf16[144,384]{1,0:T(8,128)(2,1)S(1)} %fusion.7), channel_id=1, source_target_pairs={{2,0},{3,1},{0,2},{1,3},{6,4},{7,5},{4,6},{5,7},{10,8},{11,9},{8,1... | collective-permute-start | bytes 331784 | tf_op jit(solution)/shard_map/ppermute | solution.py:39
  72.5 8.4 %collective-permute-start.21 = (bf16[144,384]{1,0:T(8,128)(2,1)S(1)}, bf16[144,384]{1,0:T(8,128)(2,1)S(1)}, u32[]{:S(2)}, u32[]{:S(2)}) collective-permute-start(bf16[144,384]{1,0:T(8,128)(2,1)S(1)} %fusion.6), channel_id=1, source_target_pairs={{2,0},{3,1},{0,2},{1,3},{6,4},{7,5},{4,6},{5,7},{10,8},{11,9},{8,1... | collective-permute-start | bytes 331784 | tf_op jit(solution)/shard_map/ppermute | solution.py:39
  73.8 9.1 %collective-permute-start.19 = (bf16[144,384]{1,0:T(8,128)(2,1)S(1)}, bf16[144,384]{1,0:T(8,128)(2,1)S(1)}, u32[]{:S(2)}, u32[]{:S(2)}) collective-permute-start(bf16[144,384]{1,0:T(8,128)(2,1)S(1)} %fusion.5), channel_id=1, source_target_pairs={{2,0},{3,1},{0,2},{1,3},{6,4},{7,5},{4,6},{5,7},{10,8},{11,9},{8,1... | collective-permute-start | bytes 331784 | tf_op jit(solution)/shard_map/ppermute | solution.py:39
  76.3 6.7 %collective-permute-start.28 = (bf16[144,384]{1,0:T(8,128)(2,1)S(1)}, bf16[144,384]{1,0:T(8,128)(2,1)S(1)}, u32[]{:S(2)}, u32[]{:S(2)}) collective-permute-start(bf16[144,384]{1,0:T(8,128)(2,1)S(1)} %fusion.2), channel_id=1, source_target_pairs={{0,12},{1,13},{2,14},{3,15},{4,0},{5,1},{6,2},{7,3},{8,4},{9,5},{1... | collective-permute-start | bytes 331784 | tf_op jit(solution)/shard_map/ppermute | solution.py:39
  78.6 10.5 %collective-permute-start.25 = (bf16[144,384]{1,0:T(8,128)(2,1)S(1)}, bf16[144,384]{1,0:T(8,128)(2,1)S(1)}, u32[]{:S(2)}, u32[]{:S(2)}) collective-permute-start(bf16[144,384]{1,0:T(8,128)(2,1)S(1)} %fusion.3), channel_id=1, source_target_pairs={{0,8},{1,9},{2,10},{3,11},{4,12},{5,13},{6,14},{7,15},{8,0},{9,1},... | collective-permute-start | bytes 331784 | tf_op jit(solution)/shard_map/ppermute | solution.py:39
  81.0 8.2 %collective-permute-start.22 = (bf16[144,384]{1,0:T(8,128)(2,1)S(1)}, bf16[144,384]{1,0:T(8,128)(2,1)S(1)}, u32[]{:S(2)}, u32[]{:S(2)}) collective-permute-start(bf16[144,384]{1,0:T(8,128)(2,1)S(1)} %fusion.4), channel_id=1, source_target_pairs={{0,4},{1,5},{2,6},{3,7},{4,8},{5,9},{6,10},{7,11},{8,12},{9,13},{1... | collective-permute-start | bytes 331784 | tf_op jit(solution)/shard_map/ppermute | solution.py:39
  97.4 6.5 %collective-permute-start.30 = (bf16[4,16,384]{2,1,0:T(8,128)(2,1)S(1)}, bf16[4,16,384]{2,1,0:T(8,128)(2,1)S(1)}, u32[]{:S(2)}, u32[]{:S(2)}) collective-permute-start(bf16[4,16,384]{2,1,0:T(8,128)(2,1)S(1)} %get-tuple-element.61), channel_id=1, source_target_pairs={{0,4},{1,5},{2,6},{3,7},{4,8},{5,9},{6,10},{7,11},{8,12},{9,13},{1... | collective-permute-start | bytes 147464 | tf_op jit(solution)/shard_map/ppermute | solution.py:39
  97.5 7.2 %collective-permute-start.31 = (bf16[4,16,384]{2,1,0:T(8,128)(2,1)S(1)}, bf16[4,16,384]{2,1,0:T(8,128)(2,1)S(1)}, u32[]{:S(2)}, u32[]{:S(2)}) collective-permute-start(bf16[4,16,384]{2,1,0:T(8,128)(2,1)S(1)} %get-tuple-element.62), channel_id=1, source_target_pairs={{0,8},{1,9},{2,10},{3,11},{4,12},{5,13},{6,14},{7,15},{8,0},{9,1},... | collective-permute-start | bytes 147464 | tf_op jit(solution)/shard_map/ppermute | solution.py:39
  98.6 6.0 %collective-permute-start.32 = (bf16[4,16,384]{2,1,0:T(8,128)(2,1)S(1)}, bf16[4,16,384]{2,1,0:T(8,128)(2,1)S(1)}, u32[]{:S(2)}, u32[]{:S(2)}) collective-permute-start(bf16[4,16,384]{2,1,0:T(8,128)(2,1)S(1)} %get-tuple-element.63), channel_id=1, source_target_pairs={{0,12},{1,13},{2,14},{3,15},{4,0},{5,1},{6,2},{7,3},{8,4},{9,5},{1... | collective-permute-start | bytes 147464 | tf_op jit(solution)/shard_map/ppermute | solution.py:39
  (25 other events, 243.3 us)

commit v3 on v1

--- a/solution.py
+++ b/solution.py
@@ -1,6 +1,10 @@
+import functools
+
 import jax
 import jax.numpy as jnp
 from jax import lax
+from jax.experimental import pallas as pl
+from jax.experimental.pallas import tpu as pltpu
 from jax.sharding import PartitionSpec as P
 
 IMG_ROWS = 32
@@ -70,7 +74,7 @@
     return jnp.concatenate([send(tail, fwd), cells, send(head, bwd)], axis=0)
 
 
-def on_device(
+def generic_device(
     features,
     cotangent,
     depth_kernel,
@@ -222,6 +226,594 @@
     )
 
 
+LANES = 128
+VMEM = pltpu.VMEM
+VSPEC = pl.BlockSpec(memory_space=pltpu.VMEM)
+SSPEC = pl.BlockSpec(memory_space=pltpu.SMEM)
+EXACT = lax.Precision.HIGHEST
+MIB = 1024 * 1024
+
+
+def z_pairs(step):
+    return from_ahead(16, 4, 4, step)
+
+
+def flipped(pairs):
+    return [(dst, src) for src, dst in pairs]
+
+
+Y_PAIRS = from_ahead(16, 2, 2, 1)
+C_PAIRS = from_ahead(16, 1, 2, 1)
+
+
+def after(value, other):
+    return lax.optimization_barrier((value, other))[0]
+
+
+def gather_chips(shard):
+    with jax.named_scope("feat_z"):
+        planes = [shard] + [send(shard, z_pairs(step)) for step in (1, 2, 3)]
+    with jax.named_scope("feat_y"):
+        return planes, [send(plane, Y_PAIRS) for plane in planes]
+
+
+def lane_tile(tile):
+    return pl.ds(pl.multiple_of(tile * LANES, LANES), LANES)
+
+
+def sixteen(block):
+    return pl.ds(pl.multiple_of(block * 16, 16), 16)
+
+
+def place_and_convolve(idx, pieces, came, kern, bias, feats, conv, turn, total, first_tile):
+    z, y, core = idx[0], idx[1], idx[2]
+    tiles = feats.shape[0]
+    edge = jnp.zeros((tiles, 4, 8, LANES), F32)
+    feats[:, :, 0:8, :] = edge
+    feats[:, :, 40:48, :] = edge
+
+    def place(piece, row):
+        for tile in range(tiles):
+            lanes = slice((first_tile + tile) * LANES, (first_tile + tile + 1) * LANES)
+            for r in range(4):
+                turn[tile % 4, 4 * r : 4 * r + 4, :] = piece[r, :, lanes].astype(F32)
+            for col in range(4):
+                feats[tile, col, pl.ds(8 + row, 4), :] = turn[
+                    tile % 4, pl.ds(col, 4, stride=4), :
+                ]
+
+    for yr in range(2):
+        for step in range(4):
+            at = (z + step + 3) % 4
+
+            @pl.when(at // 2 == core)
+            def _():
+                place(pieces[4 * yr + step], 16 * (at % 2) + 8 * ((y + yr) % 2) + 4 * core)
+
+        for half in range(2):
+            place(came[yr].at[half], 16 * half + 8 * ((y + yr) % 2) + 4 * (1 - core))
+
+    def conv_tile(tile, carry):
+        lanes = lane_tile(first_tile + tile)
+        for part in range(2):
+            acc = [jnp.broadcast_to(bias[0:1, lanes], (16, LANES))] * 4
+            for i in range(7):
+                for src in range(4):
+                    rows = feats[tile, src, pl.ds(5 + 16 * part + i, 16), :]
+                    for col in range(4):
+                        j = src - col + 3
+                        acc[col] = acc[col] + kern[i, j : j + 1, lanes] * rows
+            for col in range(4):
+                at = pl.ds(64 * part + col, 16, stride=4)
+                conv[tile, at, :] = acc[col]
+        total[...] = total[...] + conv[tile]
+        return carry
+
+    lax.fori_loop(0, tiles, conv_tile, 0)
+
+
+def conv_kernel(idx, *refs):
+    kern, bias, feats, conv, total, turn = refs[10:]
+    total[...] = jnp.zeros_like(total)
+    place_and_convolve(
+        idx, refs[:8], refs[8:10], kern, bias, feats, conv, turn, total, 0
+    )
+
+
+def conv_norm_kernel(idx, *refs):
+    kern, bias, gain, shift, feats_low, conv_low, total_low = refs[10:17]
+    normed, f_slice, u_slice, inv_slice = refs[17:21]
+    feats, conv, turn, total, mean_ref, inv_ref = refs[21:]
+    tiles = feats.shape[0]
+    channels = 2 * tiles * LANES
+    total[...] = total_low[...]
+    place_and_convolve(
+        idx, refs[:8], refs[8:10], kern, bias, feats, conv, turn, total, tiles
+    )
+    mean = jnp.sum(total[...], axis=-1, keepdims=True) / channels
+    mean_ref[...] = jnp.broadcast_to(mean, mean_ref.shape)
+    total[...] = jnp.zeros_like(total)
+    halves = ((0, conv_low, feats_low), (tiles, conv, feats))
+
+    def square_tile(tile, carry):
+        low, high = conv_low[tile] - mean_ref[...], conv[tile] - mean_ref[...]
+        total[...] = total[...] + (low * low + high * high)
+        return carry
+
+    lax.fori_loop(0, tiles, square_tile, 0)
+    spread = jnp.sum(total[...], axis=-1, keepdims=True) / channels
+    inv_ref[...] = jnp.broadcast_to(lax.rsqrt(spread + 1e-06), inv_ref.shape)
+
+    def norm_tile(tile, carry):
+        for start, values, _ in halves:
+            lanes = lane_tile(start + tile)
+            unit = (values[tile] - mean_ref[...]) * inv_ref[...]
+            normed[:, lanes] = (unit * gain[0:1, lanes] + shift[0:1, lanes]).astype(BF16)
+        return carry
+
+    lax.fori_loop(0, tiles, norm_tile, 0)
+    chip = idx[0] * 2 + idx[1]
+    inv_slice[...] = inv_ref[...]
+    for start, values, padded in halves:
+
+        @pl.when((chip >= 4) == (start > 0))
+        def _():
+            for k in range(3):
+                tile = (chip % 4) * 3 + k
+                u_slice[k] = (values[tile] - mean_ref[...]) * inv_ref[...]
+                f_slice[k] = padded[tile]
+
+
+def cot_kernel(idx, *refs):
+    layer_scale, cot_all, cot_slice = refs[8:]
+    z, y, core = idx[0], idx[1], idx[2]
+    chip = z * 2 + y
+    own = lane_tile(chip * 3), lane_tile(chip * 3 + 1), lane_tile(chip * 3 + 2)
+    for yr in range(2):
+        for cr in range(2):
+            for step in range(4):
+                piece = refs[4 * cr + step].at[yr]
+                at = (z + step + 3) % 4
+                away = (at // 2 + core) % 2
+                block = 4 * (at % 2) + 2 * ((y + yr) % 2) + (core + cr) % 2
+                scaled = piece[...].astype(F32) * layer_scale[...]
+                cot_all[sixteen(8 * away + block), :] = scaled.astype(BF16)
+
+                @pl.when(away == 0)
+                def _():
+                    for k in range(3):
+                        cot_slice[k, sixteen(block), :] = piece[:, own[k]].astype(F32)
+
+
+def fold_kernel(gain, shift, weight, kern, shard, gain_dot, shift_dot, kern_out, shard_out):
+    kern_out[...] = kern[...]
+    shard_out[...] = shard[...]
+    place = lax.broadcasted_iota(jnp.int32, (16, gain.shape[1]), 0)
+    scale, offset = gain[...], shift[...]
+    scale_hi = scale.astype(BF16).astype(F32)
+    offset_hi = offset.astype(BF16).astype(F32)
+    both = jnp.where(place == 0, scale_hi, 0.0)
+    both = jnp.where(place == 1, scale - scale_hi, both)
+    both = jnp.where(place == 2, offset_hi, both)
+    both = jnp.where(place == 3, offset - offset_hi, both)
+    product = jnp.dot(both.astype(BF16), weight[...], preferred_element_type=F32)
+    gain_dot[...] = jnp.broadcast_to(product[0:1] + product[1:2], gain_dot.shape)
+    shift_dot[...] = jnp.broadcast_to(product[2:3] + product[3:4], shift_dot.shape)
+
+
+def hid_kernel(cot_all, weight, hid_grad):
+    hid_grad[...] = contract(cot_all[...], weight[...], 1, 1)
+
+
+def act_kernel(
+    half, normed, weight, up_bias, hid_grad, gain_dot, shift_dot,
+    hidden, act_grad, bias_grad, sums,
+):
+    tile = 256
+    first = jnp.zeros((128, LANES), F32)
+    second = jnp.zeros((128, LANES), F32)
+    for start in range(0, hidden.shape[1], tile):
+        at = slice(start, start + tile)
+        plain = jnp.dot(normed[...], weight[:, at], preferred_element_type=F32)
+        pre_act = plain + up_bias[0:1, at]
+        cdf = 0.5 * (1.0 + lax.erf(pre_act * 0.7071067811865476))
+        hidden[:, at] = (pre_act * cdf).astype(BF16)
+        slope = cdf + pre_act * jnp.exp(-0.5 * pre_act * pre_act) * 0.3989422804014327
+        act = (hid_grad[128 * half : 128 * half + 128, at] * slope).astype(BF16)
+        act_grad[:, at] = act
+        act = act.astype(F32)
+        bias_grad[0:1, at] = jnp.sum(act, axis=0, keepdims=True)
+        by_gain = act * gain_dot[0:1, at]
+        by_unit = act * (plain - shift_dot[0:1, at])
+        for lane in range(0, tile, LANES):
+            first = first + by_gain[:, lane : lane + LANES]
+            second = second + by_unit[:, lane : lane + LANES]
+    ones = jnp.ones((8, LANES), F32)
+    for row, part in ((0, first), (8, second)):
+        sums[row : row + 8, :] = lax.dot_general(
+            ones, part, (((1,), (1,)), ((), ())), precision=EXACT, preferred_element_type=F32
+        )
+
+
+def norm_grad_kernel(steps, idx, act_own, act_other, weight, sums_own, sums_other, keep, away):
+    both = jnp.concatenate([act_other[...], act_own[...]], axis=0)
+    for at, step in enumerate(steps):
+        for yr in range(2):
+            chip = 2 * ((idx[0] + step) % 4) + (idx[1] + yr) % 2
+            rows = weight[pl.ds(pl.multiple_of(chip * 384, 128), 384), :]
+            product = contract(both, rows, 1, 1)
+            for ref, part, sums in ((away, 0, sums_other), (keep, 128, sums_own)):
+                ref[at, yr, 0:128, :] = product[part : part + 128].astype(ref.dtype)
+                ref[at, yr, 128:144, 0:128] = sums[...].astype(ref.dtype)
+                ref[at, yr, 128:144, 128:384] = jnp.zeros((16, 256), ref.dtype)
+
+
+def grad_kernel(left_own, left_other, right_own, right_other, *rest):
+    left = jnp.concatenate([left_own[...], left_other[...]], axis=0).T
+    right = jnp.concatenate([right_own[...], right_other[...]], axis=0)
+    rest[-1][...] = contract(left, right, 1, 0)
+
+
+def conv_back_kernel(
+    idx, own, near_1, near_2, near_3, f_slice, u_slice, inv_slice, gain, kern, cot_slice,
+    ig_keep, core_msg, small_keep, cg, turn, back, small,
+):
+    chip, y, core = idx[0] * 2 + idx[1], idx[1], idx[2]
+    channels = gain.shape[1]
+
+    def summed(rows, lanes):
+        return (
+            own[rows, lanes]
+            + near_1[rows, lanes].astype(F32)
+            + near_2[rows, lanes].astype(F32)
+            + near_3[rows, lanes].astype(F32)
+        )
+
+    sums = summed(slice(128, 144), slice(0, 128))
+    place = lax.broadcasted_iota(jnp.int32, (16, LANES), 0)
+
+    def per_token(row):
+        pick = jnp.where(place == row, 1.0 / channels, 0.0).astype(F32)
+        return lax.dot_general(
+            sums, pick, (((0,), (0,)), ((), ())), precision=EXACT, preferred_element_type=F32
+        )
+
+    mean_1, mean_2 = per_token(0), per_token(8)
+    cg[:, :, 0:8, :] = jnp.zeros((3, 4, 8, LANES), F32)
+    cg[:, :, 40:48, :] = jnp.zeros((3, 4, 8, LANES), F32)
+    small[...] = jnp.zeros_like(small)
+    for k in range(3):
+        lanes = slice(k * LANES, (k + 1) * LANES)
+        wide = lane_tile(chip * 3 + k)
+        norm_grad = summed(slice(0, 128), lanes)
+        unit = u_slice[k]
+        scaled = norm_grad * gain[0:1, wide]
+        grad = inv_slice[...] * (scaled - mean_1 - unit * mean_2)
+        turn[k] = grad
+        for col in range(4):
+            cg[k, col, 8:40, :] = turn[k, pl.ds(col, 32, stride=4), :]
+        small[56:57, lanes] = jnp.sum(norm_grad * unit, axis=0, keepdims=True)
+        small[57:58, lanes] = jnp.sum(norm_grad, axis=0, keepdims=True)
+        small[58:59, lanes] = jnp.sum(grad, axis=0, keepdims=True)
+        for i in range(7):
+            acc = [None] * 7
+            for src in range(4):
+                rows = f_slice[k, src, 5 + i : 37 + i, :]
+                for col in range(4):
+                    j = src - col + 3
+                    term = cg[k, col, 8:40, :] * rows
+                    acc[j] = term if acc[j] is None else acc[j] + term
+            for j in range(7):
+                small[8 * i + j : 8 * i + j + 1, lanes] = jnp.sum(acc[j], axis=0, keepdims=True)
+        for part in range(2):
+            acc = [cot_slice[k, pl.ds(64 * part + col, 16, stride=4), :] for col in range(4)]
+            for i in range(7):
+                for src in range(4):
+                    start = 11 + 16 * part - i
+                    rows = cg[k, src, start : start + 16, :]
+                    for col in range(4):
+                        j = col - src + 3
+                        acc[col] = acc[col] + kern[i, j : j + 1, wide] * rows
+            for col in range(4):
+                back[k, pl.ds(64 * part + col, 16, stride=4), :] = acc[col]
+        for half in range(2):
+            for yr in range(2):
+                for cr in range(2):
+                    block = 4 * half + 2 * ((y + yr) % 2) + (core + cr) % 2
+                    ref = core_msg if cr else ig_keep
+                    ref[2 * half + yr, :, lanes] = back[k, sixteen(block), :].astype(BF16)
+    for part in range(2):
+        core_msg[4 + part] = small[sixteen(2 * (1 - core) + part), :].astype(BF16)
+        small_keep[part] = small[sixteen(2 * core + part), :]
+
+
+def route_kernel(idx, ig_keep, core_msg, small_keep, *msgs):
+    z, core = idx[0], idx[2]
+    total = [
+        (small_keep[part] + core_msg[4 + part].astype(F32)).astype(BF16) for part in range(2)
+    ]
+    for step in range(4):
+        at = (z + step + 3) % 4
+        image, half = at // 2, at % 2
+        for yr in range(2):
+            kept, came = ig_keep[2 * half + yr], core_msg[2 * half + yr]
+            msgs[step][yr] = jnp.where(image == core, kept, came)
+        for part in range(2):
+            msgs[step][2 + part] = total[part]
+
+
+def place_kernel(idx, *refs):
+    msgs, came, core_a, core_b = refs[:4], refs[4], refs[5], refs[6]
+    tokens, kernel_grad, gain_grad, shift_grad, bias_grad = refs[7:]
+    z, y, core = idx[0], idx[1], idx[2]
+    for step in range(4):
+        plane = (z + 4 - step) % 4
+        for yr in range(2):
+            chip = plane * 2 + (y + yr) % 2
+            lanes = pl.ds(pl.multiple_of(chip * 384, 128), 384)
+            block = (came[step, 0] if yr else msgs[step][0]).astype(F32)
+            for row in range(4):
+                tokens[row, :, lanes] = block[4 * row : 4 * row + 4].astype(BF16)
+            for part in range(2):
+                mine = (came[step, 1 + part] if yr else msgs[step][2 + part]).astype(F32)
+                other = (core_b[step, part] if yr else core_a[step, part]).astype(F32)
+                low = jnp.where(core == 0, mine, other)
+                high = jnp.where(core == 0, other, mine)
+                for sub in range(2):
+                    at = 2 * part + sub
+                    rows = slice(8 * sub, 8 * sub + 7)
+                    kernel_grad[at, :, lanes] = low[rows]
+                    if at < 3:
+                        kernel_grad[4 + at, :, lanes] = high[rows]
+                    else:
+                        gain_grad[0:1, lanes] = high[8:9]
+                        shift_grad[0:1, lanes] = high[9:10]
+                        bias_grad[0:1, lanes] = high[10:11]
+
+
+def shape(dims, dtype):
+    return jax.ShapeDtypeStruct(dims, dtype)
+
+
+def call(kernel, micros, room, out_shape, inputs, scratch=(), scalars=1):
+    return pl.pallas_call(
+        kernel,
+        out_shape=out_shape,
+        in_specs=[SSPEC] * scalars + [VSPEC] * (len(inputs) - scalars),
+        out_specs=jax.tree.map(lambda _: VSPEC, out_shape),
+        scratch_shapes=list(scratch),
+        compiler_params=pltpu.CompilerParams(vmem_limit_bytes=room * MIB),
+        cost_estimate=cost(micros),
+    )(*inputs)
+
+
+def cost(micros):
+    return pl.CostEstimate(
+        flops=int(micros * 1.1e9), bytes_accessed=int(micros * 3.4e6), transcendentals=0
+    )
+
+
+def half_gradient(part, left, right, tile, so_far=None):
+    rows, cols = left[0].shape[1], right[0].shape[1]
+    steps = rows // 2 // tile
+    left_spec = pl.BlockSpec((128, tile), lambda m: (0, part * steps + m))
+    right_spec = pl.BlockSpec((128, cols), lambda m: (0, 0))
+    whole = right[1] is right[0]
+    other_spec = pl.BlockSpec((128, cols), lambda m: (1, 0)) if whole else right_spec
+    extra = () if so_far is None else (so_far,)
+    return pl.pallas_call(
+        grad_kernel,
+        grid=(steps,),
+        out_shape=shape((rows, cols), F32),
+        in_specs=[left_spec, left_spec, right_spec, other_spec]
+        + [pl.BlockSpec(memory_space=pl.ANY)] * len(extra),
+        out_specs=pl.BlockSpec((tile, cols), lambda m: (part * steps + m, 0)),
+        input_output_aliases={4: 0} if extra else {},
+        compiler_params=pltpu.CompilerParams(vmem_limit_bytes=16 * MIB),
+        cost_estimate=cost(2.5),
+    )(*left, *right, *extra)
+
+
+def sliced_device(
+    features,
+    cotangent,
+    depth_kernel,
+    depth_bias,
+    norm_gain,
+    norm_shift,
+    up_weight,
+    up_bias,
+    down_weight,
+    layer_scale,
+):
+    channels, hidden_dev = up_weight.shape
+    tiles = channels // LANES
+    index = lax.axis_index("rows")
+    z, y, core = index // 4, (index // 2) % 2, index % 2
+    idx = jnp.stack([z, y, core]).astype(jnp.int32)
+    bias_row, gain_row = depth_bias.reshape(1, channels), norm_gain.reshape(1, channels)
+    shift_row, scale_row = norm_shift.reshape(1, channels), layer_scale.reshape(1, channels)
+    up_bias_row = up_bias.reshape(1, hidden_dev)
+
+    cot_shard = cotangent.reshape(16, channels)
+    planes, across = gather_chips(features)
+    gain_dot, shift_dot, kern, own_shard = call(
+        fold_kernel,
+        1.5,
+        10,
+        (
+            shape((8, hidden_dev), F32),
+            shape((8, hidden_dev), F32),
+            shape(depth_kernel.shape, F32),
+            shape(features.shape, BF16),
+        ),
+        (gain_row, shift_row, up_weight, depth_kernel, features),
+        scalars=0,
+    )
+    planes = [own_shard] + planes[1:]
+    picks = [(2 * (1 - core) + half + 1 - z) % 4 for half in range(2)]
+    chosen = [
+        jnp.stack([lax.select_n(pick, *pieces) for pick in picks]) for pieces in (planes, across)
+    ]
+    with jax.named_scope("feat_core"):
+        feat_came = [send(pieces, C_PAIRS) for pieces in chosen]
+    with jax.named_scope("cot_y"):
+        cot_pair = jnp.stack([cot_shard, send(cot_shard, Y_PAIRS)])
+    with jax.named_scope("cot_z"):
+        cot_late = after(cot_pair, tuple(planes[1:]))
+        cot_planes = [cot_pair] + [send(cot_late, z_pairs(step)) for step in (1, 2, 3)]
+    half_tiles = tiles // 2
+    turn = VMEM((4, 16, LANES), F32)
+    square = VMEM((128, LANES), F32)
+    conv_args = (*planes, *across, *feat_came, kern, bias_row)
+    feats_low, conv_low, total_low = call(
+        conv_kernel,
+        8.0,
+        12,
+        (
+            shape((half_tiles, 4, 48, LANES), F32),
+            shape((half_tiles, 128, LANES), F32),
+            shape((128, LANES), F32),
+        ),
+        (after(idx, (cot_planes[1], cot_planes[3])), *conv_args),
+        (turn,),
+    )
+    normed, f_slice, u_slice, inv_slice = call(
+        conv_norm_kernel,
+        8.0,
+        12,
+        (
+            shape((128, channels), BF16),
+            shape((3, 4, 48, LANES), F32),
+            shape((3, 128, LANES), F32),
+            shape((128, LANES), F32),
+        ),
+        (
+            idx, *conv_args, gain_row, shift_row,
+            feats_low, conv_low, total_low,
+        ),
+        (
+            VMEM((half_tiles, 4, 48, LANES), F32),
+            VMEM((half_tiles, 128, LANES), F32),
+            turn,
+            square,
+            square,
+            square,
+        ),
+    )
+    with jax.named_scope("cot_core"):
+        cot_came = [send(after(plane, inv_slice), C_PAIRS) for plane in cot_planes]
+    normed_other = send(normed, C_PAIRS)
+    cot_all, cot_slice = call(
+        cot_kernel,
+        1.5,
+        8,
+        (shape((256, channels), BF16), shape((3, 128, LANES), F32)),
+        (idx, *cot_planes, *cot_came, scale_row),
+    )
+    hid_grad = call(
+        hid_kernel, 1.5, 8, shape((256, hidden_dev), F32), (cot_all, down_weight), scalars=0
+    )
+    halves = [
+        call(
+            functools.partial(act_kernel, half),
+            1.7,
+            12,
+            (
+                shape((128, hidden_dev), BF16),
+                shape((128, hidden_dev), BF16),
+                shape((1, hidden_dev), F32),
+                shape((16, LANES), F32),
+            ),
+            (value, up_weight, up_bias_row, hid_grad, gain_dot, shift_dot),
+            scalars=0,
+        )
+        for half, value in enumerate((normed, normed_other))
+    ]
+    hidden = [part[0] for part in halves]
+    act_grad = [part[1] for part in halves]
+    sums = [part[3] for part in halves]
+
+    arrived, came_at, keep_at, across_at = {}, {}, {}, {}
+    for pair in ((1, 2), (3, 0)):
+        keep, away = call(
+            functools.partial(norm_grad_kernel, pair),
+            1.6,
+            10,
+            (shape((2, 2, 144, 384), F32), shape((2, 2, 144, 384), BF16)),
+            (idx, *act_grad, up_weight, *sums),
+        )
+        came = send(away, C_PAIRS)
+        for at, step in enumerate(pair):
+            came_at[step], keep_at[step] = came[at].astype(F32), keep[at]
+            across_at[step] = send((keep[at, 1] + came_at[step][1]).astype(BF16), Y_PAIRS)
+    cots = (cot_all, cot_all)
+    down_low = half_gradient(0, after(tuple(hidden), came), cots, 128)
+    for step in (1, 2, 3, 0):
+        total = keep_at[step][0] + came_at[step][0]
+        if step == 2:
+            total = after(total, down_low[0, 0])
+        total = total + across_at[step].astype(F32)
+        if step:
+            total = send(total.astype(BF16), flipped(z_pairs(step)))
+        arrived[step] = total
+    down_grad = half_gradient(1, after(tuple(hidden), across_at[0]), cots, 128, down_low)
+    ig_keep, core_msg, small_keep = call(
+        conv_back_kernel,
+        2.2,
+        12,
+        (shape((4, 16, 384), BF16), shape((6, 16, 384), BF16), shape((2, 16, 384), F32)),
+        (
+            after(idx, down_grad[0, 0]), arrived[0], arrived[1], arrived[2], arrived[3], f_slice, u_slice, inv_slice,
+            gain_row, kern, cot_slice,
+        ),
+        (
+            VMEM((3, 4, 48, LANES), F32),
+            VMEM((3, 128, LANES), F32),
+            VMEM((3, 128, LANES), F32),
+            VMEM((64, 384), F32),
+        ),
+    )
+    core_msg = send(core_msg, C_PAIRS)
+    msgs = call(
+        route_kernel,
+        0.5,
+        4,
+        tuple(shape((4, 16, 384), BF16) for _ in range(4)),
+        (idx, ig_keep, core_msg, small_keep),
+    )
+    msgs = [msgs[0]] + [send(msgs[step], flipped(z_pairs(step))) for step in (1, 2, 3)]
+    up_low = half_gradient(0, after((normed, normed_other), msgs[1]), act_grad, 512)
+    came = send(jnp.stack([msg[1:4] for msg in msgs]), Y_PAIRS)
+    core_a = send(jnp.stack([msg[2:4] for msg in msgs]), C_PAIRS)
+    up_grad = half_gradient(1, after((normed, normed_other), core_a), act_grad, 512, up_low)
+    core_b = send(came[:, 1:3], C_PAIRS)
+    row = shape((1, channels), F32)
+    tokens, kernel_grad, gain_grad, shift_grad, depth_bias_grad = call(
+        place_kernel,
+        0.8,
+        8,
+        (shape((4, 4, channels), BF16), shape((7, 7, channels), F32), row, row, row),
+        (idx, *msgs, came, core_a, core_b),
+    )
+    return (
+        tokens,
+        up_grad,
+        (halves[0][2] + halves[1][2]).reshape(hidden_dev),
+        down_grad,
+        kernel_grad,
+        depth_bias_grad.reshape(channels),
+        gain_grad.reshape(channels),
+        shift_grad.reshape(channels),
+    )
+
+
+def on_device(features, *rest):
+    rows_dev, cols, channels = features.shape
+    fits = lax.axis_size("rows") == 16 and rows_dev == 4 and cols == 4 and channels == 3072
+    return (sliced_device if fits else generic_device)(features, *rest)
+
+
 def solution(mesh):
     in_specs = (
         P(("groups", "rows"), None, None),

time: 162 us -> 98.6 us (0.61)
  starting transfers between devices: 66.4 us -> 29.2 us
  Pallas kernels: 0 us -> 32.3 us
  other arithmetic: 29 us -> 1.68 us
  matrix products: 16.8 us -> 0 us
  waiting for transfers between devices: 33.4 us -> 25.5 us
  local copies, waits for them, and re-layouts: 13.2 us -> 8.37 us
  between operations: 2.77 us -> 1.09 us
    ppermute x50 -> x34, starting transfers between devices: 66.4 us -> 29.2 us  [send(): return lax.ppermute(value, 'rows', pairs)]
    pallas_call x0 -> x16, Pallas kernels: none -> 32.3 us  [the longest x12 19.7 us: call(): pl.pallas_call(kernel, out_shape=out_shape, in_specs=[SSPEC] * scalars +...]
    dot_general x10 -> x0, matrix products: 16.8 us -> none  [contract(): lax.dot_general(left, right, (((left_dim,), (right_dim,)), ((), ())), pre...]
    concatenate x4 -> x0, other arithmetic: 11.5 us -> none  [the longest x1 6.68 us: on_device(): jnp.concatenate([contract(n, act_grad, 0, 0) for n in normed_all], axis=0)]
    reduce_sum x7 -> x0, other arithmetic: 9.62 us -> none  [the longest x1 5.13 us: on_device(): row_mean = jnp.mean(conv_out, axis=-1, keepdims=True)]
    slice x8 -> x1, local copies, waits for them, and re-layouts: 8.16 us -> 0.01 us  [sliced_device(): core_b = send(came[:, 1:3], C_PAIRS)]
    ppermute x50 -> x34, waiting for transfers between devices: 33.4 us -> 25.5 us  [send(): return lax.ppermute(value, 'rows', pairs)]
    convert_element_type x13 -> x7, other arithmetic: 6.32 us -> 0.4 us  [the longest x3 0.16 us: sliced_device(): total = send(total.astype(BF16), flipped(z_pairs(step)))]
  transfers between devices with their start and end apart: 50 -> 34, of which waited for: 13 -> 17; matrix products, arithmetic and copies ran while one was open for 24% -> 4% of each run, Pallas kernels for 0% -> 25%
where the time goes in v3:
time: 98.6 us; the launch traced here: 98.1 us
  Pallas kernels  32.3 us (33%)
  starting transfers between devices  29.2 us (30%)
  waiting for transfers between devices  25.5 us (26%)
  local copies, waits for them, and re-layouts  8.37 us (8%)
  other arithmetic  1.68 us (2%)
  between operations  1.09 us (1%)
    ppermute x34, starting transfers between devices, send(): return lax.ppermute(value, 'rows', pairs)  29.2 us
    ppermute x34, waiting for transfers between devices, send(): return lax.ppermute(value, 'rows', pairs)  25.5 us
    pallas_call x12, Pallas kernels, call(): pl.pallas_call(kernel, out_shape=out_shape, in_specs=[SSPEC] * scalars +...  19.7 us
    pallas_call x4, Pallas kernels, half_gradient(): pl.pallas_call(grad_kernel, grid=(steps,), out_shape=shape((rows, cols),...  12.6 us
    unnamed x30, local copies, waits for them, and re-layouts  6.49 us
  transfers between devices with their start and end apart: 34, of which 17 were waited for; matrix products, arithmetic and copies ran while one was open for 4% of the time, Pallas kernels for 25%

profile of v3, /device:TPU:0, one launch (start us, length us, event | category | flops | bytes accessed | tf_op | source)
XLA Modules:
  0.0 98.1 jit_solution(18282051379066353350)
XLA Ops:
  0.6 5.1 %collective-permute-start = (bf16[4,4,3072]{2,1,0:T(4,128)(2,1)}, bf16[4,4,3072]{2,1,0:T(4,128)(2,1)S(1)}, u32[]{:S(2)}, u32[]{:S(2)}) collective-permute-start(bf16[4,4,3072]{2,1,0:T(4,128)(2,1)} %shard.1), channel_id=1, source_target_pairs={{4,0},{5,1},{6,2},{7,3},{8,4},{9,5},{10,6},{11,7},{12,8},{13,9},{1... | collective-permute-start | bytes 294920 | tf_op jit(solution)/shard_map/feat_z/ppermute | solution.py:41
  6.7 1.5 %collective-permute-start.3 = (bf16[4,4,3072]{2,1,0:T(4,128)(2,1)}, bf16[4,4,3072]{2,1,0:T(4,128)(2,1)S(1)}, u32[]{:S(2)}, u32[]{:S(2)}) collective-permute-start(bf16[4,4,3072]{2,1,0:T(4,128)(2,1)} %shard.1), channel_id=1, source_target_pairs={{2,0},{3,1},{0,2},{1,3},{6,4},{7,5},{4,6},{5,7},{10,8},{11,9},{8,1... | collective-permute-start | bytes 294920 | tf_op jit(solution)/shard_map/feat_y/ppermute | solution.py:41
  10.7 2.3 %copy-done = bf16[3072,768]{1,0:T(8,128)(2,1)S(1)} copy-done((bf16[3072,768]{1,0:T(8,128)(2,1)S(1)}, bf16[3072,768]{1,0:T(8,128)(2,1)}, u32[]{:S(2)}) %copy-start) | copy-done | bytes 4718616
  17.3 2.9 %collective-permute-start.10 = (bf16[2,16,3072]{2,1,0:T(8,128)(2,1)S(1)}, bf16[2,16,3072]{2,1,0:T(8,128)(2,1)S(1)}, u32[]{:S(2)}, u32[]{:S(2)}) collective-permute-start(bf16[2,16,3072]{2,1,0:T(8,128)(2,1)S(1)} %pad_maximum_fusion.2.refs_0_), channel_id=1, source_target_pairs={{4,0},{5,1},{6,2},{7,3},{8,4},{9,5},{10,6},{11,7},{12,8},{13,9},{1... | collective-permute-start | bytes 589832 | tf_op jit(solution)/shard_map/cot_z/ppermute | solution.py:41
  20.2 1.5 %collective-permute-start.4 = (bf16[4,4,3072]{2,1,0:T(4,128)(2,1)S(1)}, bf16[4,4,3072]{2,1,0:T(4,128)(2,1)S(1)}, u32[]{:S(2)}, u32[]{:S(2)}) collective-permute-start(bf16[4,4,3072]{2,1,0:T(4,128)(2,1)S(1)} %collective-permute-done.refs_1_), channel_id=1, source_target_pairs={{2,0},{3,1},{0,2},{1,3},{6,4},{7,5},{4,6},{5,7},{10,8},{11,9},{8,1... | collective-permute-start | bytes 294920 | tf_op jit(solution)/shard_map/feat_y/ppermute | solution.py:41
  24.1 1.5 %collective-permute-done.4.refs_5_ = bf16[4,4,3072]{2,1,0:T(4,128)(2,1)S(1)} collective-permute-done((bf16[4,4,3072]{2,1,0:T(4,128)(2,1)S(1)}, bf16[4,4,3072]{2,1,0:T(4,128)(2,1)S(1)}, u32[]{:S(2)}, u32[]{:S(2)}) %collective-permute-start.4) | collective-permute-done | bytes 98336 | tf_op jit(solution)/shard_map/feat_y/ppermute | solution.py:41
  29.0 2.7 %collective-permute-done.11.refs_3_ = bf16[2,16,3072]{2,1,0:T(8,128)(2,1)S(1)} collective-permute-done((bf16[2,16,3072]{2,1,0:T(8,128)(2,1)S(1)}, bf16[2,16,3072]{2,1,0:T(8,128)(2,1)S(1)}, u32[]{:S(2)}, u32[]{:S(2)}) %collective-permute-start.11) | collective-permute-done | bytes 196640 | tf_op jit(solution)/shard_map/cot_z/ppermute | solution.py:41
  32.4 2.6 %shard_map.162 = (f32[12,4,48,128]{3,2,1,0:T(8,128)S(1)}, f32[12,128,128]{2,1,0:T(8,128)S(1)}, f32[128,128]{1,0:T(8,128)S(1)}) custom-call(s32[3]{0:T(128)S(1)} %pad_add_fusion.idx, bf16[4,4,3072]{2,1,0:T(4,128)(2,1)S(1)} %get-tuple-element.59.refs_0_, bf16[4,4,3072]{2,1,0:T(4,128)(2,1)S(1)} %collective-permute-done.refs_1_, ...), custom_call_target="tpu_custom_call" | custom-call | flops 8800000000 | bytes 27200000 | tf_op jit(solution)/shard_map/pallas_call | solution.py:579
  35.1 3.4 %shard_map.163 = (bf16[128,3072]{1,0:T(8,128)(2,1)S(1)}, f32[3,4,48,128]{3,2,1,0:T(8,128)S(1)}, f32[3,128,128]{2,1,0:T(8,128)S(1)}, f32[128,128]{1,0:T(8,128)S(1)}) custom-call(s32[3]{0:T(128)S(1)} %pad_add_fusion.idx, bf16[4,4,3072]{2,1,0:T(4,128)(2,1)S(1)} %get-tuple-element.59.refs_0_, bf16[4,4,3072]{2,1,0:T(4,128)(2,1)S(1)} %collective-permute-done.refs_1_, ...), custom_call_target="tpu_custom_call" | custom-call | flops 8800000000 | bytes 27200000 | tf_op jit(solution)/shard_map/pallas_call | solution.py:579
  44.4 1.7 %shard_map.166 = (bf16[128,768]{1,0:T(8,128)(2,1)S(1)}, bf16[128,768]{1,0:T(8,128)(2,1)S(1)}, f32[1,768]{1,0:T(1,128)S(1)}, f32[16,128]{1,0:T(8,128)S(1)}) custom-call(bf16[128,3072]{1,0:T(8,128)(2,1)S(1)} %get-tuple-element.96.normed.left_own, bf16[3072,768]{1,0:T(8,128)(2,1)S(1)} %bitcast.64, f32[1,768]{1,0:T(1,128)S(1)} %reshape.90.up_bias, ...), custom_call_target="tpu_custom_call" | custom-call | flops 1870000000 | bytes 5780000 | tf_op jit(solution)/shard_map/pallas_call | solution.py:579
  46.1 1.7 %shard_map.167 = (bf16[128,768]{1,0:T(8,128)(2,1)S(1)}, bf16[128,768]{1,0:T(8,128)(2,1)S(1)}, f32[1,768]{1,0:T(1,128)S(1)}, f32[16,128]{1,0:T(8,128)S(1)}) custom-call(bf16[128,3072]{1,0:T(8,128)(2,1)S(1)} %collective-permute-done.17.normed.left_other, bf16[3072,768]{1,0:T(8,128)(2,1)S(1)} %bitcast.64, f32[1,768]{1,0:T(1,128)S(1)} %reshape.90.up_bias, ...), custom_call_target="tpu_custom_call" | custom-call | flops 1870000000 | bytes 5780000 | tf_op jit(solution)/shard_map/pallas_call | solution.py:579
  47.8 1.6 %shard_map.169 = (f32[2,2,144,384]{3,2,1,0:T(8,128)S(1)}, bf16[2,2,144,384]{3,2,1,0:T(8,128)(2,1)S(1)}) custom-call(s32[3]{0:T(128)S(1)} %pad_add_fusion.idx, bf16[128,768]{1,0:T(8,128)(2,1)S(1)} %get-tuple-element.75.act_own.right_own, bf16[128,768]{1,0:T(8,128)(2,1)S(1)} %get-tuple-element.76.act_other.right_other, bf16[3072,768]{1,0:T(8,128)(2,1)S(1)} %bitcast.64, ...), custom_call_target="tpu_custom_call" | custom-call | flops 1760000000 | bytes 5440000 | tf_op jit(solution)/shard_map/pallas_call | solution.py:579
  49.6 1.5 %shard_map.168 = (f32[2,2,144,384]{3,2,1,0:T(8,128)S(1)}, bf16[2,2,144,384]{3,2,1,0:T(8,128)(2,1)S(1)}) custom-call(s32[3]{0:T(128)S(1)} %pad_add_fusion.idx, bf16[128,768]{1,0:T(8,128)(2,1)S(1)} %get-tuple-element.75.act_own.right_own, bf16[128,768]{1,0:T(8,128)(2,1)S(1)} %get-tuple-element.76.act_other.right_other, bf16[3072,768]{1,0:T(8,128)(2,1)S(1)} %bitcast.64, ...), custom_call_target="tpu_custom_call" | custom-call | flops 1760000000 | bytes 5440000 | tf_op jit(solution)/shard_map/pallas_call | solution.py:579
  56.6 1.7 %collective-permute-done.23 = bf16[144,384]{1,0:T(8,128)(2,1)S(1)} collective-permute-done((bf16[144,384]{1,0:T(8,128)(2,1)S(1)}, bf16[144,384]{1,0:T(8,128)(2,1)S(1)}, u32[]{:S(2)}, u32[]{:S(2)}) %collective-permute-start.23) | collective-permute-done | bytes 110624 | tf_op jit(solution)/shard_map/ppermute | solution.py:41
  58.4 4.6 %collective-permute-done.21 = bf16[144,384]{1,0:T(8,128)(2,1)S(1)} collective-permute-done((bf16[144,384]{1,0:T(8,128)(2,1)S(1)}, bf16[144,384]{1,0:T(8,128)(2,1)S(1)}, u32[]{:S(2)}, u32[]{:S(2)}) %collective-permute-start.21) | collective-permute-done | bytes 110624 | tf_op jit(solution)/shard_map/ppermute | solution.py:41
  64.7 2.6 %collective-permute-start.26 = (bf16[144,384]{1,0:T(8,128)(2,1)S(1)}, bf16[144,384]{1,0:T(8,128)(2,1)S(1)}, u32[]{:S(2)}, u32[]{:S(2)}) collective-permute-start(bf16[144,384]{1,0:T(8,128)(2,1)S(1)} %get-tuple-element.112), channel_id=1, source_target_pairs={{0,12},{1,13},{2,14},{3,15},{4,0},{5,1},{6,2},{7,3},{8,4},{9,5},{1... | collective-permute-start | bytes 331784 | tf_op jit(solution)/shard_map/ppermute | solution.py:41
  67.2 3.1 %shard_map.175.rest_0_ = f32[768,3072]{1,0:T(8,128)} custom-call(bf16[128,768]{1,0:T(8,128)(2,1)S(1)} %get-tuple-element.104.left_own, bf16[128,768]{1,0:T(8,128)(2,1)S(1)} %get-tuple-element.105.left_other, bf16[256,3072]{1,0:T(8,128)(2,1)S(1)} %get-tuple-element.72.cot_all.right_own.right_other, ...), custom_call_target="tpu_custom_call" | custom-call | flops 2750000128 | bytes 8500000 | tf_op jit(solution)/shard_map/pallas_call | solution.py:604
  70.9 2.0 %shard_map.170 = (bf16[4,16,384]{2,1,0:T(8,128)(2,1)S(1)}, bf16[6,16,384]{2,1,0:T(8,128)(2,1)S(1)}, f32[2,16,384]{2,1,0:T(8,128)S(1)}) custom-call(s32[3]{0:T(128)S(1)} %pad_add_fusion.idx, f32[144,384]{1,0:T(8,128)S(1)} %get-tuple-element.113.own, bf16[144,384]{1,0:T(8,128)(2,1)S(1)} %collective-permute-done.22.near_1, ...), custom_call_target="tpu_custom_call" | custom-call | flops 2420000000 | bytes 7480000 | tf_op jit(solution)/shard_map/pallas_call | solution.py:579
  72.9 3.1 %shard_map.176 = f32[768,3072]{1,0:T(8,128)} custom-call(bf16[128,768]{1,0:T(8,128)(2,1)S(1)} %get-tuple-element.104.left_own, bf16[128,768]{1,0:T(8,128)(2,1)S(1)} %get-tuple-element.105.left_other, bf16[256,3072]{1,0:T(8,128)(2,1)S(1)} %get-tuple-element.72.cot_all.right_own.right_other, ...), custom_call_target="tpu_custom_call", output_to_operand_aliasing={{}: (4, {})} | custom-call | flops 2750000128 | bytes 8500000 | tf_op jit(solution)/shard_map/pallas_call | solution.py:604
  76.7 3.0 %collective-permute-start.30 = (bf16[4,16,384]{2,1,0:T(8,128)(2,1)S(1)}, bf16[4,16,384]{2,1,0:T(8,128)(2,1)S(1)}, u32[]{:S(2)}, u32[]{:S(2)}) collective-permute-start(bf16[4,16,384]{2,1,0:T(8,128)(2,1)S(1)} %get-tuple-element.92), channel_id=1, source_target_pairs={{0,12},{1,13},{2,14},{3,15},{4,0},{5,1},{6,2},{7,3},{8,4},{9,5},{1... | collective-permute-start | bytes 147464 | tf_op jit(solution)/shard_map/ppermute | solution.py:41
  81.7 4.3 %collective-permute-done.28.refs_1_ = bf16[4,16,384]{2,1,0:T(8,128)(2,1)S(1)} collective-permute-done((bf16[4,16,384]{2,1,0:T(8,128)(2,1)S(1)}, bf16[4,16,384]{2,1,0:T(8,128)(2,1)S(1)}, u32[]{:S(2)}, u32[]{:S(2)}) %collective-permute-start.28) | collective-permute-done | bytes 49184 | tf_op jit(solution)/shard_map/ppermute | solution.py:41
  88.2 3.2 %shard_map.173.rest_0_ = f32[3072,768]{1,0:T(8,128)} custom-call(bf16[128,3072]{1,0:T(8,128)(2,1)S(1)} %get-tuple-element.96.normed.left_own, bf16[128,3072]{1,0:T(8,128)(2,1)S(1)} %collective-permute-done.17.normed.left_other, bf16[128,768]{1,0:T(8,128)(2,1)S(1)} %get-tuple-element.75.act_own.right_own, ...), custom_call_target="tpu_custom_call" | custom-call | flops 2750000128 | bytes 8500000 | tf_op jit(solution)/shard_map/pallas_call | solution.py:604
  91.4 2.0 %collective-permute-done.31.refs_4_ = bf16[4,3,16,384]{3,2,1,0:T(8,128)(2,1)S(1)} collective-permute-done((bf16[4,3,16,384]{3,2,1,0:T(8,128)(2,1)S(1)}, bf16[4,3,16,384]{3,2,1,0:T(8,128)(2,1)S(1)}, u32[]{:S(2)}, u32[]{:S(2)}) %collective-permute-start.31) | collective-permute-done | bytes 147488 | tf_op jit(solution)/shard_map/ppermute | solution.py:41
  93.5 3.2 %shard_map.174 = f32[3072,768]{1,0:T(8,128)} custom-call(bf16[128,3072]{1,0:T(8,128)(2,1)S(1)} %get-tuple-element.96.normed.left_own, bf16[128,3072]{1,0:T(8,128)(2,1)S(1)} %collective-permute-done.17.normed.left_other, bf16[128,768]{1,0:T(8,128)(2,1)S(1)} %get-tuple-element.75.act_own.right_own, ...), custom_call_target="tpu_custom_call", output_to_operand_aliasing={{}: (4, {})} | custom-call | flops 2750000128 | bytes 8500000 | tf_op jit(solution)/shard_map/pallas_call | solution.py:604
  (120 shorter events, 34.3 us)
Async XLA Ops:
  0.6 16.6 %collective-permute-start = (bf16[4,4,3072]{2,1,0:T(4,128)(2,1)}, bf16[4,4,3072]{2,1,0:T(4,128)(2,1)S(1)}, u32[]{:S(2)}, u32[]{:S(2)}) collective-permute-start(bf16[4,4,3072]{2,1,0:T(4,128)(2,1)} %shard.1), channel_id=1, source_target_pairs={{4,0},{5,1},{6,2},{7,3},{8,4},{9,5},{10,6},{11,7},{12,8},{13,9},{1... | collective-permute-start | bytes 294920 | tf_op jit(solution)/shard_map/feat_z/ppermute | solution.py:41
  5.7 11.5 %collective-permute-start.1 = (bf16[4,4,3072]{2,1,0:T(4,128)(2,1)}, bf16[4,4,3072]{2,1,0:T(4,128)(2,1)S(1)}, u32[]{:S(2)}, u32[]{:S(2)}) collective-permute-start(bf16[4,4,3072]{2,1,0:T(4,128)(2,1)} %shard.1), channel_id=1, source_target_pairs={{8,0},{9,1},{10,2},{11,3},{12,4},{13,5},{14,6},{15,7},{0,8},{1,9},... | collective-permute-start | bytes 294920 | tf_op jit(solution)/shard_map/feat_z/ppermute | solution.py:41
  5.7 11.6 %collective-permute-start.2 = (bf16[4,4,3072]{2,1,0:T(4,128)(2,1)}, bf16[4,4,3072]{2,1,0:T(4,128)(2,1)S(1)}, u32[]{:S(2)}, u32[]{:S(2)}) collective-permute-start(bf16[4,4,3072]{2,1,0:T(4,128)(2,1)} %shard.1), channel_id=1, source_target_pairs={{12,0},{13,1},{14,2},{15,3},{0,4},{1,5},{2,6},{3,7},{4,8},{5,9},{6... | collective-permute-start | bytes 294920 | tf_op jit(solution)/shard_map/feat_z/ppermute | solution.py:41
  6.7 17.2 %collective-permute-start.3 = (bf16[4,4,3072]{2,1,0:T(4,128)(2,1)}, bf16[4,4,3072]{2,1,0:T(4,128)(2,1)S(1)}, u32[]{:S(2)}, u32[]{:S(2)}) collective-permute-start(bf16[4,4,3072]{2,1,0:T(4,128)(2,1)} %shard.1), channel_id=1, source_target_pairs={{2,0},{3,1},{0,2},{1,3},{6,4},{7,5},{4,6},{5,7},{10,8},{11,9},{8,1... | collective-permute-start | bytes 294920 | tf_op jit(solution)/shard_map/feat_y/ppermute | solution.py:41
  9.2 8.0 %collective-permute-start.9 = (bf16[16,3072]{1,0:T(8,128)(2,1)S(1)}, bf16[16,3072]{1,0:T(8,128)(2,1)S(1)}, u32[]{:S(2)}, u32[]{:S(2)}) collective-permute-start(bf16[16,3072]{1,0:T(8,128)(2,1)S(1)} %reshape.89), channel_id=1, source_target_pairs={{2,0},{3,1},{0,2},{1,3},{6,4},{7,5},{4,6},{5,7},{10,8},{11,9},{8,1... | collective-permute-start | bytes 294920 | tf_op jit(solution)/shard_map/cot_y/ppermute | solution.py:41
  17.3 11.7 %collective-permute-start.10 = (bf16[2,16,3072]{2,1,0:T(8,128)(2,1)S(1)}, bf16[2,16,3072]{2,1,0:T(8,128)(2,1)S(1)}, u32[]{:S(2)}, u32[]{:S(2)}) collective-permute-start(bf16[2,16,3072]{2,1,0:T(8,128)(2,1)S(1)} %pad_maximum_fusion.2.refs_0_), channel_id=1, source_target_pairs={{4,0},{5,1},{6,2},{7,3},{8,4},{9,5},{10,6},{11,7},{12,8},{13,9},{1... | collective-permute-start | bytes 589832 | tf_op jit(solution)/shard_map/cot_z/ppermute | solution.py:41
  20.2 5.4 %collective-permute-start.4 = (bf16[4,4,3072]{2,1,0:T(4,128)(2,1)S(1)}, bf16[4,4,3072]{2,1,0:T(4,128)(2,1)S(1)}, u32[]{:S(2)}, u32[]{:S(2)}) collective-permute-start(bf16[4,4,3072]{2,1,0:T(4,128)(2,1)S(1)} %collective-permute-done.refs_1_), channel_id=1, source_target_pairs={{2,0},{3,1},{0,2},{1,3},{6,4},{7,5},{4,6},{5,7},{10,8},{11,9},{8,1... | collective-permute-start | bytes 294920 | tf_op jit(solution)/shard_map/feat_y/ppermute | solution.py:41
  21.7 5.0 %collective-permute-start.5 = (bf16[4,4,3072]{2,1,0:T(4,128)(2,1)S(1)}, bf16[4,4,3072]{2,1,0:T(4,128)(2,1)S(1)}, u32[]{:S(2)}, u32[]{:S(2)}) collective-permute-start(bf16[4,4,3072]{2,1,0:T(4,128)(2,1)S(1)} %collective-permute-done.1.refs_2_), channel_id=1, source_target_pairs={{2,0},{3,1},{0,2},{1,3},{6,4},{7,5},{4,6},{5,7},{10,8},{11,9},{8,1... | collective-permute-start | bytes 294920 | tf_op jit(solution)/shard_map/feat_y/ppermute | solution.py:41
  22.2 5.5 %collective-permute-start.6 = (bf16[4,4,3072]{2,1,0:T(4,128)(2,1)S(1)}, bf16[4,4,3072]{2,1,0:T(4,128)(2,1)S(1)}, u32[]{:S(2)}, u32[]{:S(2)}) collective-permute-start(bf16[4,4,3072]{2,1,0:T(4,128)(2,1)S(1)} %collective-permute-done.2.refs_3_), channel_id=1, source_target_pairs={{2,0},{3,1},{0,2},{1,3},{6,4},{7,5},{4,6},{5,7},{10,8},{11,9},{8,1... | collective-permute-start | bytes 294920 | tf_op jit(solution)/shard_map/feat_y/ppermute | solution.py:41
  24.0 7.7 %collective-permute-start.11 = (bf16[2,16,3072]{2,1,0:T(8,128)(2,1)S(1)}, bf16[2,16,3072]{2,1,0:T(8,128)(2,1)S(1)}, u32[]{:S(2)}, u32[]{:S(2)}) collective-permute-start(bf16[2,16,3072]{2,1,0:T(8,128)(2,1)S(1)} %pad_maximum_fusion.2.refs_0_), channel_id=1, source_target_pairs={{12,0},{13,1},{14,2},{15,3},{0,4},{1,5},{2,6},{3,7},{4,8},{5,9},{6... | collective-permute-start | bytes 589832 | tf_op jit(solution)/shard_map/cot_z/ppermute | solution.py:41
  25.6 6.1 %collective-permute-start.7 = (bf16[2,4,4,3072]{3,2,1,0:T(4,128)(2,1)S(1)}, bf16[2,4,4,3072]{3,2,1,0:T(4,128)(2,1)S(1)}, u32[]{:S(2)}, u32[]{:S(2)}) collective-permute-start(bf16[2,4,4,3072]{3,2,1,0:T(4,128)(2,1)S(1)} %pad_maximum_fusion), channel_id=1, source_target_pairs={{1,0},{0,1},{3,2},{2,3},{5,4},{4,5},{7,6},{6,7},{9,8},{8,9},{11,10... | collective-permute-start | bytes 589832 | tf_op jit(solution)/shard_map/feat_core/ppermute | solution.py:41
  28.2 11.8 %collective-permute-start.12 = (bf16[2,16,3072]{2,1,0:T(8,128)(2,1)S(1)}, bf16[2,16,3072]{2,1,0:T(8,128)(2,1)S(1)}, u32[]{:S(2)}, u32[]{:S(2)}) collective-permute-start(bf16[2,16,3072]{2,1,0:T(8,128)(2,1)S(1)} %pad_maximum_fusion.2.refs_0_), channel_id=1, source_target_pairs={{8,0},{9,1},{10,2},{11,3},{12,4},{13,5},{14,6},{15,7},{0,8},{1,9},... | collective-permute-start | bytes 589832 | tf_op jit(solution)/shard_map/cot_z/ppermute | solution.py:41
  38.5 7.6 %collective-permute-start.17 = (bf16[128,3072]{1,0:T(8,128)(2,1)S(1)}, bf16[128,3072]{1,0:T(8,128)(2,1)S(1)}, u32[]{:S(2)}, u32[]{:S(2)}) collective-permute-start(bf16[128,3072]{1,0:T(8,128)(2,1)S(1)} %get-tuple-element.96.normed.left_own), channel_id=1, source_target_pairs={{1,0},{0,1},{3,2},{2,3},{5,4},{4,5},{7,6},{6,7},{9,8},{8,9},{11,10... | collective-permute-start | bytes 2359304 | tf_op jit(solution)/shard_map/ppermute | solution.py:41
  52.3 6.0 %collective-permute-start.23 = (bf16[144,384]{1,0:T(8,128)(2,1)S(1)}, bf16[144,384]{1,0:T(8,128)(2,1)S(1)}, u32[]{:S(2)}, u32[]{:S(2)}) collective-permute-start(bf16[144,384]{1,0:T(8,128)(2,1)S(1)} %get-tuple-element.110), channel_id=1, source_target_pairs={{2,0},{3,1},{0,2},{1,3},{6,4},{7,5},{4,6},{5,7},{10,8},{11,9},{8,1... | collective-permute-start | bytes 331784 | tf_op jit(solution)/shard_map/ppermute | solution.py:41
  53.5 9.6 %collective-permute-start.19 = (bf16[144,384]{1,0:T(8,128)(2,1)S(1)}, bf16[144,384]{1,0:T(8,128)(2,1)S(1)}, u32[]{:S(2)}, u32[]{:S(2)}) collective-permute-start(bf16[144,384]{1,0:T(8,128)(2,1)S(1)} %get-tuple-element.115), channel_id=1, source_target_pairs={{2,0},{3,1},{0,2},{1,3},{6,4},{7,5},{4,6},{5,7},{10,8},{11,9},{8,1... | collective-permute-start | bytes 331784 | tf_op jit(solution)/shard_map/ppermute | solution.py:41
  54.6 8.4 %collective-permute-start.21 = (bf16[144,384]{1,0:T(8,128)(2,1)S(1)}, bf16[144,384]{1,0:T(8,128)(2,1)S(1)}, u32[]{:S(2)}, u32[]{:S(2)}) collective-permute-start(bf16[144,384]{1,0:T(8,128)(2,1)S(1)} %get-tuple-element.116), channel_id=1, source_target_pairs={{2,0},{3,1},{0,2},{1,3},{6,4},{7,5},{4,6},{5,7},{10,8},{11,9},{8,1... | collective-permute-start | bytes 331784 | tf_op jit(solution)/shard_map/ppermute | solution.py:41
  55.6 9.0 %collective-permute-start.25 = (bf16[144,384]{1,0:T(8,128)(2,1)S(1)}, bf16[144,384]{1,0:T(8,128)(2,1)S(1)}, u32[]{:S(2)}, u32[]{:S(2)}) collective-permute-start(bf16[144,384]{1,0:T(8,128)(2,1)S(1)} %get-tuple-element.114), channel_id=1, source_target_pairs={{2,0},{3,1},{0,2},{1,3},{6,4},{7,5},{4,6},{5,7},{10,8},{11,9},{8,1... | collective-permute-start | bytes 331784 | tf_op jit(solution)/shard_map/ppermute | solution.py:41
  58.3 12.1 %collective-permute-start.24 = (bf16[144,384]{1,0:T(8,128)(2,1)S(1)}, bf16[144,384]{1,0:T(8,128)(2,1)S(1)}, u32[]{:S(2)}, u32[]{:S(2)}) collective-permute-start(bf16[144,384]{1,0:T(8,128)(2,1)S(1)} %add_convert_fusion), channel_id=1, source_target_pairs={{0,8},{1,9},{2,10},{3,11},{4,12},{5,13},{6,14},{7,15},{8,0},{9,1},... | collective-permute-start | bytes 331784 | tf_op jit(solution)/shard_map/ppermute | solution.py:41
  63.0 7.3 %collective-permute-start.22 = (bf16[144,384]{1,0:T(8,128)(2,1)S(1)}, bf16[144,384]{1,0:T(8,128)(2,1)S(1)}, u32[]{:S(2)}, u32[]{:S(2)}) collective-permute-start(bf16[144,384]{1,0:T(8,128)(2,1)S(1)} %fusion.9), channel_id=1, source_target_pairs={{0,4},{1,5},{2,6},{3,7},{4,8},{5,9},{6,10},{7,11},{8,12},{9,13},{1... | collective-permute-start | bytes 331784 | tf_op jit(solution)/shard_map/ppermute | solution.py:41
  64.7 6.2 %collective-permute-start.26 = (bf16[144,384]{1,0:T(8,128)(2,1)S(1)}, bf16[144,384]{1,0:T(8,128)(2,1)S(1)}, u32[]{:S(2)}, u32[]{:S(2)}) collective-permute-start(bf16[144,384]{1,0:T(8,128)(2,1)S(1)} %get-tuple-element.112), channel_id=1, source_target_pairs={{0,12},{1,13},{2,14},{3,15},{4,0},{5,1},{6,2},{7,3},{8,4},{9,5},{1... | collective-permute-start | bytes 331784 | tf_op jit(solution)/shard_map/ppermute | solution.py:41
  76.7 5.0 %collective-permute-start.30 = (bf16[4,16,384]{2,1,0:T(8,128)(2,1)S(1)}, bf16[4,16,384]{2,1,0:T(8,128)(2,1)S(1)}, u32[]{:S(2)}, u32[]{:S(2)}) collective-permute-start(bf16[4,16,384]{2,1,0:T(8,128)(2,1)S(1)} %get-tuple-element.92), channel_id=1, source_target_pairs={{0,12},{1,13},{2,14},{3,15},{4,0},{5,1},{6,2},{7,3},{8,4},{9,5},{1... | collective-permute-start | bytes 147464 | tf_op jit(solution)/shard_map/ppermute | solution.py:41
  79.7 6.3 %collective-permute-start.28 = (bf16[4,16,384]{2,1,0:T(8,128)(2,1)S(1)}, bf16[4,16,384]{2,1,0:T(8,128)(2,1)S(1)}, u32[]{:S(2)}, u32[]{:S(2)}) collective-permute-start(bf16[4,16,384]{2,1,0:T(8,128)(2,1)S(1)} %get-tuple-element.90), channel_id=1, source_target_pairs={{0,4},{1,5},{2,6},{3,7},{4,8},{5,9},{6,10},{7,11},{8,12},{9,13},{1... | collective-permute-start | bytes 147464 | tf_op jit(solution)/shard_map/ppermute | solution.py:41
  79.7 7.2 %collective-permute-start.29 = (bf16[4,16,384]{2,1,0:T(8,128)(2,1)S(1)}, bf16[4,16,384]{2,1,0:T(8,128)(2,1)S(1)}, u32[]{:S(2)}, u32[]{:S(2)}) collective-permute-start(bf16[4,16,384]{2,1,0:T(8,128)(2,1)S(1)} %get-tuple-element.91), channel_id=1, source_target_pairs={{0,8},{1,9},{2,10},{3,11},{4,12},{5,13},{6,14},{7,15},{8,0},{9,1},... | collective-permute-start | bytes 147464 | tf_op jit(solution)/shard_map/ppermute | solution.py:41
  87.1 6.3 %collective-permute-start.31 = (bf16[4,3,16,384]{3,2,1,0:T(8,128)(2,1)S(1)}, bf16[4,3,16,384]{3,2,1,0:T(8,128)(2,1)S(1)}, u32[]{:S(2)}, u32[]{:S(2)}) collective-permute-start(bf16[4,3,16,384]{3,2,1,0:T(8,128)(2,1)S(1)} %pad_maximum_fusion.3), channel_id=1, source_target_pairs={{2,0},{3,1},{0,2},{1,3},{6,4},{7,5},{4,6},{5,7},{10,8},{11,9},{8,1... | collective-permute-start | bytes 442376 | tf_op jit(solution)/shard_map/ppermute | solution.py:41
  (25 other events, 91.0 us)

commit v4 on v3

--- a/solution.py
+++ b/solution.py
@@ -661,7 +661,8 @@
         cot_pair = jnp.stack([cot_shard, send(cot_shard, Y_PAIRS)])
     with jax.named_scope("cot_z"):
         cot_late = after(cot_pair, tuple(planes[1:]))
-        cot_planes = [cot_pair] + [send(cot_late, z_pairs(step)) for step in (1, 2, 3)]
+        ahead, behind = send(cot_late, z_pairs(1)), send(cot_late, z_pairs(3))
+        cot_planes = [cot_pair, ahead, send(ahead, z_pairs(1)), behind]
     half_tiles = tiles // 2
     turn = VMEM((4, 16, LANES), F32)
     square = VMEM((128, LANES), F32)
@@ -735,7 +736,7 @@
     sums = [part[3] for part in halves]
 
     arrived, came_at, keep_at, across_at = {}, {}, {}, {}
-    for pair in ((1, 2), (3, 0)):
+    for pair in ((2, 3), (1, 0)):
         keep, away = call(
             functools.partial(norm_grad_kernel, pair),
             1.6,
@@ -749,22 +750,23 @@
             across_at[step] = send((keep[at, 1] + came_at[step][1]).astype(BF16), Y_PAIRS)
     cots = (cot_all, cot_all)
     down_low = half_gradient(0, after(tuple(hidden), came), cots, 128)
-    for step in (1, 2, 3, 0):
+    for step in (2, 3, 1, 0):
         total = keep_at[step][0] + came_at[step][0]
-        if step == 2:
-            total = after(total, down_low[0, 0])
+        if step == 1:
+            total, down_low = lax.optimization_barrier((total, down_low))
         total = total + across_at[step].astype(F32)
         if step:
             total = send(total.astype(BF16), flipped(z_pairs(step)))
         arrived[step] = total
     down_grad = half_gradient(1, after(tuple(hidden), across_at[0]), cots, 128, down_low)
+    late_idx, down_grad = lax.optimization_barrier((idx, down_grad))
     ig_keep, core_msg, small_keep = call(
         conv_back_kernel,
         2.2,
         12,
         (shape((4, 16, 384), BF16), shape((6, 16, 384), BF16), shape((2, 16, 384), F32)),
         (
-            after(idx, down_grad[0, 0]), arrived[0], arrived[1], arrived[2], arrived[3], f_slice, u_slice, inv_slice,
+            late_idx, arrived[0], arrived[1], arrived[2], arrived[3], f_slice, u_slice, inv_slice,
             gain_row, kern, cot_slice,
         ),
         (
@@ -783,11 +785,13 @@
         (idx, ig_keep, core_msg, small_keep),
     )
     msgs = [msgs[0]] + [send(msgs[step], flipped(z_pairs(step))) for step in (1, 2, 3)]
-    up_low = half_gradient(0, after((normed, normed_other), msgs[1]), act_grad, 512)
+    up_low = half_gradient(0, after((normed, normed_other), msgs[3]), act_grad, 512)
+    msgs, up_low = lax.optimization_barrier((msgs, up_low))
     came = send(jnp.stack([msg[1:4] for msg in msgs]), Y_PAIRS)
     core_a = send(jnp.stack([msg[2:4] for msg in msgs]), C_PAIRS)
     up_grad = half_gradient(1, after((normed, normed_other), core_a), act_grad, 512, up_low)
-    core_b = send(came[:, 1:3], C_PAIRS)
+    late, up_grad = lax.optimization_barrier((came[:, 1:3], up_grad))
+    core_b = send(late, C_PAIRS)
     row = shape((1, channels), F32)
     tokens, kernel_grad, gain_grad, shift_grad, depth_bias_grad = call(
         place_kernel,

time: 98.6 us -> 93.3 us (0.946)
  waiting for transfers between devices: 25.5 us -> 18.5 us
  starting transfers between devices: 29.2 us -> 31 us
    ppermute x34, waiting for transfers between devices: 25.5 us -> 18.5 us  [send(): return lax.ppermute(value, 'rows', pairs)]
    ppermute x34, starting transfers between devices: 29.2 us -> 31 us  [send(): return lax.ppermute(value, 'rows', pairs)]
  transfers between devices with their start and end apart: 34 -> 34, of which waited for: 17 -> 18; matrix products, arithmetic and copies ran while one was open for 4% -> 4% of each run, Pallas kernels for 25% -> 27%
where the time goes in v4:
time: 93.3 us; the launch traced here: 92.8 us
  Pallas kernels  32.3 us (35%)
  starting transfers between devices  31 us (33%)
  waiting for transfers between devices  18.5 us (20%)
  local copies, waits for them, and re-layouts  8.36 us (9%)
  other arithmetic  1.67 us (2%)
  between operations  1.07 us (1%)
    ppermute x34, starting transfers between devices, send(): return lax.ppermute(value, 'rows', pairs)  31 us
    pallas_call x12, Pallas kernels, call(): pl.pallas_call(kernel, out_shape=out_shape, in_specs=[SSPEC] * scalars +...  19.7 us
    ppermute x34, waiting for transfers between devices, send(): return lax.ppermute(value, 'rows', pairs)  18.5 us
    pallas_call x4, Pallas kernels, half_gradient(): pl.pallas_call(grad_kernel, grid=(steps,), out_shape=shape((rows, cols),...  12.6 us
    unnamed x30, local copies, waits for them, and re-layouts  6.48 us
  transfers between devices with their start and end apart: 34, of which 18 were waited for; matrix products, arithmetic and copies ran while one was open for 4% of the time, Pallas kernels for 27%

profile of v4, /device:TPU:0, one launch (start us, length us, event | category | flops | bytes accessed | tf_op | source)
XLA Modules:
  0.0 92.8 jit_solution(12172455556114367978)
XLA Ops:
  0.6 5.1 %collective-permute-start = (bf16[4,4,3072]{2,1,0:T(4,128)(2,1)}, bf16[4,4,3072]{2,1,0:T(4,128)(2,1)S(1)}, u32[]{:S(2)}, u32[]{:S(2)}) collective-permute-start(bf16[4,4,3072]{2,1,0:T(4,128)(2,1)} %shard.1), channel_id=1, source_target_pairs={{4,0},{5,1},{6,2},{7,3},{8,4},{9,5},{10,6},{11,7},{12,8},{13,9},{1... | collective-permute-start | bytes 294920 | tf_op jit(solution)/shard_map/feat_z/ppermute | solution.py:41
  6.7 1.5 %collective-permute-start.3 = (bf16[4,4,3072]{2,1,0:T(4,128)(2,1)}, bf16[4,4,3072]{2,1,0:T(4,128)(2,1)S(1)}, u32[]{:S(2)}, u32[]{:S(2)}) collective-permute-start(bf16[4,4,3072]{2,1,0:T(4,128)(2,1)} %shard.1), channel_id=1, source_target_pairs={{2,0},{3,1},{0,2},{1,3},{6,4},{7,5},{4,6},{5,7},{10,8},{11,9},{8,1... | collective-permute-start | bytes 294920 | tf_op jit(solution)/shard_map/feat_y/ppermute | solution.py:41
  10.7 2.3 %copy-done = bf16[3072,768]{1,0:T(8,128)(2,1)S(1)} copy-done((bf16[3072,768]{1,0:T(8,128)(2,1)S(1)}, bf16[3072,768]{1,0:T(8,128)(2,1)}, u32[]{:S(2)}) %copy-start) | copy-done | bytes 4718616
  17.3 2.9 %collective-permute-start.10 = (bf16[2,16,3072]{2,1,0:T(8,128)(2,1)S(1)}, bf16[2,16,3072]{2,1,0:T(8,128)(2,1)S(1)}, u32[]{:S(2)}, u32[]{:S(2)}) collective-permute-start(bf16[2,16,3072]{2,1,0:T(8,128)(2,1)S(1)} %pad_maximum_fusion.2.refs_0_), channel_id=1, source_target_pairs={{4,0},{5,1},{6,2},{7,3},{8,4},{9,5},{10,6},{11,7},{12,8},{13,9},{1... | collective-permute-start | bytes 589832 | tf_op jit(solution)/shard_map/cot_z/ppermute | solution.py:41
  20.2 1.5 %collective-permute-start.4 = (bf16[4,4,3072]{2,1,0:T(4,128)(2,1)S(1)}, bf16[4,4,3072]{2,1,0:T(4,128)(2,1)S(1)}, u32[]{:S(2)}, u32[]{:S(2)}) collective-permute-start(bf16[4,4,3072]{2,1,0:T(4,128)(2,1)S(1)} %collective-permute-done.refs_1_), channel_id=1, source_target_pairs={{2,0},{3,1},{0,2},{1,3},{6,4},{7,5},{4,6},{5,7},{10,8},{11,9},{8,1... | collective-permute-start | bytes 294920 | tf_op jit(solution)/shard_map/feat_y/ppermute | solution.py:41
  24.1 1.5 %collective-permute-done.4.refs_5_ = bf16[4,4,3072]{2,1,0:T(4,128)(2,1)S(1)} collective-permute-done((bf16[4,4,3072]{2,1,0:T(4,128)(2,1)S(1)}, bf16[4,4,3072]{2,1,0:T(4,128)(2,1)S(1)}, u32[]{:S(2)}, u32[]{:S(2)}) %collective-permute-start.4) | collective-permute-done | bytes 98336 | tf_op jit(solution)/shard_map/feat_y/ppermute | solution.py:41
  28.2 3.5 %collective-permute-done.11.refs_3_ = bf16[2,16,3072]{2,1,0:T(8,128)(2,1)S(1)} collective-permute-done((bf16[2,16,3072]{2,1,0:T(8,128)(2,1)S(1)}, bf16[2,16,3072]{2,1,0:T(8,128)(2,1)S(1)}, u32[]{:S(2)}, u32[]{:S(2)}) %collective-permute-start.11) | collective-permute-done | bytes 196640 | tf_op jit(solution)/shard_map/cot_z/ppermute | solution.py:41
  32.4 2.6 %shard_map.162 = (f32[12,4,48,128]{3,2,1,0:T(8,128)S(1)}, f32[12,128,128]{2,1,0:T(8,128)S(1)}, f32[128,128]{1,0:T(8,128)S(1)}) custom-call(s32[3]{0:T(128)S(1)} %pad_add_fusion.idx, bf16[4,4,3072]{2,1,0:T(4,128)(2,1)S(1)} %get-tuple-element.70.refs_0_, bf16[4,4,3072]{2,1,0:T(4,128)(2,1)S(1)} %collective-permute-done.refs_1_, ...), custom_call_target="tpu_custom_call" | custom-call | flops 8800000000 | bytes 27200000 | tf_op jit(solution)/shard_map/pallas_call | solution.py:579
  35.1 3.5 %shard_map.163 = (bf16[128,3072]{1,0:T(8,128)(2,1)S(1)}, f32[3,4,48,128]{3,2,1,0:T(8,128)S(1)}, f32[3,128,128]{2,1,0:T(8,128)S(1)}, f32[128,128]{1,0:T(8,128)S(1)}) custom-call(s32[3]{0:T(128)S(1)} %pad_add_fusion.idx, bf16[4,4,3072]{2,1,0:T(4,128)(2,1)S(1)} %get-tuple-element.70.refs_0_, bf16[4,4,3072]{2,1,0:T(4,128)(2,1)S(1)} %collective-permute-done.refs_1_, ...), custom_call_target="tpu_custom_call" | custom-call | flops 8800000000 | bytes 27200000 | tf_op jit(solution)/shard_map/pallas_call | solution.py:579
  44.5 1.7 %shard_map.166 = (bf16[128,768]{1,0:T(8,128)(2,1)S(1)}, bf16[128,768]{1,0:T(8,128)(2,1)S(1)}, f32[1,768]{1,0:T(1,128)S(1)}, f32[16,128]{1,0:T(8,128)S(1)}) custom-call(bf16[128,3072]{1,0:T(8,128)(2,1)S(1)} %get-tuple-element.119.normed.left_own, bf16[3072,768]{1,0:T(8,128)(2,1)S(1)} %bitcast.64, f32[1,768]{1,0:T(1,128)S(1)} %reshape.90.up_bias, ...), custom_call_target="tpu_custom_call" | custom-call | flops 1870000000 | bytes 5780000 | tf_op jit(solution)/shard_map/pallas_call | solution.py:579
  46.2 1.7 %shard_map.167 = (bf16[128,768]{1,0:T(8,128)(2,1)S(1)}, bf16[128,768]{1,0:T(8,128)(2,1)S(1)}, f32[1,768]{1,0:T(1,128)S(1)}, f32[16,128]{1,0:T(8,128)S(1)}) custom-call(bf16[128,3072]{1,0:T(8,128)(2,1)S(1)} %collective-permute-done.17.normed.left_other, bf16[3072,768]{1,0:T(8,128)(2,1)S(1)} %bitcast.64, f32[1,768]{1,0:T(1,128)S(1)} %reshape.90.up_bias, ...), custom_call_target="tpu_custom_call" | custom-call | flops 1870000000 | bytes 5780000 | tf_op jit(solution)/shard_map/pallas_call | solution.py:579
  47.9 1.6 %shard_map.171 = (f32[2,2,144,384]{3,2,1,0:T(8,128)S(1)}, bf16[2,2,144,384]{3,2,1,0:T(8,128)(2,1)S(1)}) custom-call(s32[3]{0:T(128)S(1)} %pad_add_fusion.idx, bf16[128,768]{1,0:T(8,128)(2,1)S(1)} %get-tuple-element.88.act_own.right_own, bf16[128,768]{1,0:T(8,128)(2,1)S(1)} %get-tuple-element.89.act_other.right_other, bf16[3072,768]{1,0:T(8,128)(2,1)S(1)} %bitcast.64, ...), custom_call_target="tpu_custom_call" | custom-call | flops 1760000000 | bytes 5440000 | tf_op jit(solution)/shard_map/pallas_call | solution.py:579
  49.6 1.5 %shard_map.168 = (f32[2,2,144,384]{3,2,1,0:T(8,128)S(1)}, bf16[2,2,144,384]{3,2,1,0:T(8,128)(2,1)S(1)}) custom-call(s32[3]{0:T(128)S(1)} %pad_add_fusion.idx, bf16[128,768]{1,0:T(8,128)(2,1)S(1)} %get-tuple-element.88.act_own.right_own, bf16[128,768]{1,0:T(8,128)(2,1)S(1)} %get-tuple-element.89.act_other.right_other, bf16[3072,768]{1,0:T(8,128)(2,1)S(1)} %bitcast.64, ...), custom_call_target="tpu_custom_call" | custom-call | flops 1760000000 | bytes 5440000 | tf_op jit(solution)/shard_map/pallas_call | solution.py:579
  51.7 1.6 %collective-permute-start.23 = (bf16[144,384]{1,0:T(8,128)(2,1)S(1)}, bf16[144,384]{1,0:T(8,128)(2,1)S(1)}, u32[]{:S(2)}, u32[]{:S(2)}) collective-permute-start(bf16[144,384]{1,0:T(8,128)(2,1)S(1)} %get-tuple-element.137), channel_id=1, source_target_pairs={{2,0},{3,1},{0,2},{1,3},{6,4},{7,5},{4,6},{5,7},{10,8},{11,9},{8,1... | collective-permute-start | bytes 331784 | tf_op jit(solution)/shard_map/ppermute | solution.py:41
  53.8 3.1 %shard_map.169.rest_0_ = f32[768,3072]{1,0:T(8,128)} custom-call(bf16[128,768]{1,0:T(8,128)(2,1)S(1)} %get-tuple-element.96.left_own, bf16[128,768]{1,0:T(8,128)(2,1)S(1)} %get-tuple-element.97.left_other, bf16[256,3072]{1,0:T(8,128)(2,1)S(1)} %get-tuple-element.83.cot_all.right_own.right_other, ...), custom_call_target="tpu_custom_call" | custom-call | flops 2750000128 | bytes 8500000 | tf_op jit(solution)/shard_map/pallas_call | solution.py:604
  57.1 1.6 %collective-permute-start.20 = (bf16[144,384]{1,0:T(8,128)(2,1)S(1)}, bf16[144,384]{1,0:T(8,128)(2,1)S(1)}, u32[]{:S(2)}, u32[]{:S(2)}) collective-permute-start(bf16[144,384]{1,0:T(8,128)(2,1)S(1)} %get-tuple-element.132), channel_id=1, source_target_pairs={{2,0},{3,1},{0,2},{1,3},{6,4},{7,5},{4,6},{5,7},{10,8},{11,9},{8,1... | collective-permute-start | bytes 331784 | tf_op jit(solution)/shard_map/ppermute | solution.py:41
  59.4 4.4 %collective-permute-start.26 = (bf16[144,384]{1,0:T(8,128)(2,1)S(1)}, bf16[144,384]{1,0:T(8,128)(2,1)S(1)}, u32[]{:S(2)}, u32[]{:S(2)}) collective-permute-start(bf16[144,384]{1,0:T(8,128)(2,1)S(1)} %get-tuple-element.134), channel_id=1, source_target_pairs={{0,12},{1,13},{2,14},{3,15},{4,0},{5,1},{6,2},{7,3},{8,4},{9,5},{1... | collective-permute-start | bytes 331784 | tf_op jit(solution)/shard_map/ppermute | solution.py:41
  65.2 3.1 %shard_map.170 = f32[768,3072]{1,0:T(8,128)} custom-call(bf16[128,768]{1,0:T(8,128)(2,1)S(1)} %get-tuple-element.96.left_own, bf16[128,768]{1,0:T(8,128)(2,1)S(1)} %get-tuple-element.97.left_other, bf16[256,3072]{1,0:T(8,128)(2,1)S(1)} %get-tuple-element.83.cot_all.right_own.right_other, ...), custom_call_target="tpu_custom_call", output_to_operand_aliasing={{}: (4, {})} | custom-call | flops 2750000128 | bytes 8500000 | tf_op jit(solution)/shard_map/pallas_call | solution.py:604
  69.1 1.7 %collective-permute-done.21.near_1 = bf16[144,384]{1,0:T(8,128)(2,1)S(1)} collective-permute-done((bf16[144,384]{1,0:T(8,128)(2,1)S(1)}, bf16[144,384]{1,0:T(8,128)(2,1)S(1)}, u32[]{:S(2)}, u32[]{:S(2)}) %collective-permute-start.21) | collective-permute-done | bytes 110624 | tf_op jit(solution)/shard_map/ppermute | solution.py:41
  70.9 2.0 %shard_map.172 = (bf16[4,16,384]{2,1,0:T(8,128)(2,1)S(1)}, bf16[6,16,384]{2,1,0:T(8,128)(2,1)S(1)}, f32[2,16,384]{2,1,0:T(8,128)S(1)}) custom-call(s32[3]{0:T(128)S(1)} %pad_add_fusion.idx, f32[144,384]{1,0:T(8,128)S(1)} %fusion.10.own, bf16[144,384]{1,0:T(8,128)(2,1)S(1)} %collective-permute-done.21.near_1, ...), custom_call_target="tpu_custom_call" | custom-call | flops 2420000000 | bytes 7480000 | tf_op jit(solution)/shard_map/pallas_call | solution.py:579
  74.8 1.8 %collective-permute-start.30 = (bf16[4,16,384]{2,1,0:T(8,128)(2,1)S(1)}, bf16[4,16,384]{2,1,0:T(8,128)(2,1)S(1)}, u32[]{:S(2)}, u32[]{:S(2)}) collective-permute-start(bf16[4,16,384]{2,1,0:T(8,128)(2,1)S(1)} %get-tuple-element.112), channel_id=1, source_target_pairs={{0,12},{1,13},{2,14},{3,15},{4,0},{5,1},{6,2},{7,3},{8,4},{9,5},{1... | collective-permute-start | bytes 147464 | tf_op jit(solution)/shard_map/ppermute | solution.py:41
  78.9 3.2 %shard_map.174.rest_0_ = f32[3072,768]{1,0:T(8,128)} custom-call(bf16[128,3072]{1,0:T(8,128)(2,1)S(1)} %get-tuple-element.119.normed.left_own, bf16[128,3072]{1,0:T(8,128)(2,1)S(1)} %collective-permute-done.17.normed.left_other, bf16[128,768]{1,0:T(8,128)(2,1)S(1)} %get-tuple-element.88.act_own.right_own, ...), custom_call_target="tpu_custom_call" | custom-call | flops 2750000128 | bytes 8500000 | tf_op jit(solution)/shard_map/pallas_call | solution.py:604
  84.9 3.2 %shard_map.175 = f32[3072,768]{1,0:T(8,128)} custom-call(bf16[128,3072]{1,0:T(8,128)(2,1)S(1)} %get-tuple-element.119.normed.left_own, bf16[128,3072]{1,0:T(8,128)(2,1)S(1)} %collective-permute-done.17.normed.left_other, bf16[128,768]{1,0:T(8,128)(2,1)S(1)} %get-tuple-element.88.act_own.right_own, ...), custom_call_target="tpu_custom_call", output_to_operand_aliasing={{}: (4, {})} | custom-call | flops 2750000128 | bytes 8500000 | tf_op jit(solution)/shard_map/pallas_call | solution.py:604
  88.1 1.9 %collective-permute-done.31.refs_4_ = bf16[4,3,16,384]{3,2,1,0:T(8,128)(2,1)S(1)} collective-permute-done((bf16[4,3,16,384]{3,2,1,0:T(8,128)(2,1)S(1)}, bf16[4,3,16,384]{3,2,1,0:T(8,128)(2,1)S(1)}, u32[]{:S(2)}, u32[]{:S(2)}) %collective-permute-start.31) | collective-permute-done | bytes 147488 | tf_op jit(solution)/shard_map/ppermute | solution.py:41
  (116 shorter events, 33.3 us)
Async XLA Ops:
  0.6 16.6 %collective-permute-start = (bf16[4,4,3072]{2,1,0:T(4,128)(2,1)}, bf16[4,4,3072]{2,1,0:T(4,128)(2,1)S(1)}, u32[]{:S(2)}, u32[]{:S(2)}) collective-permute-start(bf16[4,4,3072]{2,1,0:T(4,128)(2,1)} %shard.1), channel_id=1, source_target_pairs={{4,0},{5,1},{6,2},{7,3},{8,4},{9,5},{10,6},{11,7},{12,8},{13,9},{1... | collective-permute-start | bytes 294920 | tf_op jit(solution)/shard_map/feat_z/ppermute | solution.py:41
  5.7 11.5 %collective-permute-start.1 = (bf16[4,4,3072]{2,1,0:T(4,128)(2,1)}, bf16[4,4,3072]{2,1,0:T(4,128)(2,1)S(1)}, u32[]{:S(2)}, u32[]{:S(2)}) collective-permute-start(bf16[4,4,3072]{2,1,0:T(4,128)(2,1)} %shard.1), channel_id=1, source_target_pairs={{8,0},{9,1},{10,2},{11,3},{12,4},{13,5},{14,6},{15,7},{0,8},{1,9},... | collective-permute-start | bytes 294920 | tf_op jit(solution)/shard_map/feat_z/ppermute | solution.py:41
  5.7 11.6 %collective-permute-start.2 = (bf16[4,4,3072]{2,1,0:T(4,128)(2,1)}, bf16[4,4,3072]{2,1,0:T(4,128)(2,1)S(1)}, u32[]{:S(2)}, u32[]{:S(2)}) collective-permute-start(bf16[4,4,3072]{2,1,0:T(4,128)(2,1)} %shard.1), channel_id=1, source_target_pairs={{12,0},{13,1},{14,2},{15,3},{0,4},{1,5},{2,6},{3,7},{4,8},{5,9},{6... | collective-permute-start | bytes 294920 | tf_op jit(solution)/shard_map/feat_z/ppermute | solution.py:41
  6.7 17.2 %collective-permute-start.3 = (bf16[4,4,3072]{2,1,0:T(4,128)(2,1)}, bf16[4,4,3072]{2,1,0:T(4,128)(2,1)S(1)}, u32[]{:S(2)}, u32[]{:S(2)}) collective-permute-start(bf16[4,4,3072]{2,1,0:T(4,128)(2,1)} %shard.1), channel_id=1, source_target_pairs={{2,0},{3,1},{0,2},{1,3},{6,4},{7,5},{4,6},{5,7},{10,8},{11,9},{8,1... | collective-permute-start | bytes 294920 | tf_op jit(solution)/shard_map/feat_y/ppermute | solution.py:41
  9.2 8.0 %collective-permute-start.9 = (bf16[16,3072]{1,0:T(8,128)(2,1)S(1)}, bf16[16,3072]{1,0:T(8,128)(2,1)S(1)}, u32[]{:S(2)}, u32[]{:S(2)}) collective-permute-start(bf16[16,3072]{1,0:T(8,128)(2,1)S(1)} %reshape.89), channel_id=1, source_target_pairs={{2,0},{3,1},{0,2},{1,3},{6,4},{7,5},{4,6},{5,7},{10,8},{11,9},{8,1... | collective-permute-start | bytes 294920 | tf_op jit(solution)/shard_map/cot_y/ppermute | solution.py:41
  17.3 10.9 %collective-permute-start.10 = (bf16[2,16,3072]{2,1,0:T(8,128)(2,1)S(1)}, bf16[2,16,3072]{2,1,0:T(8,128)(2,1)S(1)}, u32[]{:S(2)}, u32[]{:S(2)}) collective-permute-start(bf16[2,16,3072]{2,1,0:T(8,128)(2,1)S(1)} %pad_maximum_fusion.2.refs_0_), channel_id=1, source_target_pairs={{4,0},{5,1},{6,2},{7,3},{8,4},{9,5},{10,6},{11,7},{12,8},{13,9},{1... | collective-permute-start | bytes 589832 | tf_op jit(solution)/shard_map/cot_z/ppermute | solution.py:41
  20.2 5.4 %collective-permute-start.4 = (bf16[4,4,3072]{2,1,0:T(4,128)(2,1)S(1)}, bf16[4,4,3072]{2,1,0:T(4,128)(2,1)S(1)}, u32[]{:S(2)}, u32[]{:S(2)}) collective-permute-start(bf16[4,4,3072]{2,1,0:T(4,128)(2,1)S(1)} %collective-permute-done.refs_1_), channel_id=1, source_target_pairs={{2,0},{3,1},{0,2},{1,3},{6,4},{7,5},{4,6},{5,7},{10,8},{11,9},{8,1... | collective-permute-start | bytes 294920 | tf_op jit(solution)/shard_map/feat_y/ppermute | solution.py:41
  21.7 5.0 %collective-permute-start.5 = (bf16[4,4,3072]{2,1,0:T(4,128)(2,1)S(1)}, bf16[4,4,3072]{2,1,0:T(4,128)(2,1)S(1)}, u32[]{:S(2)}, u32[]{:S(2)}) collective-permute-start(bf16[4,4,3072]{2,1,0:T(4,128)(2,1)S(1)} %collective-permute-done.1.refs_2_), channel_id=1, source_target_pairs={{2,0},{3,1},{0,2},{1,3},{6,4},{7,5},{4,6},{5,7},{10,8},{11,9},{8,1... | collective-permute-start | bytes 294920 | tf_op jit(solution)/shard_map/feat_y/ppermute | solution.py:41
  22.2 5.5 %collective-permute-start.6 = (bf16[4,4,3072]{2,1,0:T(4,128)(2,1)S(1)}, bf16[4,4,3072]{2,1,0:T(4,128)(2,1)S(1)}, u32[]{:S(2)}, u32[]{:S(2)}) collective-permute-start(bf16[4,4,3072]{2,1,0:T(4,128)(2,1)S(1)} %collective-permute-done.2.refs_3_), channel_id=1, source_target_pairs={{2,0},{3,1},{0,2},{1,3},{6,4},{7,5},{4,6},{5,7},{10,8},{11,9},{8,1... | collective-permute-start | bytes 294920 | tf_op jit(solution)/shard_map/feat_y/ppermute | solution.py:41
  24.0 7.7 %collective-permute-start.11 = (bf16[2,16,3072]{2,1,0:T(8,128)(2,1)S(1)}, bf16[2,16,3072]{2,1,0:T(8,128)(2,1)S(1)}, u32[]{:S(2)}, u32[]{:S(2)}) collective-permute-start(bf16[2,16,3072]{2,1,0:T(8,128)(2,1)S(1)} %pad_maximum_fusion.2.refs_0_), channel_id=1, source_target_pairs={{12,0},{13,1},{14,2},{15,3},{0,4},{1,5},{2,6},{3,7},{4,8},{5,9},{6... | collective-permute-start | bytes 589832 | tf_op jit(solution)/shard_map/cot_z/ppermute | solution.py:41
  25.6 6.1 %collective-permute-start.7 = (bf16[2,4,4,3072]{3,2,1,0:T(4,128)(2,1)S(1)}, bf16[2,4,4,3072]{3,2,1,0:T(4,128)(2,1)S(1)}, u32[]{:S(2)}, u32[]{:S(2)}) collective-permute-start(bf16[2,4,4,3072]{3,2,1,0:T(4,128)(2,1)S(1)} %pad_maximum_fusion), channel_id=1, source_target_pairs={{1,0},{0,1},{3,2},{2,3},{5,4},{4,5},{7,6},{6,7},{9,8},{8,9},{11,10... | collective-permute-start | bytes 589832 | tf_op jit(solution)/shard_map/feat_core/ppermute | solution.py:41
  31.7 8.0 %collective-permute-start.12 = (bf16[2,16,3072]{2,1,0:T(8,128)(2,1)S(1)}, bf16[2,16,3072]{2,1,0:T(8,128)(2,1)S(1)}, u32[]{:S(2)}, u32[]{:S(2)}) collective-permute-start(bf16[2,16,3072]{2,1,0:T(8,128)(2,1)S(1)} %collective-permute-done.10.refs_1_), channel_id=1, source_target_pairs={{4,0},{5,1},{6,2},{7,3},{8,4},{9,5},{10,6},{11,7},{12,8},{13,9},{1... | collective-permute-start | bytes 589832 | tf_op jit(solution)/shard_map/cot_z/ppermute | solution.py:41
  38.6 7.6 %collective-permute-start.17 = (bf16[128,3072]{1,0:T(8,128)(2,1)S(1)}, bf16[128,3072]{1,0:T(8,128)(2,1)S(1)}, u32[]{:S(2)}, u32[]{:S(2)}) collective-permute-start(bf16[128,3072]{1,0:T(8,128)(2,1)S(1)} %get-tuple-element.119.normed.left_own), channel_id=1, source_target_pairs={{1,0},{0,1},{3,2},{2,3},{5,4},{4,5},{7,6},{6,7},{9,8},{8,9},{11,10... | collective-permute-start | bytes 2359304 | tf_op jit(solution)/shard_map/ppermute | solution.py:41
  51.7 7.5 %collective-permute-start.23 = (bf16[144,384]{1,0:T(8,128)(2,1)S(1)}, bf16[144,384]{1,0:T(8,128)(2,1)S(1)}, u32[]{:S(2)}, u32[]{:S(2)}) collective-permute-start(bf16[144,384]{1,0:T(8,128)(2,1)S(1)} %get-tuple-element.137), channel_id=1, source_target_pairs={{2,0},{3,1},{0,2},{1,3},{6,4},{7,5},{4,6},{5,7},{10,8},{11,9},{8,1... | collective-permute-start | bytes 331784 | tf_op jit(solution)/shard_map/ppermute | solution.py:41
  53.3 5.9 %collective-permute-start.25 = (bf16[144,384]{1,0:T(8,128)(2,1)S(1)}, bf16[144,384]{1,0:T(8,128)(2,1)S(1)}, u32[]{:S(2)}, u32[]{:S(2)}) collective-permute-start(bf16[144,384]{1,0:T(8,128)(2,1)S(1)} %get-tuple-element.136), channel_id=1, source_target_pairs={{2,0},{3,1},{0,2},{1,3},{6,4},{7,5},{4,6},{5,7},{10,8},{11,9},{8,1... | collective-permute-start | bytes 331784 | tf_op jit(solution)/shard_map/ppermute | solution.py:41
  57.1 6.7 %collective-permute-start.20 = (bf16[144,384]{1,0:T(8,128)(2,1)S(1)}, bf16[144,384]{1,0:T(8,128)(2,1)S(1)}, u32[]{:S(2)}, u32[]{:S(2)}) collective-permute-start(bf16[144,384]{1,0:T(8,128)(2,1)S(1)} %get-tuple-element.132), channel_id=1, source_target_pairs={{2,0},{3,1},{0,2},{1,3},{6,4},{7,5},{4,6},{5,7},{10,8},{11,9},{8,1... | collective-permute-start | bytes 331784 | tf_op jit(solution)/shard_map/ppermute | solution.py:41
  58.7 6.5 %collective-permute-start.19 = (bf16[144,384]{1,0:T(8,128)(2,1)S(1)}, bf16[144,384]{1,0:T(8,128)(2,1)S(1)}, u32[]{:S(2)}, u32[]{:S(2)}) collective-permute-start(bf16[144,384]{1,0:T(8,128)(2,1)S(1)} %get-tuple-element.138), channel_id=1, source_target_pairs={{2,0},{3,1},{0,2},{1,3},{6,4},{7,5},{4,6},{5,7},{10,8},{11,9},{8,1... | collective-permute-start | bytes 331784 | tf_op jit(solution)/shard_map/ppermute | solution.py:41
  59.4 9.8 %collective-permute-start.24 = (bf16[144,384]{1,0:T(8,128)(2,1)S(1)}, bf16[144,384]{1,0:T(8,128)(2,1)S(1)}, u32[]{:S(2)}, u32[]{:S(2)}) collective-permute-start(bf16[144,384]{1,0:T(8,128)(2,1)S(1)} %get-tuple-element.135), channel_id=1, source_target_pairs={{0,8},{1,9},{2,10},{3,11},{4,12},{5,13},{6,14},{7,15},{8,0},{9,1},... | collective-permute-start | bytes 331784 | tf_op jit(solution)/shard_map/ppermute | solution.py:41
  59.4 9.7 %collective-permute-start.26 = (bf16[144,384]{1,0:T(8,128)(2,1)S(1)}, bf16[144,384]{1,0:T(8,128)(2,1)S(1)}, u32[]{:S(2)}, u32[]{:S(2)}) collective-permute-start(bf16[144,384]{1,0:T(8,128)(2,1)S(1)} %get-tuple-element.134), channel_id=1, source_target_pairs={{0,12},{1,13},{2,14},{3,15},{4,0},{5,1},{6,2},{7,3},{8,4},{9,5},{1... | collective-permute-start | bytes 331784 | tf_op jit(solution)/shard_map/ppermute | solution.py:41
  63.8 7.0 %collective-permute-start.21 = (bf16[144,384]{1,0:T(8,128)(2,1)S(1)}, bf16[144,384]{1,0:T(8,128)(2,1)S(1)}, u32[]{:S(2)}, u32[]{:S(2)}) collective-permute-start(bf16[144,384]{1,0:T(8,128)(2,1)S(1)} %add_convert_fusion), channel_id=1, source_target_pairs={{0,4},{1,5},{2,6},{3,7},{4,8},{5,9},{6,10},{7,11},{8,12},{9,13},{1... | collective-permute-start | bytes 331784 | tf_op jit(solution)/shard_map/ppermute | solution.py:41
  74.8 4.1 %collective-permute-start.30 = (bf16[4,16,384]{2,1,0:T(8,128)(2,1)S(1)}, bf16[4,16,384]{2,1,0:T(8,128)(2,1)S(1)}, u32[]{:S(2)}, u32[]{:S(2)}) collective-permute-start(bf16[4,16,384]{2,1,0:T(8,128)(2,1)S(1)} %get-tuple-element.112), channel_id=1, source_target_pairs={{0,12},{1,13},{2,14},{3,15},{4,0},{5,1},{6,2},{7,3},{8,4},{9,5},{1... | collective-permute-start | bytes 147464 | tf_op jit(solution)/shard_map/ppermute | solution.py:41
  76.6 5.9 %collective-permute-start.28 = (bf16[4,16,384]{2,1,0:T(8,128)(2,1)S(1)}, bf16[4,16,384]{2,1,0:T(8,128)(2,1)S(1)}, u32[]{:S(2)}, u32[]{:S(2)}) collective-permute-start(bf16[4,16,384]{2,1,0:T(8,128)(2,1)S(1)} %get-tuple-element.110), channel_id=1, source_target_pairs={{0,4},{1,5},{2,6},{3,7},{4,8},{5,9},{6,10},{7,11},{8,12},{9,13},{1... | collective-permute-start | bytes 147464 | tf_op jit(solution)/shard_map/ppermute | solution.py:41
  76.9 6.6 %collective-permute-start.29 = (bf16[4,16,384]{2,1,0:T(8,128)(2,1)S(1)}, bf16[4,16,384]{2,1,0:T(8,128)(2,1)S(1)}, u32[]{:S(2)}, u32[]{:S(2)}) collective-permute-start(bf16[4,16,384]{2,1,0:T(8,128)(2,1)S(1)} %get-tuple-element.111), channel_id=1, source_target_pairs={{0,8},{1,9},{2,10},{3,11},{4,12},{5,13},{6,14},{7,15},{8,0},{9,1},... | collective-permute-start | bytes 147464 | tf_op jit(solution)/shard_map/ppermute | solution.py:41
  83.7 6.3 %collective-permute-start.31 = (bf16[4,3,16,384]{3,2,1,0:T(8,128)(2,1)S(1)}, bf16[4,3,16,384]{3,2,1,0:T(8,128)(2,1)S(1)}, u32[]{:S(2)}, u32[]{:S(2)}) collective-permute-start(bf16[4,3,16,384]{3,2,1,0:T(8,128)(2,1)S(1)} %pad_maximum_fusion.3), channel_id=1, source_target_pairs={{2,0},{3,1},{0,2},{1,3},{6,4},{7,5},{4,6},{5,7},{10,8},{11,9},{8,1... | collective-permute-start | bytes 442376 | tf_op jit(solution)/shard_map/ppermute | solution.py:41
  (25 other events, 85.8 us)

commit v5 on v4

--- a/solution.py
+++ b/solution.py
@@ -401,38 +401,50 @@
     shift_dot[...] = jnp.broadcast_to(product[2:3] + product[3:4], shift_dot.shape)
 
 
-def hid_kernel(cot_all, weight, hid_grad):
-    hid_grad[...] = contract(cot_all[...], weight[...], 1, 1)
-
-
-def act_kernel(
-    half, normed, weight, up_bias, hid_grad, gain_dot, shift_dot,
-    hidden, act_grad, bias_grad, sums,
-):
+def up_kernel(normed, weight, up_bias, shift_dot, hidden, slope, centred):
     tile = 256
-    first = jnp.zeros((128, LANES), F32)
-    second = jnp.zeros((128, LANES), F32)
     for start in range(0, hidden.shape[1], tile):
         at = slice(start, start + tile)
         plain = jnp.dot(normed[...], weight[:, at], preferred_element_type=F32)
         pre_act = plain + up_bias[0:1, at]
         cdf = 0.5 * (1.0 + lax.erf(pre_act * 0.7071067811865476))
         hidden[:, at] = (pre_act * cdf).astype(BF16)
-        slope = cdf + pre_act * jnp.exp(-0.5 * pre_act * pre_act) * 0.3989422804014327
-        act = (hid_grad[128 * half : 128 * half + 128, at] * slope).astype(BF16)
-        act_grad[:, at] = act
-        act = act.astype(F32)
-        bias_grad[0:1, at] = jnp.sum(act, axis=0, keepdims=True)
-        by_gain = act * gain_dot[0:1, at]
-        by_unit = act * (plain - shift_dot[0:1, at])
-        for lane in range(0, tile, LANES):
-            first = first + by_gain[:, lane : lane + LANES]
-            second = second + by_unit[:, lane : lane + LANES]
+        slope[:, at] = cdf + pre_act * jnp.exp(-0.5 * pre_act * pre_act) * 0.3989422804014327
+        centred[:, at] = plain - shift_dot[0:1, at]
+
+
+def act_kernel(
+    cot_all, weight, gain_dot, slope_own, slope_other, centred_own, centred_other,
+    act_own, act_other, bias_grad, sums_own, sums_other,
+):
+    tile = 256
+    halves = (
+        (0, slope_own, centred_own, act_own, sums_own),
+        (128, slope_other, centred_other, act_other, sums_other),
+    )
+    parts = [jnp.zeros((128, LANES), F32) for _ in range(4)]
+    for start in range(0, act_own.shape[1], tile):
+        at = slice(start, start + tile)
+        hid_grad = contract(cot_all[...], weight[at, :], 1, 1)
+        column = jnp.zeros((1, tile), F32)
+        for half, (row, slope, centred, act_grad, _) in enumerate(halves):
+            act = (hid_grad[row : row + 128] * slope[:, at]).astype(BF16)
+            act_grad[:, at] = act
+            act = act.astype(F32)
+            column = column + jnp.sum(act, axis=0, keepdims=True)
+            by_gain = act * gain_dot[0:1, at]
+            by_unit = act * centred[:, at]
+            for lane in range(0, tile, LANES):
+                parts[2 * half] = parts[2 * half] + by_gain[:, lane : lane + LANES]
+                parts[2 * half + 1] = parts[2 * half + 1] + by_unit[:, lane : lane + LANES]
+        bias_grad[0:1, at] = column
     ones = jnp.ones((8, LANES), F32)
-    for row, part in ((0, first), (8, second)):
-        sums[row : row + 8, :] = lax.dot_general(
-            ones, part, (((1,), (1,)), ((), ())), precision=EXACT, preferred_element_type=F32
-        )
+    for half, (_, _, _, _, sums) in enumerate(halves):
+        for which in range(2):
+            sums[8 * which : 8 * which + 8, :] = lax.dot_general(
+                ones, parts[2 * half + which], (((1,), (1,)), ((), ())),
+                precision=EXACT, preferred_element_type=F32,
+            )
 
 
 def norm_grad_kernel(steps, idx, act_own, act_other, weight, sums_own, sums_other, keep, away):
@@ -543,8 +555,8 @@
 
 
 def place_kernel(idx, *refs):
-    msgs, came, core_a, core_b = refs[:4], refs[4], refs[5], refs[6]
-    tokens, kernel_grad, gain_grad, shift_grad, bias_grad = refs[7:]
+    msgs, came, across_core = refs[:4], refs[4], refs[5]
+    tokens, kernel_grad, gain_grad, shift_grad, bias_grad = refs[6:]
     z, y, core = idx[0], idx[1], idx[2]
     for step in range(4):
         plane = (z + 4 - step) % 4
@@ -556,7 +568,7 @@
                 tokens[row, :, lanes] = block[4 * row : 4 * row + 4].astype(BF16)
             for part in range(2):
                 mine = (came[step, 1 + part] if yr else msgs[step][2 + part]).astype(F32)
-                other = (core_b[step, part] if yr else core_a[step, part]).astype(F32)
+                other = across_core[yr, step, part].astype(F32)
                 low = jnp.where(core == 0, mine, other)
                 high = jnp.where(core == 0, other, mine)
                 for sub in range(2):
@@ -704,36 +716,43 @@
     )
     with jax.named_scope("cot_core"):
         cot_came = [send(after(plane, inv_slice), C_PAIRS) for plane in cot_planes]
-    normed_other = send(normed, C_PAIRS)
+    normed_other = send(after(normed, cot_planes[2]), C_PAIRS)
+    half_f32 = shape((128, hidden_dev), F32)
+    half_bf16 = shape((128, hidden_dev), BF16)
+    ups = [
+        call(
+            up_kernel,
+            0.1,
+            12,
+            (half_bf16, half_f32, half_f32),
+            (value, up_weight, up_bias_row, shift_dot),
+            scalars=0,
+        )
+        for value in (normed, normed_other)
+    ]
+    hidden, slope, centred = zip(*ups)
     cot_all, cot_slice = call(
         cot_kernel,
         1.5,
         8,
         (shape((256, channels), BF16), shape((3, 128, LANES), F32)),
-        (idx, *cot_planes, *cot_came, scale_row),
-    )
-    hid_grad = call(
-        hid_kernel, 1.5, 8, shape((256, hidden_dev), F32), (cot_all, down_weight), scalars=0
-    )
-    halves = [
-        call(
-            functools.partial(act_kernel, half),
-            1.7,
-            12,
-            (
-                shape((128, hidden_dev), BF16),
-                shape((128, hidden_dev), BF16),
-                shape((1, hidden_dev), F32),
-                shape((16, LANES), F32),
-            ),
-            (value, up_weight, up_bias_row, hid_grad, gain_dot, shift_dot),
-            scalars=0,
-        )
-        for half, value in enumerate((normed, normed_other))
-    ]
-    hidden = [part[0] for part in halves]
-    act_grad = [part[1] for part in halves]
-    sums = [part[3] for part in halves]
+        (after(idx, slope), *cot_planes, *cot_came, scale_row),
+    )
+    act_own, act_other, up_bias_grad, *sums = call(
+        act_kernel,
+        2.2,
+        12,
+        (
+            half_bf16,
+            half_bf16,
+            shape((1, hidden_dev), F32),
+            shape((16, LANES), F32),
+            shape((16, LANES), F32),
+        ),
+        (cot_all, down_weight, gain_dot, *slope, *centred),
+        scalars=0,
+    )
+    act_grad = (act_own, act_other)
 
     arrived, came_at, keep_at, across_at = {}, {}, {}, {}
     for pair in ((2, 3), (1, 0)):
@@ -749,7 +768,7 @@
             came_at[step], keep_at[step] = came[at].astype(F32), keep[at]
             across_at[step] = send((keep[at, 1] + came_at[step][1]).astype(BF16), Y_PAIRS)
     cots = (cot_all, cot_all)
-    down_low = half_gradient(0, after(tuple(hidden), came), cots, 128)
+    down_low = half_gradient(0, after(hidden, came), cots, 128)
     for step in (2, 3, 1, 0):
         total = keep_at[step][0] + came_at[step][0]
         if step == 1:
@@ -758,7 +777,7 @@
         if step:
             total = send(total.astype(BF16), flipped(z_pairs(step)))
         arrived[step] = total
-    down_grad = half_gradient(1, after(tuple(hidden), across_at[0]), cots, 128, down_low)
+    down_grad = half_gradient(1, after(hidden, across_at[0]), cots, 128, down_low)
     late_idx, down_grad = lax.optimization_barrier((idx, down_grad))
     ig_keep, core_msg, small_keep = call(
         conv_back_kernel,
@@ -788,22 +807,22 @@
     up_low = half_gradient(0, after((normed, normed_other), msgs[3]), act_grad, 512)
     msgs, up_low = lax.optimization_barrier((msgs, up_low))
     came = send(jnp.stack([msg[1:4] for msg in msgs]), Y_PAIRS)
-    core_a = send(jnp.stack([msg[2:4] for msg in msgs]), C_PAIRS)
-    up_grad = half_gradient(1, after((normed, normed_other), core_a), act_grad, 512, up_low)
-    late, up_grad = lax.optimization_barrier((came[:, 1:3], up_grad))
-    core_b = send(late, C_PAIRS)
+    up_grad = half_gradient(1, after((normed, normed_other), msgs[1]), act_grad, 512, up_low)
+    near = jnp.stack([msg[2:4] for msg in msgs])
+    both, up_grad = lax.optimization_barrier((jnp.stack([near, came[:, 1:3]]), up_grad))
+    across_core = send(both, C_PAIRS)
     row = shape((1, channels), F32)
     tokens, kernel_grad, gain_grad, shift_grad, depth_bias_grad = call(
         place_kernel,
         0.8,
         8,
         (shape((4, 4, channels), BF16), shape((7, 7, channels), F32), row, row, row),
-        (idx, *msgs, came, core_a, core_b),
+        (idx, *msgs, came, across_core),
     )
     return (
         tokens,
         up_grad,
-        (halves[0][2] + halves[1][2]).reshape(hidden_dev),
+        up_bias_grad.reshape(hidden_dev),
         down_grad,
         kernel_grad,
         depth_bias_grad.reshape(channels),

time: 93.3 us -> 90.2 us (0.967)
  waiting for transfers between devices: 18.5 us -> 15.6 us
    ppermute x34 -> x33, waiting for transfers between devices: 18.5 us -> 15.6 us  [send(): return lax.ppermute(value, 'rows', pairs)]
    ppermute x34 -> x33, starting transfers between devices: 31 us -> 30.9 us  [send(): return lax.ppermute(value, 'rows', pairs)]
  transfers between devices with their start and end apart: 34 -> 33, of which waited for: 18 -> 15; matrix products, arithmetic and copies ran while one was open for 4% -> 4% of each run, Pallas kernels for 27% -> 25%
where the time goes in v5:
time: 90.2 us; the launch traced here: 89.8 us
  Pallas kernels  32.2 us (36%)
  starting transfers between devices  30.9 us (34%)
  waiting for transfers between devices  15.6 us (17%)
  local copies, waits for them, and re-layouts  8.37 us (9%)
  other arithmetic  1.73 us (2%)
  between operations  1.08 us (1%)
    ppermute x33, starting transfers between devices, send(): return lax.ppermute(value, 'rows', pairs)  30.9 us
    pallas_call x12, Pallas kernels, call(): pl.pallas_call(kernel, out_shape=out_shape, in_specs=[SSPEC] * scalars +...  19.6 us
    ppermute x33, waiting for transfers between devices, send(): return lax.ppermute(value, 'rows', pairs)  15.6 us
    pallas_call x4, Pallas kernels, half_gradient(): pl.pallas_call(grad_kernel, grid=(steps,), out_shape=shape((rows, cols),...  12.6 us
    unnamed x30, local copies, waits for them, and re-layouts  6.49 us
  transfers between devices with their start and end apart: 33, of which 15 were waited for; matrix products, arithmetic and copies ran while one was open for 4% of the time, Pallas kernels for 25%

profile of v5, /device:TPU:0, one launch (start us, length us, event | category | flops | bytes accessed | tf_op | source)
XLA Modules:
  0.0 89.8 jit_solution(2201722484448265664)
XLA Ops:
  0.6 5.1 %collective-permute-start = (bf16[4,4,3072]{2,1,0:T(4,128)(2,1)}, bf16[4,4,3072]{2,1,0:T(4,128)(2,1)S(1)}, u32[]{:S(2)}, u32[]{:S(2)}) collective-permute-start(bf16[4,4,3072]{2,1,0:T(4,128)(2,1)} %shard.1), channel_id=1, source_target_pairs={{4,0},{5,1},{6,2},{7,3},{8,4},{9,5},{10,6},{11,7},{12,8},{13,9},{1... | collective-permute-start | bytes 294920 | tf_op jit(solution)/shard_map/feat_z/ppermute | solution.py:41
  6.7 1.5 %collective-permute-start.3 = (bf16[4,4,3072]{2,1,0:T(4,128)(2,1)}, bf16[4,4,3072]{2,1,0:T(4,128)(2,1)S(1)}, u32[]{:S(2)}, u32[]{:S(2)}) collective-permute-start(bf16[4,4,3072]{2,1,0:T(4,128)(2,1)} %shard.1), channel_id=1, source_target_pairs={{2,0},{3,1},{0,2},{1,3},{6,4},{7,5},{4,6},{5,7},{10,8},{11,9},{8,1... | collective-permute-start | bytes 294920 | tf_op jit(solution)/shard_map/feat_y/ppermute | solution.py:41
  10.7 2.3 %copy-done = bf16[3072,768]{1,0:T(8,128)(2,1)S(1)} copy-done((bf16[3072,768]{1,0:T(8,128)(2,1)S(1)}, bf16[3072,768]{1,0:T(8,128)(2,1)}, u32[]{:S(2)}) %copy-start) | copy-done | bytes 4718616
  17.3 2.9 %collective-permute-start.10 = (bf16[2,16,3072]{2,1,0:T(8,128)(2,1)S(1)}, bf16[2,16,3072]{2,1,0:T(8,128)(2,1)S(1)}, u32[]{:S(2)}, u32[]{:S(2)}) collective-permute-start(bf16[2,16,3072]{2,1,0:T(8,128)(2,1)S(1)} %pad_maximum_fusion.2.refs_0_), channel_id=1, source_target_pairs={{4,0},{5,1},{6,2},{7,3},{8,4},{9,5},{10,6},{11,7},{12,8},{13,9},{1... | collective-permute-start | bytes 589832 | tf_op jit(solution)/shard_map/cot_z/ppermute | solution.py:41
  20.2 1.5 %collective-permute-start.4 = (bf16[4,4,3072]{2,1,0:T(4,128)(2,1)S(1)}, bf16[4,4,3072]{2,1,0:T(4,128)(2,1)S(1)}, u32[]{:S(2)}, u32[]{:S(2)}) collective-permute-start(bf16[4,4,3072]{2,1,0:T(4,128)(2,1)S(1)} %collective-permute-done.refs_1_), channel_id=1, source_target_pairs={{2,0},{3,1},{0,2},{1,3},{6,4},{7,5},{4,6},{5,7},{10,8},{11,9},{8,1... | collective-permute-start | bytes 294920 | tf_op jit(solution)/shard_map/feat_y/ppermute | solution.py:41
  22.2 1.5 %collective-permute-start.6 = (bf16[4,4,3072]{2,1,0:T(4,128)(2,1)S(1)}, bf16[4,4,3072]{2,1,0:T(4,128)(2,1)S(1)}, u32[]{:S(2)}, u32[]{:S(2)}) collective-permute-start(bf16[4,4,3072]{2,1,0:T(4,128)(2,1)S(1)} %collective-permute-done.2.refs_3_), channel_id=1, source_target_pairs={{2,0},{3,1},{0,2},{1,3},{6,4},{7,5},{4,6},{5,7},{10,8},{11,9},{8,1... | collective-permute-start | bytes 294920 | tf_op jit(solution)/shard_map/feat_y/ppermute | solution.py:41
  24.1 1.5 %collective-permute-done.4.refs_5_ = bf16[4,4,3072]{2,1,0:T(4,128)(2,1)S(1)} collective-permute-done((bf16[4,4,3072]{2,1,0:T(4,128)(2,1)S(1)}, bf16[4,4,3072]{2,1,0:T(4,128)(2,1)S(1)}, u32[]{:S(2)}, u32[]{:S(2)}) %collective-permute-start.4) | collective-permute-done | bytes 98336 | tf_op jit(solution)/shard_map/feat_y/ppermute | solution.py:41
  28.2 3.5 %collective-permute-done.11.refs_3_ = bf16[2,16,3072]{2,1,0:T(8,128)(2,1)S(1)} collective-permute-done((bf16[2,16,3072]{2,1,0:T(8,128)(2,1)S(1)}, bf16[2,16,3072]{2,1,0:T(8,128)(2,1)S(1)}, u32[]{:S(2)}, u32[]{:S(2)}) %collective-permute-start.11) | collective-permute-done | bytes 196640 | tf_op jit(solution)/shard_map/cot_z/ppermute | solution.py:41
  32.4 2.6 %shard_map.162 = (f32[12,4,48,128]{3,2,1,0:T(8,128)S(1)}, f32[12,128,128]{2,1,0:T(8,128)S(1)}, f32[128,128]{1,0:T(8,128)S(1)}) custom-call(s32[3]{0:T(128)S(1)} %pad_add_fusion.idx, bf16[4,4,3072]{2,1,0:T(4,128)(2,1)S(1)} %get-tuple-element.75.refs_0_, bf16[4,4,3072]{2,1,0:T(4,128)(2,1)S(1)} %collective-permute-done.refs_1_, ...), custom_call_target="tpu_custom_call" | custom-call | flops 8800000000 | bytes 27200000 | tf_op jit(solution)/shard_map/pallas_call | solution.py:591
  35.1 3.4 %shard_map.163 = (bf16[128,3072]{1,0:T(8,128)(2,1)S(1)}, f32[3,4,48,128]{3,2,1,0:T(8,128)S(1)}, f32[3,128,128]{2,1,0:T(8,128)S(1)}, f32[128,128]{1,0:T(8,128)S(1)}) custom-call(s32[3]{0:T(128)S(1)} %pad_add_fusion.idx, bf16[4,4,3072]{2,1,0:T(4,128)(2,1)S(1)} %get-tuple-element.75.refs_0_, bf16[4,4,3072]{2,1,0:T(4,128)(2,1)S(1)} %collective-permute-done.refs_1_, ...), custom_call_target="tpu_custom_call" | custom-call | flops 8800000000 | bytes 27200000 | tf_op jit(solution)/shard_map/pallas_call | solution.py:591
  43.0 2.8 %shard_map.167 = (bf16[128,768]{1,0:T(8,128)(2,1)S(1)}, bf16[128,768]{1,0:T(8,128)(2,1)S(1)}, f32[1,768]{1,0:T(1,128)S(1)}, f32[16,128]{1,0:T(8,128)S(1)}, f32[16,128]{1,0:T(8,128)S(1)}) custom-call(bf16[256,3072]{1,0:T(8,128)(2,1)S(1)} %get-tuple-element.95.cot_all.right_own.right_other, bf16[768,3072]{1,0:T(8,128)(2,1)S(1)} %bitcast.68, ...), custom_call_target="tpu_custom_call" | custom-call | flops 2420000000 | bytes 7480000 | tf_op jit(solution)/shard_map/pallas_call | solution.py:591
  45.8 1.6 %shard_map.171 = (f32[2,2,144,384]{3,2,1,0:T(8,128)S(1)}, bf16[2,2,144,384]{3,2,1,0:T(8,128)(2,1)S(1)}) custom-call(s32[3]{0:T(128)S(1)} %pad_add_fusion.idx, bf16[128,768]{1,0:T(8,128)(2,1)S(1)} %get-tuple-element.99.act_own.right_own, bf16[128,768]{1,0:T(8,128)(2,1)S(1)} %get-tuple-element.100.act_other.right_other, bf16[3072,768]{1,0:T(8,128)(2,1)S(1)} %bitcast.66, ...), custom_call_target="tpu_custom_call" | custom-call | flops 1760000000 | bytes 5440000 | tf_op jit(solution)/shard_map/pallas_call | solution.py:591
  47.6 1.5 %shard_map.168 = (f32[2,2,144,384]{3,2,1,0:T(8,128)S(1)}, bf16[2,2,144,384]{3,2,1,0:T(8,128)(2,1)S(1)}) custom-call(s32[3]{0:T(128)S(1)} %pad_add_fusion.idx, bf16[128,768]{1,0:T(8,128)(2,1)S(1)} %get-tuple-element.99.act_own.right_own, bf16[128,768]{1,0:T(8,128)(2,1)S(1)} %get-tuple-element.100.act_other.right_other, bf16[3072,768]{1,0:T(8,128)(2,1)S(1)} %bitcast.66, ...), custom_call_target="tpu_custom_call" | custom-call | flops 1760000000 | bytes 5440000 | tf_op jit(solution)/shard_map/pallas_call | solution.py:591
  49.7 1.6 %collective-permute-start.23 = (bf16[144,384]{1,0:T(8,128)(2,1)S(1)}, bf16[144,384]{1,0:T(8,128)(2,1)S(1)}, u32[]{:S(2)}, u32[]{:S(2)}) collective-permute-start(bf16[144,384]{1,0:T(8,128)(2,1)S(1)} %get-tuple-element.147), channel_id=1, source_target_pairs={{2,0},{3,1},{0,2},{1,3},{6,4},{7,5},{4,6},{5,7},{10,8},{11,9},{8,1... | collective-permute-start | bytes 331784 | tf_op jit(solution)/shard_map/ppermute | solution.py:41
  51.8 3.1 %shard_map.169.rest_0_ = f32[768,3072]{1,0:T(8,128)} custom-call(bf16[128,768]{1,0:T(8,128)(2,1)S(1)} %get-tuple-element.107.left_own, bf16[128,768]{1,0:T(8,128)(2,1)S(1)} %get-tuple-element.108.left_other, bf16[256,3072]{1,0:T(8,128)(2,1)S(1)} %get-tuple-element.95.cot_all.right_own.right_other, ...), custom_call_target="tpu_custom_call" | custom-call | flops 2750000128 | bytes 8500000 | tf_op jit(solution)/shard_map/pallas_call | solution.py:616
  55.0 1.6 %collective-permute-start.20 = (bf16[144,384]{1,0:T(8,128)(2,1)S(1)}, bf16[144,384]{1,0:T(8,128)(2,1)S(1)}, u32[]{:S(2)}, u32[]{:S(2)}) collective-permute-start(bf16[144,384]{1,0:T(8,128)(2,1)S(1)} %get-tuple-element.142), channel_id=1, source_target_pairs={{2,0},{3,1},{0,2},{1,3},{6,4},{7,5},{4,6},{5,7},{10,8},{11,9},{8,1... | collective-permute-start | bytes 331784 | tf_op jit(solution)/shard_map/ppermute | solution.py:41
  57.4 4.4 %collective-permute-start.26 = (bf16[144,384]{1,0:T(8,128)(2,1)S(1)}, bf16[144,384]{1,0:T(8,128)(2,1)S(1)}, u32[]{:S(2)}, u32[]{:S(2)}) collective-permute-start(bf16[144,384]{1,0:T(8,128)(2,1)S(1)} %get-tuple-element.144), channel_id=1, source_target_pairs={{0,12},{1,13},{2,14},{3,15},{4,0},{5,1},{6,2},{7,3},{8,4},{9,5},{1... | collective-permute-start | bytes 331784 | tf_op jit(solution)/shard_map/ppermute | solution.py:41
  63.1 3.1 %shard_map.170 = f32[768,3072]{1,0:T(8,128)} custom-call(bf16[128,768]{1,0:T(8,128)(2,1)S(1)} %get-tuple-element.107.left_own, bf16[128,768]{1,0:T(8,128)(2,1)S(1)} %get-tuple-element.108.left_other, bf16[256,3072]{1,0:T(8,128)(2,1)S(1)} %get-tuple-element.95.cot_all.right_own.right_other, ...), custom_call_target="tpu_custom_call", output_to_operand_aliasing={{}: (4, {})} | custom-call | flops 2750000128 | bytes 8500000 | tf_op jit(solution)/shard_map/pallas_call | solution.py:616
  67.1 1.8 %collective-permute-done.21.near_1 = bf16[144,384]{1,0:T(8,128)(2,1)S(1)} collective-permute-done((bf16[144,384]{1,0:T(8,128)(2,1)S(1)}, bf16[144,384]{1,0:T(8,128)(2,1)S(1)}, u32[]{:S(2)}, u32[]{:S(2)}) %collective-permute-start.21) | collective-permute-done | bytes 110624 | tf_op jit(solution)/shard_map/ppermute | solution.py:41
  68.8 2.0 %shard_map.172 = (bf16[4,16,384]{2,1,0:T(8,128)(2,1)S(1)}, bf16[6,16,384]{2,1,0:T(8,128)(2,1)S(1)}, f32[2,16,384]{2,1,0:T(8,128)S(1)}) custom-call(s32[3]{0:T(128)S(1)} %pad_add_fusion.idx, f32[144,384]{1,0:T(8,128)S(1)} %fusion.10.own, bf16[144,384]{1,0:T(8,128)(2,1)S(1)} %collective-permute-done.21.near_1, ...), custom_call_target="tpu_custom_call" | custom-call | flops 2420000000 | bytes 7480000 | tf_op jit(solution)/shard_map/pallas_call | solution.py:591
  72.8 1.8 %collective-permute-start.30 = (bf16[4,16,384]{2,1,0:T(8,128)(2,1)S(1)}, bf16[4,16,384]{2,1,0:T(8,128)(2,1)S(1)}, u32[]{:S(2)}, u32[]{:S(2)}) collective-permute-start(bf16[4,16,384]{2,1,0:T(8,128)(2,1)S(1)} %get-tuple-element.123), channel_id=1, source_target_pairs={{0,12},{1,13},{2,14},{3,15},{4,0},{5,1},{6,2},{7,3},{8,4},{9,5},{1... | collective-permute-start | bytes 147464 | tf_op jit(solution)/shard_map/ppermute | solution.py:41
  76.9 3.2 %shard_map.174.rest_0_ = f32[3072,768]{1,0:T(8,128)} custom-call(bf16[128,3072]{1,0:T(8,128)(2,1)S(1)} %get-tuple-element.130.normed.left_own, bf16[128,3072]{1,0:T(8,128)(2,1)S(1)} %collective-permute-done.13.normed.left_other, bf16[128,768]{1,0:T(8,128)(2,1)S(1)} %get-tuple-element.99.act_own.right_own, ...), custom_call_target="tpu_custom_call" | custom-call | flops 2750000128 | bytes 8500000 | tf_op jit(solution)/shard_map/pallas_call | solution.py:616
  82.5 3.2 %shard_map.175 = f32[3072,768]{1,0:T(8,128)} custom-call(bf16[128,3072]{1,0:T(8,128)(2,1)S(1)} %get-tuple-element.130.normed.left_own, bf16[128,3072]{1,0:T(8,128)(2,1)S(1)} %collective-permute-done.13.normed.left_other, bf16[128,768]{1,0:T(8,128)(2,1)S(1)} %get-tuple-element.99.act_own.right_own, ...), custom_call_target="tpu_custom_call", output_to_operand_aliasing={{}: (4, {})} | custom-call | flops 2750000128 | bytes 8500000 | tf_op jit(solution)/shard_map/pallas_call | solution.py:616
  88.3 1.5 %shard_map.176 = (bf16[4,4,3072]{2,1,0:T(4,128)(2,1)}, f32[7,7,3072]{2,1,0:T(8,128)}, f32[1,3072]{1,0:T(1,128)}, f32[1,3072]{1,0:T(1,128)}, f32[1,3072]{1,0:T(1,128)}) custom-call(s32[3]{0:T(128)S(1)} %pad_add_fusion.idx, bf16[4,16,384]{2,1,0:T(8,128)(2,1)S(1)} %get-tuple-element.126.refs_0_, bf16[4,16,384]{2,1,0:T(8,128)(2,1)S(1)} %collective-permute-done.28.refs_1_, ...), custom_call_target="tpu_custom_call" | custom-call | flops 880000000 | bytes 2720000 | tf_op jit(solution)/shard_map/pallas_call | solution.py:591
  (115 shorter events, 29.7 us)
Async XLA Ops:
  0.6 16.6 %collective-permute-start = (bf16[4,4,3072]{2,1,0:T(4,128)(2,1)}, bf16[4,4,3072]{2,1,0:T(4,128)(2,1)S(1)}, u32[]{:S(2)}, u32[]{:S(2)}) collective-permute-start(bf16[4,4,3072]{2,1,0:T(4,128)(2,1)} %shard.1), channel_id=1, source_target_pairs={{4,0},{5,1},{6,2},{7,3},{8,4},{9,5},{10,6},{11,7},{12,8},{13,9},{1... | collective-permute-start | bytes 294920 | tf_op jit(solution)/shard_map/feat_z/ppermute | solution.py:41
  5.7 11.5 %collective-permute-start.1 = (bf16[4,4,3072]{2,1,0:T(4,128)(2,1)}, bf16[4,4,3072]{2,1,0:T(4,128)(2,1)S(1)}, u32[]{:S(2)}, u32[]{:S(2)}) collective-permute-start(bf16[4,4,3072]{2,1,0:T(4,128)(2,1)} %shard.1), channel_id=1, source_target_pairs={{8,0},{9,1},{10,2},{11,3},{12,4},{13,5},{14,6},{15,7},{0,8},{1,9},... | collective-permute-start | bytes 294920 | tf_op jit(solution)/shard_map/feat_z/ppermute | solution.py:41
  5.7 11.6 %collective-permute-start.2 = (bf16[4,4,3072]{2,1,0:T(4,128)(2,1)}, bf16[4,4,3072]{2,1,0:T(4,128)(2,1)S(1)}, u32[]{:S(2)}, u32[]{:S(2)}) collective-permute-start(bf16[4,4,3072]{2,1,0:T(4,128)(2,1)} %shard.1), channel_id=1, source_target_pairs={{12,0},{13,1},{14,2},{15,3},{0,4},{1,5},{2,6},{3,7},{4,8},{5,9},{6... | collective-permute-start | bytes 294920 | tf_op jit(solution)/shard_map/feat_z/ppermute | solution.py:41
  6.7 17.2 %collective-permute-start.3 = (bf16[4,4,3072]{2,1,0:T(4,128)(2,1)}, bf16[4,4,3072]{2,1,0:T(4,128)(2,1)S(1)}, u32[]{:S(2)}, u32[]{:S(2)}) collective-permute-start(bf16[4,4,3072]{2,1,0:T(4,128)(2,1)} %shard.1), channel_id=1, source_target_pairs={{2,0},{3,1},{0,2},{1,3},{6,4},{7,5},{4,6},{5,7},{10,8},{11,9},{8,1... | collective-permute-start | bytes 294920 | tf_op jit(solution)/shard_map/feat_y/ppermute | solution.py:41
  9.2 8.0 %collective-permute-start.9 = (bf16[16,3072]{1,0:T(8,128)(2,1)S(1)}, bf16[16,3072]{1,0:T(8,128)(2,1)S(1)}, u32[]{:S(2)}, u32[]{:S(2)}) collective-permute-start(bf16[16,3072]{1,0:T(8,128)(2,1)S(1)} %reshape.89), channel_id=1, source_target_pairs={{2,0},{3,1},{0,2},{1,3},{6,4},{7,5},{4,6},{5,7},{10,8},{11,9},{8,1... | collective-permute-start | bytes 294920 | tf_op jit(solution)/shard_map/cot_y/ppermute | solution.py:41
  17.3 10.9 %collective-permute-start.10 = (bf16[2,16,3072]{2,1,0:T(8,128)(2,1)S(1)}, bf16[2,16,3072]{2,1,0:T(8,128)(2,1)S(1)}, u32[]{:S(2)}, u32[]{:S(2)}) collective-permute-start(bf16[2,16,3072]{2,1,0:T(8,128)(2,1)S(1)} %pad_maximum_fusion.2.refs_0_), channel_id=1, source_target_pairs={{4,0},{5,1},{6,2},{7,3},{8,4},{9,5},{10,6},{11,7},{12,8},{13,9},{1... | collective-permute-start | bytes 589832 | tf_op jit(solution)/shard_map/cot_z/ppermute | solution.py:41
  20.2 5.4 %collective-permute-start.4 = (bf16[4,4,3072]{2,1,0:T(4,128)(2,1)S(1)}, bf16[4,4,3072]{2,1,0:T(4,128)(2,1)S(1)}, u32[]{:S(2)}, u32[]{:S(2)}) collective-permute-start(bf16[4,4,3072]{2,1,0:T(4,128)(2,1)S(1)} %collective-permute-done.refs_1_), channel_id=1, source_target_pairs={{2,0},{3,1},{0,2},{1,3},{6,4},{7,5},{4,6},{5,7},{10,8},{11,9},{8,1... | collective-permute-start | bytes 294920 | tf_op jit(solution)/shard_map/feat_y/ppermute | solution.py:41
  21.7 5.0 %collective-permute-start.5 = (bf16[4,4,3072]{2,1,0:T(4,128)(2,1)S(1)}, bf16[4,4,3072]{2,1,0:T(4,128)(2,1)S(1)}, u32[]{:S(2)}, u32[]{:S(2)}) collective-permute-start(bf16[4,4,3072]{2,1,0:T(4,128)(2,1)S(1)} %collective-permute-done.1.refs_2_), channel_id=1, source_target_pairs={{2,0},{3,1},{0,2},{1,3},{6,4},{7,5},{4,6},{5,7},{10,8},{11,9},{8,1... | collective-permute-start | bytes 294920 | tf_op jit(solution)/shard_map/feat_y/ppermute | solution.py:41
  22.2 5.5 %collective-permute-start.6 = (bf16[4,4,3072]{2,1,0:T(4,128)(2,1)S(1)}, bf16[4,4,3072]{2,1,0:T(4,128)(2,1)S(1)}, u32[]{:S(2)}, u32[]{:S(2)}) collective-permute-start(bf16[4,4,3072]{2,1,0:T(4,128)(2,1)S(1)} %collective-permute-done.2.refs_3_), channel_id=1, source_target_pairs={{2,0},{3,1},{0,2},{1,3},{6,4},{7,5},{4,6},{5,7},{10,8},{11,9},{8,1... | collective-permute-start | bytes 294920 | tf_op jit(solution)/shard_map/feat_y/ppermute | solution.py:41
  24.0 7.7 %collective-permute-start.11 = (bf16[2,16,3072]{2,1,0:T(8,128)(2,1)S(1)}, bf16[2,16,3072]{2,1,0:T(8,128)(2,1)S(1)}, u32[]{:S(2)}, u32[]{:S(2)}) collective-permute-start(bf16[2,16,3072]{2,1,0:T(8,128)(2,1)S(1)} %pad_maximum_fusion.2.refs_0_), channel_id=1, source_target_pairs={{12,0},{13,1},{14,2},{15,3},{0,4},{1,5},{2,6},{3,7},{4,8},{5,9},{6... | collective-permute-start | bytes 589832 | tf_op jit(solution)/shard_map/cot_z/ppermute | solution.py:41
  25.6 6.1 %collective-permute-start.7 = (bf16[2,4,4,3072]{3,2,1,0:T(4,128)(2,1)S(1)}, bf16[2,4,4,3072]{3,2,1,0:T(4,128)(2,1)S(1)}, u32[]{:S(2)}, u32[]{:S(2)}) collective-permute-start(bf16[2,4,4,3072]{3,2,1,0:T(4,128)(2,1)S(1)} %pad_maximum_fusion), channel_id=1, source_target_pairs={{1,0},{0,1},{3,2},{2,3},{5,4},{4,5},{7,6},{6,7},{9,8},{8,9},{11,10... | collective-permute-start | bytes 589832 | tf_op jit(solution)/shard_map/feat_core/ppermute | solution.py:41
  28.0 3.7 %collective-permute-start.8 = (bf16[2,4,4,3072]{3,2,1,0:T(4,128)(2,1)S(1)}, bf16[2,4,4,3072]{3,2,1,0:T(4,128)(2,1)S(1)}, u32[]{:S(2)}, u32[]{:S(2)}) collective-permute-start(bf16[2,4,4,3072]{3,2,1,0:T(4,128)(2,1)S(1)} %pad_maximum_fusion.1), channel_id=1, source_target_pairs={{1,0},{0,1},{3,2},{2,3},{5,4},{4,5},{7,6},{6,7},{9,8},{8,9},{11,10... | collective-permute-start | bytes 589832 | tf_op jit(solution)/shard_map/feat_core/ppermute | solution.py:41
  31.7 6.9 %collective-permute-start.12 = (bf16[2,16,3072]{2,1,0:T(8,128)(2,1)S(1)}, bf16[2,16,3072]{2,1,0:T(8,128)(2,1)S(1)}, u32[]{:S(2)}, u32[]{:S(2)}) collective-permute-start(bf16[2,16,3072]{2,1,0:T(8,128)(2,1)S(1)} %collective-permute-done.10.refs_1_), channel_id=1, source_target_pairs={{4,0},{5,1},{6,2},{7,3},{8,4},{9,5},{10,6},{11,7},{12,8},{13,9},{1... | collective-permute-start | bytes 589832 | tf_op jit(solution)/shard_map/cot_z/ppermute | solution.py:41
  49.7 7.5 %collective-permute-start.23 = (bf16[144,384]{1,0:T(8,128)(2,1)S(1)}, bf16[144,384]{1,0:T(8,128)(2,1)S(1)}, u32[]{:S(2)}, u32[]{:S(2)}) collective-permute-start(bf16[144,384]{1,0:T(8,128)(2,1)S(1)} %get-tuple-element.147), channel_id=1, source_target_pairs={{2,0},{3,1},{0,2},{1,3},{6,4},{7,5},{4,6},{5,7},{10,8},{11,9},{8,1... | collective-permute-start | bytes 331784 | tf_op jit(solution)/shard_map/ppermute | solution.py:41
  51.3 5.9 %collective-permute-start.25 = (bf16[144,384]{1,0:T(8,128)(2,1)S(1)}, bf16[144,384]{1,0:T(8,128)(2,1)S(1)}, u32[]{:S(2)}, u32[]{:S(2)}) collective-permute-start(bf16[144,384]{1,0:T(8,128)(2,1)S(1)} %get-tuple-element.146), channel_id=1, source_target_pairs={{2,0},{3,1},{0,2},{1,3},{6,4},{7,5},{4,6},{5,7},{10,8},{11,9},{8,1... | collective-permute-start | bytes 331784 | tf_op jit(solution)/shard_map/ppermute | solution.py:41
  55.0 6.7 %collective-permute-start.20 = (bf16[144,384]{1,0:T(8,128)(2,1)S(1)}, bf16[144,384]{1,0:T(8,128)(2,1)S(1)}, u32[]{:S(2)}, u32[]{:S(2)}) collective-permute-start(bf16[144,384]{1,0:T(8,128)(2,1)S(1)} %get-tuple-element.142), channel_id=1, source_target_pairs={{2,0},{3,1},{0,2},{1,3},{6,4},{7,5},{4,6},{5,7},{10,8},{11,9},{8,1... | collective-permute-start | bytes 331784 | tf_op jit(solution)/shard_map/ppermute | solution.py:41
  56.6 6.5 %collective-permute-start.19 = (bf16[144,384]{1,0:T(8,128)(2,1)S(1)}, bf16[144,384]{1,0:T(8,128)(2,1)S(1)}, u32[]{:S(2)}, u32[]{:S(2)}) collective-permute-start(bf16[144,384]{1,0:T(8,128)(2,1)S(1)} %get-tuple-element.148), channel_id=1, source_target_pairs={{2,0},{3,1},{0,2},{1,3},{6,4},{7,5},{4,6},{5,7},{10,8},{11,9},{8,1... | collective-permute-start | bytes 331784 | tf_op jit(solution)/shard_map/ppermute | solution.py:41
  57.3 9.7 %collective-permute-start.24 = (bf16[144,384]{1,0:T(8,128)(2,1)S(1)}, bf16[144,384]{1,0:T(8,128)(2,1)S(1)}, u32[]{:S(2)}, u32[]{:S(2)}) collective-permute-start(bf16[144,384]{1,0:T(8,128)(2,1)S(1)} %get-tuple-element.145), channel_id=1, source_target_pairs={{0,8},{1,9},{2,10},{3,11},{4,12},{5,13},{6,14},{7,15},{8,0},{9,1},... | collective-permute-start | bytes 331784 | tf_op jit(solution)/shard_map/ppermute | solution.py:41
  57.4 9.7 %collective-permute-start.26 = (bf16[144,384]{1,0:T(8,128)(2,1)S(1)}, bf16[144,384]{1,0:T(8,128)(2,1)S(1)}, u32[]{:S(2)}, u32[]{:S(2)}) collective-permute-start(bf16[144,384]{1,0:T(8,128)(2,1)S(1)} %get-tuple-element.144), channel_id=1, source_target_pairs={{0,12},{1,13},{2,14},{3,15},{4,0},{5,1},{6,2},{7,3},{8,4},{9,5},{1... | collective-permute-start | bytes 331784 | tf_op jit(solution)/shard_map/ppermute | solution.py:41
  61.8 7.1 %collective-permute-start.21 = (bf16[144,384]{1,0:T(8,128)(2,1)S(1)}, bf16[144,384]{1,0:T(8,128)(2,1)S(1)}, u32[]{:S(2)}, u32[]{:S(2)}) collective-permute-start(bf16[144,384]{1,0:T(8,128)(2,1)S(1)} %add_convert_fusion), channel_id=1, source_target_pairs={{0,4},{1,5},{2,6},{3,7},{4,8},{5,9},{6,10},{7,11},{8,12},{9,13},{1... | collective-permute-start | bytes 331784 | tf_op jit(solution)/shard_map/ppermute | solution.py:41
  72.8 4.1 %collective-permute-start.30 = (bf16[4,16,384]{2,1,0:T(8,128)(2,1)S(1)}, bf16[4,16,384]{2,1,0:T(8,128)(2,1)S(1)}, u32[]{:S(2)}, u32[]{:S(2)}) collective-permute-start(bf16[4,16,384]{2,1,0:T(8,128)(2,1)S(1)} %get-tuple-element.123), channel_id=1, source_target_pairs={{0,12},{1,13},{2,14},{3,15},{4,0},{5,1},{6,2},{7,3},{8,4},{9,5},{1... | collective-permute-start | bytes 147464 | tf_op jit(solution)/shard_map/ppermute | solution.py:41
  74.5 5.9 %collective-permute-start.28 = (bf16[4,16,384]{2,1,0:T(8,128)(2,1)S(1)}, bf16[4,16,384]{2,1,0:T(8,128)(2,1)S(1)}, u32[]{:S(2)}, u32[]{:S(2)}) collective-permute-start(bf16[4,16,384]{2,1,0:T(8,128)(2,1)S(1)} %get-tuple-element.121), channel_id=1, source_target_pairs={{0,4},{1,5},{2,6},{3,7},{4,8},{5,9},{6,10},{7,11},{8,12},{9,13},{1... | collective-permute-start | bytes 147464 | tf_op jit(solution)/shard_map/ppermute | solution.py:41
  74.8 6.6 %collective-permute-start.29 = (bf16[4,16,384]{2,1,0:T(8,128)(2,1)S(1)}, bf16[4,16,384]{2,1,0:T(8,128)(2,1)S(1)}, u32[]{:S(2)}, u32[]{:S(2)}) collective-permute-start(bf16[4,16,384]{2,1,0:T(8,128)(2,1)S(1)} %get-tuple-element.122), channel_id=1, source_target_pairs={{0,8},{1,9},{2,10},{3,11},{4,12},{5,13},{6,14},{7,15},{8,0},{9,1},... | collective-permute-start | bytes 147464 | tf_op jit(solution)/shard_map/ppermute | solution.py:41
  81.5 5.2 %collective-permute-start.31 = (bf16[4,3,16,384]{3,2,1,0:T(8,128)(2,1)S(1)}, bf16[4,3,16,384]{3,2,1,0:T(8,128)(2,1)S(1)}, u32[]{:S(2)}, u32[]{:S(2)}) collective-permute-start(bf16[4,3,16,384]{3,2,1,0:T(8,128)(2,1)S(1)} %pad_maximum_fusion.4), channel_id=1, source_target_pairs={{2,0},{3,1},{0,2},{1,3},{6,4},{7,5},{4,6},{5,7},{10,8},{11,9},{8,1... | collective-permute-start | bytes 442376 | tf_op jit(solution)/shard_map/ppermute | solution.py:41
  (24 other events, 62.2 us)

commit v6 on v5

--- a/solution.py
+++ b/solution.py
@@ -804,9 +804,11 @@
         (idx, ig_keep, core_msg, small_keep),
     )
     msgs = [msgs[0]] + [send(msgs[step], flipped(z_pairs(step))) for step in (1, 2, 3)]
+    came_near = send(msgs[0][1:4], Y_PAIRS)
     up_low = half_gradient(0, after((normed, normed_other), msgs[3]), act_grad, 512)
     msgs, up_low = lax.optimization_barrier((msgs, up_low))
-    came = send(jnp.stack([msg[1:4] for msg in msgs]), Y_PAIRS)
+    came_far = send(jnp.stack([msg[1:4] for msg in msgs[1:]]), Y_PAIRS)
+    came = jnp.concatenate([came_near[None], came_far])
     up_grad = half_gradient(1, after((normed, normed_other), msgs[1]), act_grad, 512, up_low)
     near = jnp.stack([msg[2:4] for msg in msgs])
     both, up_grad = lax.optimization_barrier((jnp.stack([near, came[:, 1:3]]), up_grad))

time: 90.2 us -> 89.8 us (level)
  waiting for transfers between devices: 15.6 us -> 14 us
  starting transfers between devices: 30.9 us -> 32 us
    ppermute x33 -> x34, waiting for transfers between devices: 15.6 us -> 14 us  [send(): return lax.ppermute(value, 'rows', pairs)]
    ppermute x33 -> x34, starting transfers between devices: 30.9 us -> 32 us  [send(): return lax.ppermute(value, 'rows', pairs)]
  transfers between devices with their start and end apart: 33 -> 34, of which waited for: 15 -> 14; matrix products, arithmetic and copies ran while one was open for 4% -> 4% of each run, Pallas kernels for 25% -> 26%
where the time goes in v6:
time: 89.8 us; the launch traced here: 89.4 us
  Pallas kernels  32.2 us (36%)
  starting transfers between devices  32 us (36%)
  waiting for transfers between devices  14 us (16%)
  local copies, waits for them, and re-layouts  8.36 us (9%)
  other arithmetic  1.75 us (2%)
  between operations  1.1 us (1%)
    ppermute x34, starting transfers between devices, send(): return lax.ppermute(value, 'rows', pairs)  32 us
    pallas_call x12, Pallas kernels, call(): pl.pallas_call(kernel, out_shape=out_shape, in_specs=[SSPEC] * scalars +...  19.6 us
    ppermute x34, waiting for transfers between devices, send(): return lax.ppermute(value, 'rows', pairs)  14 us
    pallas_call x4, Pallas kernels, half_gradient(): pl.pallas_call(grad_kernel, grid=(steps,), out_shape=shape((rows, cols),...  12.6 us
    unnamed x30, local copies, waits for them, and re-layouts  6.49 us
  transfers between devices with their start and end apart: 34, of which 14 were waited for; matrix products, arithmetic and copies ran while one was open for 4% of the time, Pallas kernels for 26%

profile of v6, /device:TPU:0, one launch (start us, length us, event | category | flops | bytes accessed | tf_op | source)
XLA Modules:
  0.0 89.4 jit_solution(14931866907492857406)
XLA Ops:
  0.6 5.1 %collective-permute-start = (bf16[4,4,3072]{2,1,0:T(4,128)(2,1)}, bf16[4,4,3072]{2,1,0:T(4,128)(2,1)S(1)}, u32[]{:S(2)}, u32[]{:S(2)}) collective-permute-start(bf16[4,4,3072]{2,1,0:T(4,128)(2,1)} %shard.1), channel_id=1, source_target_pairs={{4,0},{5,1},{6,2},{7,3},{8,4},{9,5},{10,6},{11,7},{12,8},{13,9},{1... | collective-permute-start | bytes 294920 | tf_op jit(solution)/shard_map/feat_z/ppermute | solution.py:41
  6.7 1.5 %collective-permute-start.3 = (bf16[4,4,3072]{2,1,0:T(4,128)(2,1)}, bf16[4,4,3072]{2,1,0:T(4,128)(2,1)S(1)}, u32[]{:S(2)}, u32[]{:S(2)}) collective-permute-start(bf16[4,4,3072]{2,1,0:T(4,128)(2,1)} %shard.1), channel_id=1, source_target_pairs={{2,0},{3,1},{0,2},{1,3},{6,4},{7,5},{4,6},{5,7},{10,8},{11,9},{8,1... | collective-permute-start | bytes 294920 | tf_op jit(solution)/shard_map/feat_y/ppermute | solution.py:41
  10.7 2.3 %copy-done = bf16[3072,768]{1,0:T(8,128)(2,1)S(1)} copy-done((bf16[3072,768]{1,0:T(8,128)(2,1)S(1)}, bf16[3072,768]{1,0:T(8,128)(2,1)}, u32[]{:S(2)}) %copy-start) | copy-done | bytes 4718616
  17.3 2.9 %collective-permute-start.10 = (bf16[2,16,3072]{2,1,0:T(8,128)(2,1)S(1)}, bf16[2,16,3072]{2,1,0:T(8,128)(2,1)S(1)}, u32[]{:S(2)}, u32[]{:S(2)}) collective-permute-start(bf16[2,16,3072]{2,1,0:T(8,128)(2,1)S(1)} %pad_maximum_fusion.2.refs_0_), channel_id=1, source_target_pairs={{4,0},{5,1},{6,2},{7,3},{8,4},{9,5},{10,6},{11,7},{12,8},{13,9},{1... | collective-permute-start | bytes 589832 | tf_op jit(solution)/shard_map/cot_z/ppermute | solution.py:41
  20.2 1.5 %collective-permute-start.4 = (bf16[4,4,3072]{2,1,0:T(4,128)(2,1)S(1)}, bf16[4,4,3072]{2,1,0:T(4,128)(2,1)S(1)}, u32[]{:S(2)}, u32[]{:S(2)}) collective-permute-start(bf16[4,4,3072]{2,1,0:T(4,128)(2,1)S(1)} %collective-permute-done.refs_1_), channel_id=1, source_target_pairs={{2,0},{3,1},{0,2},{1,3},{6,4},{7,5},{4,6},{5,7},{10,8},{11,9},{8,1... | collective-permute-start | bytes 294920 | tf_op jit(solution)/shard_map/feat_y/ppermute | solution.py:41
  22.2 1.5 %collective-permute-start.6 = (bf16[4,4,3072]{2,1,0:T(4,128)(2,1)S(1)}, bf16[4,4,3072]{2,1,0:T(4,128)(2,1)S(1)}, u32[]{:S(2)}, u32[]{:S(2)}) collective-permute-start(bf16[4,4,3072]{2,1,0:T(4,128)(2,1)S(1)} %collective-permute-done.2.refs_3_), channel_id=1, source_target_pairs={{2,0},{3,1},{0,2},{1,3},{6,4},{7,5},{4,6},{5,7},{10,8},{11,9},{8,1... | collective-permute-start | bytes 294920 | tf_op jit(solution)/shard_map/feat_y/ppermute | solution.py:41
  24.1 1.5 %collective-permute-done.4.refs_5_ = bf16[4,4,3072]{2,1,0:T(4,128)(2,1)S(1)} collective-permute-done((bf16[4,4,3072]{2,1,0:T(4,128)(2,1)S(1)}, bf16[4,4,3072]{2,1,0:T(4,128)(2,1)S(1)}, u32[]{:S(2)}, u32[]{:S(2)}) %collective-permute-start.4) | collective-permute-done | bytes 98336 | tf_op jit(solution)/shard_map/feat_y/ppermute | solution.py:41
  28.2 3.5 %collective-permute-done.11.refs_3_ = bf16[2,16,3072]{2,1,0:T(8,128)(2,1)S(1)} collective-permute-done((bf16[2,16,3072]{2,1,0:T(8,128)(2,1)S(1)}, bf16[2,16,3072]{2,1,0:T(8,128)(2,1)S(1)}, u32[]{:S(2)}, u32[]{:S(2)}) %collective-permute-start.11) | collective-permute-done | bytes 196640 | tf_op jit(solution)/shard_map/cot_z/ppermute | solution.py:41
  32.4 2.6 %shard_map.162 = (f32[12,4,48,128]{3,2,1,0:T(8,128)S(1)}, f32[12,128,128]{2,1,0:T(8,128)S(1)}, f32[128,128]{1,0:T(8,128)S(1)}) custom-call(s32[3]{0:T(128)S(1)} %pad_add_fusion.idx, bf16[4,4,3072]{2,1,0:T(4,128)(2,1)S(1)} %get-tuple-element.75.refs_0_, bf16[4,4,3072]{2,1,0:T(4,128)(2,1)S(1)} %collective-permute-done.refs_1_, ...), custom_call_target="tpu_custom_call" | custom-call | flops 8800000000 | bytes 27200000 | tf_op jit(solution)/shard_map/pallas_call | solution.py:591
  35.1 3.4 %shard_map.163 = (bf16[128,3072]{1,0:T(8,128)(2,1)S(1)}, f32[3,4,48,128]{3,2,1,0:T(8,128)S(1)}, f32[3,128,128]{2,1,0:T(8,128)S(1)}, f32[128,128]{1,0:T(8,128)S(1)}) custom-call(s32[3]{0:T(128)S(1)} %pad_add_fusion.idx, bf16[4,4,3072]{2,1,0:T(4,128)(2,1)S(1)} %get-tuple-element.75.refs_0_, bf16[4,4,3072]{2,1,0:T(4,128)(2,1)S(1)} %collective-permute-done.refs_1_, ...), custom_call_target="tpu_custom_call" | custom-call | flops 8800000000 | bytes 27200000 | tf_op jit(solution)/shard_map/pallas_call | solution.py:591
  43.0 2.8 %shard_map.167 = (bf16[128,768]{1,0:T(8,128)(2,1)S(1)}, bf16[128,768]{1,0:T(8,128)(2,1)S(1)}, f32[1,768]{1,0:T(1,128)S(1)}, f32[16,128]{1,0:T(8,128)S(1)}, f32[16,128]{1,0:T(8,128)S(1)}) custom-call(bf16[256,3072]{1,0:T(8,128)(2,1)S(1)} %get-tuple-element.95.cot_all.right_own.right_other, bf16[768,3072]{1,0:T(8,128)(2,1)S(1)} %bitcast.67, ...), custom_call_target="tpu_custom_call" | custom-call | flops 2420000000 | bytes 7480000 | tf_op jit(solution)/shard_map/pallas_call | solution.py:591
  45.8 1.6 %shard_map.171 = (f32[2,2,144,384]{3,2,1,0:T(8,128)S(1)}, bf16[2,2,144,384]{3,2,1,0:T(8,128)(2,1)S(1)}) custom-call(s32[3]{0:T(128)S(1)} %pad_add_fusion.idx, bf16[128,768]{1,0:T(8,128)(2,1)S(1)} %get-tuple-element.99.act_own.right_own, bf16[128,768]{1,0:T(8,128)(2,1)S(1)} %get-tuple-element.100.act_other.right_other, bf16[3072,768]{1,0:T(8,128)(2,1)S(1)} %bitcast.65, ...), custom_call_target="tpu_custom_call" | custom-call | flops 1760000000 | bytes 5440000 | tf_op jit(solution)/shard_map/pallas_call | solution.py:591
  47.6 1.5 %shard_map.168 = (f32[2,2,144,384]{3,2,1,0:T(8,128)S(1)}, bf16[2,2,144,384]{3,2,1,0:T(8,128)(2,1)S(1)}) custom-call(s32[3]{0:T(128)S(1)} %pad_add_fusion.idx, bf16[128,768]{1,0:T(8,128)(2,1)S(1)} %get-tuple-element.99.act_own.right_own, bf16[128,768]{1,0:T(8,128)(2,1)S(1)} %get-tuple-element.100.act_other.right_other, bf16[3072,768]{1,0:T(8,128)(2,1)S(1)} %bitcast.65, ...), custom_call_target="tpu_custom_call" | custom-call | flops 1760000000 | bytes 5440000 | tf_op jit(solution)/shard_map/pallas_call | solution.py:591
  49.7 1.6 %collective-permute-start.23 = (bf16[144,384]{1,0:T(8,128)(2,1)S(1)}, bf16[144,384]{1,0:T(8,128)(2,1)S(1)}, u32[]{:S(2)}, u32[]{:S(2)}) collective-permute-start(bf16[144,384]{1,0:T(8,128)(2,1)S(1)} %get-tuple-element.147), channel_id=1, source_target_pairs={{2,0},{3,1},{0,2},{1,3},{6,4},{7,5},{4,6},{5,7},{10,8},{11,9},{8,1... | collective-permute-start | bytes 331784 | tf_op jit(solution)/shard_map/ppermute | solution.py:41
  51.8 3.1 %shard_map.169.rest_0_ = f32[768,3072]{1,0:T(8,128)} custom-call(bf16[128,768]{1,0:T(8,128)(2,1)S(1)} %get-tuple-element.107.left_own, bf16[128,768]{1,0:T(8,128)(2,1)S(1)} %get-tuple-element.108.left_other, bf16[256,3072]{1,0:T(8,128)(2,1)S(1)} %get-tuple-element.95.cot_all.right_own.right_other, ...), custom_call_target="tpu_custom_call" | custom-call | flops 2750000128 | bytes 8500000 | tf_op jit(solution)/shard_map/pallas_call | solution.py:616
  55.0 1.6 %collective-permute-start.20 = (bf16[144,384]{1,0:T(8,128)(2,1)S(1)}, bf16[144,384]{1,0:T(8,128)(2,1)S(1)}, u32[]{:S(2)}, u32[]{:S(2)}) collective-permute-start(bf16[144,384]{1,0:T(8,128)(2,1)S(1)} %get-tuple-element.142), channel_id=1, source_target_pairs={{2,0},{3,1},{0,2},{1,3},{6,4},{7,5},{4,6},{5,7},{10,8},{11,9},{8,1... | collective-permute-start | bytes 331784 | tf_op jit(solution)/shard_map/ppermute | solution.py:41
  57.4 4.4 %collective-permute-start.26 = (bf16[144,384]{1,0:T(8,128)(2,1)S(1)}, bf16[144,384]{1,0:T(8,128)(2,1)S(1)}, u32[]{:S(2)}, u32[]{:S(2)}) collective-permute-start(bf16[144,384]{1,0:T(8,128)(2,1)S(1)} %get-tuple-element.144), channel_id=1, source_target_pairs={{0,12},{1,13},{2,14},{3,15},{4,0},{5,1},{6,2},{7,3},{8,4},{9,5},{1... | collective-permute-start | bytes 331784 | tf_op jit(solution)/shard_map/ppermute | solution.py:41
  63.1 3.1 %shard_map.170 = f32[768,3072]{1,0:T(8,128)} custom-call(bf16[128,768]{1,0:T(8,128)(2,1)S(1)} %get-tuple-element.107.left_own, bf16[128,768]{1,0:T(8,128)(2,1)S(1)} %get-tuple-element.108.left_other, bf16[256,3072]{1,0:T(8,128)(2,1)S(1)} %get-tuple-element.95.cot_all.right_own.right_other, ...), custom_call_target="tpu_custom_call", output_to_operand_aliasing={{}: (4, {})} | custom-call | flops 2750000128 | bytes 8500000 | tf_op jit(solution)/shard_map/pallas_call | solution.py:616
  67.0 1.8 %collective-permute-done.21.near_1 = bf16[144,384]{1,0:T(8,128)(2,1)S(1)} collective-permute-done((bf16[144,384]{1,0:T(8,128)(2,1)S(1)}, bf16[144,384]{1,0:T(8,128)(2,1)S(1)}, u32[]{:S(2)}, u32[]{:S(2)}) %collective-permute-start.21) | collective-permute-done | bytes 110624 | tf_op jit(solution)/shard_map/ppermute | solution.py:41
  68.8 2.0 %shard_map.172 = (bf16[4,16,384]{2,1,0:T(8,128)(2,1)S(1)}, bf16[6,16,384]{2,1,0:T(8,128)(2,1)S(1)}, f32[2,16,384]{2,1,0:T(8,128)S(1)}) custom-call(s32[3]{0:T(128)S(1)} %pad_add_fusion.idx, f32[144,384]{1,0:T(8,128)S(1)} %fusion.10.own, bf16[144,384]{1,0:T(8,128)(2,1)S(1)} %collective-permute-done.21.near_1, ...), custom_call_target="tpu_custom_call" | custom-call | flops 2420000000 | bytes 7480000 | tf_op jit(solution)/shard_map/pallas_call | solution.py:591
  72.8 1.8 %collective-permute-start.30 = (bf16[4,16,384]{2,1,0:T(8,128)(2,1)S(1)}, bf16[4,16,384]{2,1,0:T(8,128)(2,1)S(1)}, u32[]{:S(2)}, u32[]{:S(2)}) collective-permute-start(bf16[4,16,384]{2,1,0:T(8,128)(2,1)S(1)} %get-tuple-element.123), channel_id=1, source_target_pairs={{0,12},{1,13},{2,14},{3,15},{4,0},{5,1},{6,2},{7,3},{8,4},{9,5},{1... | collective-permute-start | bytes 147464 | tf_op jit(solution)/shard_map/ppermute | solution.py:41
  77.2 3.2 %shard_map.174.rest_0_ = f32[3072,768]{1,0:T(8,128)} custom-call(bf16[128,3072]{1,0:T(8,128)(2,1)S(1)} %get-tuple-element.130.normed.left_own, bf16[128,3072]{1,0:T(8,128)(2,1)S(1)} %collective-permute-done.13.normed.left_other, bf16[128,768]{1,0:T(8,128)(2,1)S(1)} %get-tuple-element.99.act_own.right_own, ...), custom_call_target="tpu_custom_call" | custom-call | flops 2750000128 | bytes 8500000 | tf_op jit(solution)/shard_map/pallas_call | solution.py:616
  82.5 3.2 %shard_map.175 = f32[3072,768]{1,0:T(8,128)} custom-call(bf16[128,3072]{1,0:T(8,128)(2,1)S(1)} %get-tuple-element.130.normed.left_own, bf16[128,3072]{1,0:T(8,128)(2,1)S(1)} %collective-permute-done.13.normed.left_other, bf16[128,768]{1,0:T(8,128)(2,1)S(1)} %get-tuple-element.99.act_own.right_own, ...), custom_call_target="tpu_custom_call", output_to_operand_aliasing={{}: (4, {})} | custom-call | flops 2750000128 | bytes 8500000 | tf_op jit(solution)/shard_map/pallas_call | solution.py:616
  87.9 1.5 %shard_map.176 = (bf16[4,4,3072]{2,1,0:T(4,128)(2,1)}, f32[7,7,3072]{2,1,0:T(8,128)}, f32[1,3072]{1,0:T(1,128)}, f32[1,3072]{1,0:T(1,128)}, f32[1,3072]{1,0:T(1,128)}) custom-call(s32[3]{0:T(128)S(1)} %pad_add_fusion.idx, bf16[4,16,384]{2,1,0:T(8,128)(2,1)S(1)} %get-tuple-element.126.refs_0_, bf16[4,16,384]{2,1,0:T(8,128)(2,1)S(1)} %collective-permute-done.28.refs_1_, ...), custom_call_target="tpu_custom_call" | custom-call | flops 880000000 | bytes 2720000 | tf_op jit(solution)/shard_map/pallas_call | solution.py:591
  (119 shorter events, 29.3 us)
Async XLA Ops:
  0.6 16.6 %collective-permute-start = (bf16[4,4,3072]{2,1,0:T(4,128)(2,1)}, bf16[4,4,3072]{2,1,0:T(4,128)(2,1)S(1)}, u32[]{:S(2)}, u32[]{:S(2)}) collective-permute-start(bf16[4,4,3072]{2,1,0:T(4,128)(2,1)} %shard.1), channel_id=1, source_target_pairs={{4,0},{5,1},{6,2},{7,3},{8,4},{9,5},{10,6},{11,7},{12,8},{13,9},{1... | collective-permute-start | bytes 294920 | tf_op jit(solution)/shard_map/feat_z/ppermute | solution.py:41
  5.7 11.5 %collective-permute-start.1 = (bf16[4,4,3072]{2,1,0:T(4,128)(2,1)}, bf16[4,4,3072]{2,1,0:T(4,128)(2,1)S(1)}, u32[]{:S(2)}, u32[]{:S(2)}) collective-permute-start(bf16[4,4,3072]{2,1,0:T(4,128)(2,1)} %shard.1), channel_id=1, source_target_pairs={{8,0},{9,1},{10,2},{11,3},{12,4},{13,5},{14,6},{15,7},{0,8},{1,9},... | collective-permute-start | bytes 294920 | tf_op jit(solution)/shard_map/feat_z/ppermute | solution.py:41
  5.7 11.6 %collective-permute-start.2 = (bf16[4,4,3072]{2,1,0:T(4,128)(2,1)}, bf16[4,4,3072]{2,1,0:T(4,128)(2,1)S(1)}, u32[]{:S(2)}, u32[]{:S(2)}) collective-permute-start(bf16[4,4,3072]{2,1,0:T(4,128)(2,1)} %shard.1), channel_id=1, source_target_pairs={{12,0},{13,1},{14,2},{15,3},{0,4},{1,5},{2,6},{3,7},{4,8},{5,9},{6... | collective-permute-start | bytes 294920 | tf_op jit(solution)/shard_map/feat_z/ppermute | solution.py:41
  6.7 17.2 %collective-permute-start.3 = (bf16[4,4,3072]{2,1,0:T(4,128)(2,1)}, bf16[4,4,3072]{2,1,0:T(4,128)(2,1)S(1)}, u32[]{:S(2)}, u32[]{:S(2)}) collective-permute-start(bf16[4,4,3072]{2,1,0:T(4,128)(2,1)} %shard.1), channel_id=1, source_target_pairs={{2,0},{3,1},{0,2},{1,3},{6,4},{7,5},{4,6},{5,7},{10,8},{11,9},{8,1... | collective-permute-start | bytes 294920 | tf_op jit(solution)/shard_map/feat_y/ppermute | solution.py:41
  9.2 8.0 %collective-permute-start.9 = (bf16[16,3072]{1,0:T(8,128)(2,1)S(1)}, bf16[16,3072]{1,0:T(8,128)(2,1)S(1)}, u32[]{:S(2)}, u32[]{:S(2)}) collective-permute-start(bf16[16,3072]{1,0:T(8,128)(2,1)S(1)} %reshape.89), channel_id=1, source_target_pairs={{2,0},{3,1},{0,2},{1,3},{6,4},{7,5},{4,6},{5,7},{10,8},{11,9},{8,1... | collective-permute-start | bytes 294920 | tf_op jit(solution)/shard_map/cot_y/ppermute | solution.py:41
  17.3 10.9 %collective-permute-start.10 = (bf16[2,16,3072]{2,1,0:T(8,128)(2,1)S(1)}, bf16[2,16,3072]{2,1,0:T(8,128)(2,1)S(1)}, u32[]{:S(2)}, u32[]{:S(2)}) collective-permute-start(bf16[2,16,3072]{2,1,0:T(8,128)(2,1)S(1)} %pad_maximum_fusion.2.refs_0_), channel_id=1, source_target_pairs={{4,0},{5,1},{6,2},{7,3},{8,4},{9,5},{10,6},{11,7},{12,8},{13,9},{1... | collective-permute-start | bytes 589832 | tf_op jit(solution)/shard_map/cot_z/ppermute | solution.py:41
  20.2 5.4 %collective-permute-start.4 = (bf16[4,4,3072]{2,1,0:T(4,128)(2,1)S(1)}, bf16[4,4,3072]{2,1,0:T(4,128)(2,1)S(1)}, u32[]{:S(2)}, u32[]{:S(2)}) collective-permute-start(bf16[4,4,3072]{2,1,0:T(4,128)(2,1)S(1)} %collective-permute-done.refs_1_), channel_id=1, source_target_pairs={{2,0},{3,1},{0,2},{1,3},{6,4},{7,5},{4,6},{5,7},{10,8},{11,9},{8,1... | collective-permute-start | bytes 294920 | tf_op jit(solution)/shard_map/feat_y/ppermute | solution.py:41
  21.7 5.0 %collective-permute-start.5 = (bf16[4,4,3072]{2,1,0:T(4,128)(2,1)S(1)}, bf16[4,4,3072]{2,1,0:T(4,128)(2,1)S(1)}, u32[]{:S(2)}, u32[]{:S(2)}) collective-permute-start(bf16[4,4,3072]{2,1,0:T(4,128)(2,1)S(1)} %collective-permute-done.1.refs_2_), channel_id=1, source_target_pairs={{2,0},{3,1},{0,2},{1,3},{6,4},{7,5},{4,6},{5,7},{10,8},{11,9},{8,1... | collective-permute-start | bytes 294920 | tf_op jit(solution)/shard_map/feat_y/ppermute | solution.py:41
  22.2 5.5 %collective-permute-start.6 = (bf16[4,4,3072]{2,1,0:T(4,128)(2,1)S(1)}, bf16[4,4,3072]{2,1,0:T(4,128)(2,1)S(1)}, u32[]{:S(2)}, u32[]{:S(2)}) collective-permute-start(bf16[4,4,3072]{2,1,0:T(4,128)(2,1)S(1)} %collective-permute-done.2.refs_3_), channel_id=1, source_target_pairs={{2,0},{3,1},{0,2},{1,3},{6,4},{7,5},{4,6},{5,7},{10,8},{11,9},{8,1... | collective-permute-start | bytes 294920 | tf_op jit(solution)/shard_map/feat_y/ppermute | solution.py:41
  24.0 7.7 %collective-permute-start.11 = (bf16[2,16,3072]{2,1,0:T(8,128)(2,1)S(1)}, bf16[2,16,3072]{2,1,0:T(8,128)(2,1)S(1)}, u32[]{:S(2)}, u32[]{:S(2)}) collective-permute-start(bf16[2,16,3072]{2,1,0:T(8,128)(2,1)S(1)} %pad_maximum_fusion.2.refs_0_), channel_id=1, source_target_pairs={{12,0},{13,1},{14,2},{15,3},{0,4},{1,5},{2,6},{3,7},{4,8},{5,9},{6... | collective-permute-start | bytes 589832 | tf_op jit(solution)/shard_map/cot_z/ppermute | solution.py:41
  25.6 6.1 %collective-permute-start.7 = (bf16[2,4,4,3072]{3,2,1,0:T(4,128)(2,1)S(1)}, bf16[2,4,4,3072]{3,2,1,0:T(4,128)(2,1)S(1)}, u32[]{:S(2)}, u32[]{:S(2)}) collective-permute-start(bf16[2,4,4,3072]{3,2,1,0:T(4,128)(2,1)S(1)} %pad_maximum_fusion), channel_id=1, source_target_pairs={{1,0},{0,1},{3,2},{2,3},{5,4},{4,5},{7,6},{6,7},{9,8},{8,9},{11,10... | collective-permute-start | bytes 589832 | tf_op jit(solution)/shard_map/feat_core/ppermute | solution.py:41
  31.7 6.9 %collective-permute-start.12 = (bf16[2,16,3072]{2,1,0:T(8,128)(2,1)S(1)}, bf16[2,16,3072]{2,1,0:T(8,128)(2,1)S(1)}, u32[]{:S(2)}, u32[]{:S(2)}) collective-permute-start(bf16[2,16,3072]{2,1,0:T(8,128)(2,1)S(1)} %collective-permute-done.10.refs_1_), channel_id=1, source_target_pairs={{4,0},{5,1},{6,2},{7,3},{8,4},{9,5},{10,6},{11,7},{12,8},{13,9},{1... | collective-permute-start | bytes 589832 | tf_op jit(solution)/shard_map/cot_z/ppermute | solution.py:41
  49.7 7.5 %collective-permute-start.23 = (bf16[144,384]{1,0:T(8,128)(2,1)S(1)}, bf16[144,384]{1,0:T(8,128)(2,1)S(1)}, u32[]{:S(2)}, u32[]{:S(2)}) collective-permute-start(bf16[144,384]{1,0:T(8,128)(2,1)S(1)} %get-tuple-element.147), channel_id=1, source_target_pairs={{2,0},{3,1},{0,2},{1,3},{6,4},{7,5},{4,6},{5,7},{10,8},{11,9},{8,1... | collective-permute-start | bytes 331784 | tf_op jit(solution)/shard_map/ppermute | solution.py:41
  51.3 5.9 %collective-permute-start.25 = (bf16[144,384]{1,0:T(8,128)(2,1)S(1)}, bf16[144,384]{1,0:T(8,128)(2,1)S(1)}, u32[]{:S(2)}, u32[]{:S(2)}) collective-permute-start(bf16[144,384]{1,0:T(8,128)(2,1)S(1)} %get-tuple-element.146), channel_id=1, source_target_pairs={{2,0},{3,1},{0,2},{1,3},{6,4},{7,5},{4,6},{5,7},{10,8},{11,9},{8,1... | collective-permute-start | bytes 331784 | tf_op jit(solution)/shard_map/ppermute | solution.py:41
  55.0 6.7 %collective-permute-start.20 = (bf16[144,384]{1,0:T(8,128)(2,1)S(1)}, bf16[144,384]{1,0:T(8,128)(2,1)S(1)}, u32[]{:S(2)}, u32[]{:S(2)}) collective-permute-start(bf16[144,384]{1,0:T(8,128)(2,1)S(1)} %get-tuple-element.142), channel_id=1, source_target_pairs={{2,0},{3,1},{0,2},{1,3},{6,4},{7,5},{4,6},{5,7},{10,8},{11,9},{8,1... | collective-permute-start | bytes 331784 | tf_op jit(solution)/shard_map/ppermute | solution.py:41
  56.6 6.5 %collective-permute-start.19 = (bf16[144,384]{1,0:T(8,128)(2,1)S(1)}, bf16[144,384]{1,0:T(8,128)(2,1)S(1)}, u32[]{:S(2)}, u32[]{:S(2)}) collective-permute-start(bf16[144,384]{1,0:T(8,128)(2,1)S(1)} %get-tuple-element.148), channel_id=1, source_target_pairs={{2,0},{3,1},{0,2},{1,3},{6,4},{7,5},{4,6},{5,7},{10,8},{11,9},{8,1... | collective-permute-start | bytes 331784 | tf_op jit(solution)/shard_map/ppermute | solution.py:41
  57.3 9.7 %collective-permute-start.24 = (bf16[144,384]{1,0:T(8,128)(2,1)S(1)}, bf16[144,384]{1,0:T(8,128)(2,1)S(1)}, u32[]{:S(2)}, u32[]{:S(2)}) collective-permute-start(bf16[144,384]{1,0:T(8,128)(2,1)S(1)} %get-tuple-element.145), channel_id=1, source_target_pairs={{0,8},{1,9},{2,10},{3,11},{4,12},{5,13},{6,14},{7,15},{8,0},{9,1},... | collective-permute-start | bytes 331784 | tf_op jit(solution)/shard_map/ppermute | solution.py:41
  57.4 9.7 %collective-permute-start.26 = (bf16[144,384]{1,0:T(8,128)(2,1)S(1)}, bf16[144,384]{1,0:T(8,128)(2,1)S(1)}, u32[]{:S(2)}, u32[]{:S(2)}) collective-permute-start(bf16[144,384]{1,0:T(8,128)(2,1)S(1)} %get-tuple-element.144), channel_id=1, source_target_pairs={{0,12},{1,13},{2,14},{3,15},{4,0},{5,1},{6,2},{7,3},{8,4},{9,5},{1... | collective-permute-start | bytes 331784 | tf_op jit(solution)/shard_map/ppermute | solution.py:41
  61.8 7.1 %collective-permute-start.21 = (bf16[144,384]{1,0:T(8,128)(2,1)S(1)}, bf16[144,384]{1,0:T(8,128)(2,1)S(1)}, u32[]{:S(2)}, u32[]{:S(2)}) collective-permute-start(bf16[144,384]{1,0:T(8,128)(2,1)S(1)} %add_convert_fusion), channel_id=1, source_target_pairs={{0,4},{1,5},{2,6},{3,7},{4,8},{5,9},{6,10},{7,11},{8,12},{9,13},{1... | collective-permute-start | bytes 331784 | tf_op jit(solution)/shard_map/ppermute | solution.py:41
  72.8 4.4 %collective-permute-start.30 = (bf16[4,16,384]{2,1,0:T(8,128)(2,1)S(1)}, bf16[4,16,384]{2,1,0:T(8,128)(2,1)S(1)}, u32[]{:S(2)}, u32[]{:S(2)}) collective-permute-start(bf16[4,16,384]{2,1,0:T(8,128)(2,1)S(1)} %get-tuple-element.123), channel_id=1, source_target_pairs={{0,12},{1,13},{2,14},{3,15},{4,0},{5,1},{6,2},{7,3},{8,4},{9,5},{1... | collective-permute-start | bytes 147464 | tf_op jit(solution)/shard_map/ppermute | solution.py:41
  74.5 5.9 %collective-permute-start.28 = (bf16[4,16,384]{2,1,0:T(8,128)(2,1)S(1)}, bf16[4,16,384]{2,1,0:T(8,128)(2,1)S(1)}, u32[]{:S(2)}, u32[]{:S(2)}) collective-permute-start(bf16[4,16,384]{2,1,0:T(8,128)(2,1)S(1)} %get-tuple-element.121), channel_id=1, source_target_pairs={{0,4},{1,5},{2,6},{3,7},{4,8},{5,9},{6,10},{7,11},{8,12},{9,13},{1... | collective-permute-start | bytes 147464 | tf_op jit(solution)/shard_map/ppermute | solution.py:41
  74.8 6.6 %collective-permute-start.29 = (bf16[4,16,384]{2,1,0:T(8,128)(2,1)S(1)}, bf16[4,16,384]{2,1,0:T(8,128)(2,1)S(1)}, u32[]{:S(2)}, u32[]{:S(2)}) collective-permute-start(bf16[4,16,384]{2,1,0:T(8,128)(2,1)S(1)} %get-tuple-element.122), channel_id=1, source_target_pairs={{0,8},{1,9},{2,10},{3,11},{4,12},{5,13},{6,14},{7,15},{8,0},{9,1},... | collective-permute-start | bytes 147464 | tf_op jit(solution)/shard_map/ppermute | solution.py:41
  76.0 9.7 %collective-permute-start.31 = (bf16[3,16,384]{2,1,0:T(8,128)(2,1)S(1)}, bf16[3,16,384]{2,1,0:T(8,128)(2,1)S(1)}, u32[]{:S(2)}, u32[]{:S(2)}) collective-permute-start(bf16[3,16,384]{2,1,0:T(8,128)(2,1)S(1)} %slice.127), channel_id=1, source_target_pairs={{2,0},{3,1},{0,2},{1,3},{6,4},{7,5},{4,6},{5,7},{10,8},{11,9},{8,1... | collective-permute-start | bytes 110600 | tf_op jit(solution)/shard_map/ppermute | solution.py:41
  81.5 4.8 %collective-permute-start.32 = (bf16[3,3,16,384]{3,2,1,0:T(8,128)(2,1)S(1)}, bf16[3,3,16,384]{3,2,1,0:T(8,128)(2,1)S(1)}, u32[]{:S(2)}, u32[]{:S(2)}) collective-permute-start(bf16[3,3,16,384]{3,2,1,0:T(8,128)(2,1)S(1)} %pad_maximum_fusion.5), channel_id=1, source_target_pairs={{2,0},{3,1},{0,2},{1,3},{6,4},{7,5},{4,6},{5,7},{10,8},{11,9},{8,1... | collective-permute-start | bytes 331784 | tf_op jit(solution)/shard_map/ppermute | solution.py:41
  (25 other events, 66.0 us)
